TPU v7x, 256 devices: a whole 4x4x8 slice. The times are simulated.
256 devices in a mesh: blk: 32 (over z_hi, x, core), uly: 8 (over z_lo, y).
Axes of the slice: x: 4, y: 4, z: 8 (z_hi: 4, z_lo: 2; z = z_hi * 2 + z_lo), core: 2. Of those that a mesh axis runs over, the one named last changes fastest.
Arguments:
- queries: bfloat16 [32768, 4096], P(('blk', 'uly')), may hold values from -14 to 14
- keys: bfloat16 [32768, 512], P(('blk', 'uly')), may hold values from -6 to 6
- values: bfloat16 [32768, 512], P(('blk', 'uly')), may hold values from -6 to 6
- head_grads: bfloat16 [32768, 4096], P(('blk', 'uly')), may hold values from -6 to 6
- cotangent: bfloat16 [32768, 4096], P(('blk', 'uly')), may hold values from -24 to 24
- old_logprobs: float32 [32768], P(('blk', 'uly')), may hold values from -4 to 0
- new_logprobs: float32 [32768], P(('blk', 'uly')), may hold values from -4 to 0
- doc_lengths: int32 [128], replicated, may hold values from 1 to 512, 32768 in all
Outputs:
- grad_queries: float32 [32768, 4096], P(('blk', 'uly'))
- key_gradient: float32 [32768, 512], P(('blk', 'uly'))
- value_gradient: float32 [32768, 512], P(('blk', 'uly'))
- grad_out_weight: float32 [4096, 4096], P('uly', 'blk')
Inputs may be any that keep to these rules, and one draw needn't show every extreme that they name: `doc_lengths`: the lengths sum to 32768.
All inputs are finite; a program needn't handle non-finite values.
Results may differ from a plain program's by a relative error of at most 0.035.
Values may be sent and summed in bfloat16 or wider, within the bound.
No kernel may reach another device: no remote copies, remote signals or barrier semaphores. Data moves between devices by JAX's collectives and lax.ppermute only.
A program may use at most 128 MiB of HBM per device.

v0:
```python
import math

import jax
import jax.numpy as jnp
from jax import lax
from jax.experimental import pallas as pl
from jax.experimental.pallas import tpu as pltpu
from jax.sharding import Mesh, PartitionSpec as P

HEAD = 128
TOKENS = 128
BACK = 4
SPAN = (BACK + 1) * TOKENS
KV_HEADS = 4
GROUP = 8
CLIP = 2.0
NEG = -1e30
SCALE = 1.0 / math.sqrt(HEAD)
LOG2E = math.log2(math.e)
FLAT = ("zh", "x", "core", "zl", "y")
BF = jnp.bfloat16
F32 = jnp.float32

NT = (((1,), (1,)), ((), ()))


def dot(a, b):
    return jnp.dot(a, b, preferred_element_type=F32)


def dot_nt(a, b):
    return lax.dot_general(a, b, NT, preferred_element_type=F32)


def mask_bias(here, lengths):
    row = lax.broadcasted_iota(jnp.int32, (TOKENS, TOKENS), 0)
    col = lax.broadcasted_iota(jnp.int32, (TOKENS, TOKENS), 1)
    lens = jnp.broadcast_to(lengths.astype(F32), (TOKENS, TOKENS))
    ends = jnp.sum(jnp.where(col <= row, lens, 0.0), axis=1, keepdims=True)
    lens_col = jnp.sum(jnp.where(col == row, lens, 0.0), axis=1, keepdims=True)
    base = here * TOKENS
    pos = (base + col).astype(F32)
    first = jnp.sum(jnp.where(ends <= pos, lens_col, 0.0), axis=0, keepdims=True)
    first = first.astype(jnp.int32)
    key = base - BACK * TOKENS + lax.broadcasted_iota(jnp.int32, (SPAN, TOKENS), 0)
    query = base + lax.broadcasted_iota(jnp.int32, (SPAN, TOKENS), 1)
    seen = (key <= query) & (key >= first)
    return jnp.where(seen, 0.0, NEG)


def scores_of(keys, q_pair, bias):
    return dot_nt(keys, q_pair) * (SCALE * LOG2E) + bias


def pair_rows(ref_or_val, pair):
    a = ref_or_val[:, (2 * pair) * HEAD : (2 * pair + 1) * HEAD]
    b = ref_or_val[:, (2 * pair + 1) * HEAD : (2 * pair + 2) * HEAD]
    return jnp.concatenate([a, b], axis=0)


def forward_kernel(here_ref, len_ref, q_ref, *refs):
    kv_refs, (out_ref, log_ref, bias_ref) = refs[: BACK + 1], refs[BACK + 1 :]

    @pl.when(pl.program_id(0) == 0)
    def _():
        bias_ref[...] = mask_bias(here_ref[0], len_ref[...])

    keys = jnp.concatenate([r[0] for r in kv_refs], axis=0)
    values_t = jnp.concatenate([r[1] for r in kv_refs], axis=0).T
    bias = jnp.concatenate([bias_ref[...]] * 2, axis=1)
    for pair in range(GROUP // 2):
        s = scores_of(keys, pair_rows(q_ref, pair), bias)
        top = jnp.max(s, axis=0, keepdims=True)
        p = jnp.exp2(s - top)
        total = jnp.sum(p, axis=0, keepdims=True)
        out_t = (dot(values_t, p.astype(BF)) / total).astype(BF)
        log_total = top + jnp.log2(total)
        for i in range(2):
            h = 2 * pair + i
            out_ref[h * HEAD : (h + 1) * HEAD, :] = out_t[:, i * TOKENS : (i + 1) * TOKENS]
            log_ref[0, h : h + 1, :] = log_total[:, i * TOKENS : (i + 1) * TOKENS]


def column_of(row):
    r = lax.broadcasted_iota(jnp.int32, (TOKENS, TOKENS), 0)
    c = lax.broadcasted_iota(jnp.int32, (TOKENS, TOKENS), 1)
    return jnp.sum(jnp.where(r == c, jnp.broadcast_to(row, (TOKENS, TOKENS)), 0.0), axis=1, keepdims=True)


def ratio_column(old_ref, new_ref):
    return column_of(jnp.minimum(jnp.exp(new_ref[...] - old_ref[...]), CLIP))


def backward_kernel(here_ref, len_ref, old_ref, new_ref, q_ref, g_ref, log_ref, *refs):
    kv_refs = refs[: BACK + 1]
    dq_ref, own_ref = refs[BACK + 1 : BACK + 3]
    back_refs = refs[BACK + 3 : 2 * BACK + 3]
    bias_ref, ratio_ref = refs[2 * BACK + 3 :]

    @pl.when(pl.program_id(0) == 0)
    def _():
        bias_ref[...] = mask_bias(here_ref[0], len_ref[...])
        ratio_ref[...] = jnp.broadcast_to(ratio_column(old_ref, new_ref), (TOKENS, HEAD))

    keys = jnp.concatenate([r[0] for r in kv_refs], axis=0)
    values = jnp.concatenate([r[1] for r in kv_refs], axis=0)
    keys_t = keys.T
    bias = jnp.concatenate([bias_ref[...]] * 2, axis=1)
    ratio = jnp.concatenate([ratio_ref[...]] * 2, axis=0)
    dk = jnp.zeros((SPAN, HEAD), F32)
    dv = jnp.zeros((SPAN, HEAD), F32)
    for pair in range(GROUP // 2):
        q = pair_rows(q_ref, pair)
        grad = (pair_rows(g_ref, pair).astype(F32) * ratio).astype(BF)
        logs = jnp.concatenate([log_ref[0, 2 * pair : 2 * pair + 1, :], log_ref[0, 2 * pair + 1 : 2 * pair + 2, :]], axis=1)
        p = jnp.exp2(scores_of(keys, q, bias) - logs)
        dp = dot_nt(values, grad)
        delta = jnp.sum(p * dp, axis=0, keepdims=True)
        ds = (p * (dp - delta)).astype(BF)
        dv = dv + dot(p.astype(BF), grad)
        dk = dk + dot(ds, q)
        dq_t = dot(keys_t, ds) * SCALE
        for i in range(2):
            h = 2 * pair + i
            dq_ref[:, h * HEAD : (h + 1) * HEAD] = dq_t[:, i * TOKENS : (i + 1) * TOKENS].T
    dk = dk * SCALE
    own_ref[0] = dk[BACK * TOKENS :]
    own_ref[1] = dv[BACK * TOKENS :]
    for j, ref in enumerate(back_refs):
        at = (BACK - 1 - j) * TOKENS
        ref[0] = dk[at : at + TOKENS].astype(BF)
        ref[1] = dv[at : at + TOKENS].astype(BF)


def params(mib):
    return pltpu.CompilerParams(vmem_limit_bytes=mib * 2**20)


KV_SPEC = pl.BlockSpec((2, TOKENS, HEAD), lambda g, *_: (0, 0, g))
ROW_SPEC = pl.BlockSpec((1, TOKENS), lambda g, *_: (0, 0))
Q_SPEC = pl.BlockSpec((TOKENS, GROUP * HEAD), lambda g, *_: (0, g))
LOG_SPEC = pl.BlockSpec((1, GROUP, TOKENS), lambda g, *_: (g, 0, 0))


def attention_forward(here, lengths, q, kvs):
    rows = q.shape[1]
    return pl.pallas_call(
        forward_kernel,
        grid_spec=pltpu.PrefetchScalarGridSpec(
            num_scalar_prefetch=1,
            grid=(KV_HEADS,),
            in_specs=[ROW_SPEC, Q_SPEC] + [KV_SPEC] * (BACK + 1),
            out_specs=[pl.BlockSpec((GROUP * HEAD, TOKENS), lambda g, *_: (g, 0)), LOG_SPEC],
            scratch_shapes=[pltpu.VMEM((SPAN, TOKENS), F32)],
        ),
        out_shape=[
            jax.ShapeDtypeStruct((rows, TOKENS), BF),
            jax.ShapeDtypeStruct((KV_HEADS, GROUP, TOKENS), F32),
        ],
        compiler_params=params(32),
        cost_estimate=pl.CostEstimate(flops=2 * 2 * 32 * 128 * 640 * 128, bytes_accessed=2**22, transcendentals=32 * 128 * 640),
        name="attention_forward",
    )(here, lengths, q, *kvs)


def attention_backward(here, lengths, old, new, q, g, logs, kvs):
    kv_shape = (2, TOKENS, KV_HEADS * HEAD)
    return pl.pallas_call(
        backward_kernel,
        grid_spec=pltpu.PrefetchScalarGridSpec(
            num_scalar_prefetch=1,
            grid=(KV_HEADS,),
            in_specs=[ROW_SPEC, ROW_SPEC, ROW_SPEC, Q_SPEC, Q_SPEC, LOG_SPEC] + [KV_SPEC] * (BACK + 1),
            out_specs=[Q_SPEC, KV_SPEC] + [KV_SPEC] * BACK,
            scratch_shapes=[pltpu.VMEM((SPAN, TOKENS), F32), pltpu.VMEM((TOKENS, HEAD), F32)],
        ),
        out_shape=[
            jax.ShapeDtypeStruct(q.shape, F32),
            jax.ShapeDtypeStruct(kv_shape, F32),
        ]
        + [jax.ShapeDtypeStruct(kv_shape, BF)] * BACK,
        compiler_params=params(32),
        cost_estimate=pl.CostEstimate(flops=5 * 2 * 32 * 128 * 640 * 128, bytes_accessed=2**23, transcendentals=32 * 128 * 640),
        name="attention_backward",
    )(here, lengths, old, new, q, g, logs, *kvs)


def along_tokens(v, by):
    count = 1
    for axis in FLAT:
        count *= lax.axis_size(axis)
    return lax.ppermute(v, FLAT, [(i, i + by) for i in range(count) if 0 <= i + by < count])


def turn(v, axis, by):
    size = lax.axis_size(axis)
    return lax.ppermute(v, axis, [(i, (i + by) % size) for i in range(size)])


def shards(queries, keys, values, head_grads, cotangent, old, new, doc_lengths):
    here = lax.axis_index(FLAT).astype(jnp.int32).reshape(1)
    lengths = doc_lengths.reshape(1, -1)
    old = old.reshape(1, -1)
    new = new.reshape(1, -1)
    core = lax.axis_index("core")

    kv = jnp.stack([keys, values])
    kvs = [along_tokens(kv, by) for by in range(BACK, 0, -1)] + [kv]

    ratios = jnp.minimum(jnp.exp(new - old), CLIP).reshape(-1, 1)
    weighted = (ratios * cotangent.astype(F32)).astype(BF)
    halves = weighted.reshape(TOKENS, 4, 4, 2, 128).transpose(3, 0, 1, 2, 4).reshape(2, TOKENS, -1)
    keep = lax.dynamic_index_in_dim(halves, core, 0, keepdims=False)
    send = lax.dynamic_index_in_dim(halves, 1 - core, 0, keepdims=False)
    mine = jnp.concatenate([keep, turn(send, "core", 1)], axis=0)
    w_all = lax.all_gather(mine, "y", axis=0, tiled=False)

    out_t, logs = attention_forward(here, lengths, queries, kvs)
    parts = lax.all_to_all(out_t.reshape(2, 4, 512, TOKENS), "y", split_axis=1, concat_axis=1, tiled=True)
    other = turn(parts, "core", 1)
    o_all = jnp.stack([parts, other], axis=2)
    part = jnp.einsum("zycrt,yctn->zrn", o_all, w_all.reshape(4, 2, TOKENS, -1), preferred_element_type=F32).astype(BF)
    part = part.reshape(2, 512, 4, 4, 128).transpose(3, 2, 0, 1, 4)
    part = lax.psum_scatter(part, "x", scatter_dimension=0, tiled=False)
    part = part.reshape(8, 512, 128)
    grad_weight = lax.psum_scatter(part, ("zh", "zl"), scatter_dimension=0, tiled=False).astype(F32)

    dq, own, *backs = attention_backward(here, lengths, old, new, queries, head_grads, logs, kvs)
    home = [along_tokens(b, -(j + 1)).astype(F32) for j, b in enumerate(backs)]
    dkv = own + sum(home)
    return dq, dkv[0], dkv[1], grad_weight


def solution(mesh):
    mesh = Mesh(mesh.devices.reshape(4, 4, 2, 2, 4), FLAT)
    tokens = P(FLAT, None)
    return jax.shard_map(
        shards,
        mesh=mesh,
        in_specs=(tokens, tokens, tokens, tokens, tokens, P(FLAT), P(FLAT), P()),
        out_specs=(tokens, tokens, tokens, P(("zl", "y"), ("zh", "x", "core"))),
        check_vma=False,
    )
```

profile of v0, /device:TPU:1, one launch (start us, length us, event | category | flops | bytes accessed | tf_op | source)
XLA Modules:
  0.0 214.7 jit_solution(1067015600579800976)
XLA Ops:
  7.2 1.6 copy.26
  8.9 0.2 multiply_convert_fusion
  9.3 0.2 copy.29
  9.5 3.3 %collective-permute-start.9 = (bf16[128,2048]{1,0:T(8,128)(2,1)S(1)}, bf16[128,2048]{1,0:T(8,128)(2,1)S(1)}, u32[]{:S(2)}, u32[]{:S(2)}) collective-permute-start(bf16[128,2048]{1,0:T(8,128)(2,1)S(1)} %bitcast.46), channel_id=1, source_target_pairs={{0,8},{8,0},{1,9},{9,1},{2,10},{10,2},{3,11},{11,3},{4,12},{12,4},... | collective-permute-start | bytes 1572872 | tf_op jit(solution)/shard_map/ppermute | solution.py:197
  12.8 0.2 copy.28
  13.1 1.3 collective-permute-done.9
  14.4 1.0 pad_maximum_fusion
  15.5 1.9 collective-permute-start.3
  17.5 4.1 %collective-permute-start.2 = (bf16[2,128,512]{2,1,0:T(8,128)(2,1)S(1)}, bf16[2,128,512]{2,1,0:T(8,128)(2,1)S(1)}, u32[]{:S(2)}, u32[]{:S(2)}) collective-permute-start(bf16[2,128,512]{2,1,0:T(8,128)(2,1)S(1)} %pad_maximum_fusion.1.refs_4_), channel_id=1, source_target_pairs={{0,2},{1,3},{2,4},{3,5},{4,6},{5,7},{6,8},{7,9},{8,10},{9,11},{10,... | collective-permute-start | bytes 786440 | tf_op jit(solution)/shard_map/ppermute | solution.py:192
  21.6 4.3 %collective-permute-start.1 = (bf16[2,128,512]{2,1,0:T(8,128)(2,1)S(1)}, bf16[2,128,512]{2,1,0:T(8,128)(2,1)S(1)}, u32[]{:S(2)}, u32[]{:S(2)}) collective-permute-start(bf16[2,128,512]{2,1,0:T(8,128)(2,1)S(1)} %pad_maximum_fusion.1.refs_4_), channel_id=1, source_target_pairs={{0,3},{1,4},{2,5},{3,6},{4,7},{5,8},{6,9},{7,10},{8,11},{9,12},{10... | collective-permute-start | bytes 786440 | tf_op jit(solution)/shard_map/ppermute | solution.py:192
  25.9 3.2 %collective-permute-start = (bf16[2,128,512]{2,1,0:T(8,128)(2,1)S(1)}, bf16[2,128,512]{2,1,0:T(8,128)(2,1)S(1)}, u32[]{:S(2)}, u32[]{:S(2)}) collective-permute-start(bf16[2,128,512]{2,1,0:T(8,128)(2,1)S(1)} %pad_maximum_fusion.1.refs_4_), channel_id=1, source_target_pairs={{0,4},{1,5},{2,6},{3,7},{4,8},{5,9},{6,10},{7,11},{8,12},{9,13},{1... | collective-permute-start | bytes 786440 | tf_op jit(solution)/shard_map/ppermute | solution.py:192
  29.1 0.9 collective-permute-done.2.refs_2_
  30.0 4.1 %collective-permute-done.1.refs_1_ = bf16[2,128,512]{2,1,0:T(8,128)(2,1)S(1)} collective-permute-done((bf16[2,128,512]{2,1,0:T(8,128)(2,1)S(1)}, bf16[2,128,512]{2,1,0:T(8,128)(2,1)S(1)}, u32[]{:S(2)}, u32[]{:S(2)}) %collective-permute-start.1) | collective-permute-done | bytes 262176 | tf_op jit(solution)/shard_map/ppermute | solution.py:192
  34.1 1.1 collective-permute-done.refs_0_
  35.3 8.9 %attention_forward.1 = (bf16[4096,128]{1,0:T(8,128)(2,1)S(1)}, f32[4,8,128]{2,1,0:T(8,128)S(1)}) custom-call(s32[1]{0:T(128)} %bitcast.here_ref, s32[1,128]{1,0:T(1,128)S(1)} %bitcast.36, bf16[128,4096]{1,0:T(8,128)(2,1)S(1)} %copy-done, bf16[2,128,512]{2,1,0:T(8,128)(2,1)S(1)} %collective-permute-done.refs_0_, ...), custom_call_target="tpu_custom_call" | custom-call | flops 1342177280 | bytes 4194304 | tf_op jit(solution)/shard_map/attention_forward/pallas_call | solution.py:147
  44.3 34.3 %all_to_all.5 = bf16[2,4,512,128]{3,2,0,1:T(8,128)(2,1)S(1)} all-to-all(bf16[2,4,512,128]{3,2,0,1:T(8,128)(2,1)S(1)} %copy.23), channel_id=1, replica_groups=mesh['zh'=4,'x'=4,'core'=2,'zl'=2,'y'=4] {'y'}, dimensions={1} | all-to-all | bytes 2097152 | tf_op jit(solution)/shard_map/all_to_all | solution.py:219
  78.7 0.7 collective-permute-start.8
  79.3 2.4 %collective-permute-done.8 = bf16[2,4,512,128]{3,2,1,0:T(8,128)(2,1)} collective-permute-done((bf16[2,4,512,128]{3,2,1,0:T(8,128)(2,1)S(1)}, bf16[2,4,512,128]{3,2,1,0:T(8,128)(2,1)}, u32[]{:S(2)}, u32[]{:S(2)}) %collective-permute-start.8) | collective-permute-done | bytes 1048608 | tf_op jit(solution)/shard_map/ppermute | solution.py:197
  81.7 7.9 %bitcast_convert_fusion = bf16[2,512,2048]{2,1,0:T(8,128)(2,1)} fusion(bf16[4,2,128,2048,1]{3,2,1,0,4:T(8,128)(2,1)} %bitcast.49, bf16[2,4,1,512,128]{4,3,1,0,2:T(8,128)(2,1)} %bitcast.10, bf16[2,4,1,512,128]{4,3,1,0,2:T(8,128)(2,1)S(1)} %bitcast.45), kind=kOutput, calls=%fused_computation | convolution fusion | flops 4298113024 | bytes 10485760 | tf_op jit(solution)/shard_map/zycrt,yctn->zrn/dot_general | solution.py:222
  89.6 7.7 %reshape.51 = bf16[2,512,4,4,128]{4,3,2,1,0:T(4,128)(2,1)} reshape(bf16[2,512,2048]{2,1,0:T(8,128)(2,1)} %bitcast_convert_fusion) | data formatting | bytes 8388608 | tf_op jit(solution)/shard_map/reshape | solution.py:223
  97.4 5.2 %copy.41 = bf16[2,512,4,4,128]{4,1,0,2,3:T(8,128)(2,1)} copy(bf16[2,512,4,4,128]{4,3,2,1,0:T(4,128)(2,1)} %reshape.51) | data formatting | bytes 8388608 | tf_op jit(solution)/shard_map/reshape | solution.py:223
  102.7 53.3 %reduce-scatter.3.cloned.1.call-done = bf16[1,4,2,512,128]{4,3,2,1,0:T(8,128)(2,1)} async-done(((bf16[4,4,2,512,128]{4,3,2,1,0:T(8,128)(2,1)}), bf16[1,4,2,512,128]{4,3,2,1,0:T(8,128)(2,1)}) %reduce-scatter.3.cloned.1.call-update) | async-done | bytes 1048592 | tf_op jit(solution)/shard_map/reduce_scatter | solution.py:224
  156.0 11.8 %attention_backward.1 = (f32[128,4096]{1,0:T(8,128)}, f32[2,128,512]{2,1,0:T(8,128)S(1)}, bf16[2,128,512]{2,1,0:T(8,128)(2,1)S(1)}, bf16[2,128,512]{2,1,0:T(8,12...) custom-call(s32[1]{0:T(128)} %bitcast.here_ref, s32[1,128]{1,0:T(1,128)S(1)} %bitcast.37, ...), custom_call_target="tpu_custom_call" | custom-call | flops 3355443200 | bytes 8388608 | tf_op jit(solution)/shard_map/attention_backward/pallas_call | solution.py:168
  167.8 5.9 %collective-permute-start.4 = (bf16[2,128,512]{2,1,0:T(8,128)(2,1)S(1)}, bf16[2,128,512]{2,1,0:T(8,128)(2,1)S(1)}, u32[]{:S(2)}, u32[]{:S(2)}) collective-permute-start(bf16[2,128,512]{2,1,0:T(8,128)(2,1)S(1)} %get-tuple-element.15), channel_id=1, source_target_pairs={{1,0},{2,1},{3,2},{4,3},{5,4},{6,5},{7,6},{8,7},{9,8},{10,9},{11,1... | collective-permute-start | bytes 786440 | tf_op jit(solution)/shard_map/ppermute | solution.py:192
  173.7 2.7 %collective-permute-start.5 = (bf16[2,128,512]{2,1,0:T(8,128)(2,1)S(1)}, bf16[2,128,512]{2,1,0:T(8,128)(2,1)S(1)}, u32[]{:S(2)}, u32[]{:S(2)}) collective-permute-start(bf16[2,128,512]{2,1,0:T(8,128)(2,1)S(1)} %get-tuple-element.16), channel_id=1, source_target_pairs={{2,0},{3,1},{4,2},{5,3},{6,4},{7,5},{8,6},{9,7},{10,8},{11,9},{12,... | collective-permute-start | bytes 786440 | tf_op jit(solution)/shard_map/ppermute | solution.py:192
  176.4 2.7 %collective-permute-start.6 = (bf16[2,128,512]{2,1,0:T(8,128)(2,1)S(1)}, bf16[2,128,512]{2,1,0:T(8,128)(2,1)S(1)}, u32[]{:S(2)}, u32[]{:S(2)}) collective-permute-start(bf16[2,128,512]{2,1,0:T(8,128)(2,1)S(1)} %get-tuple-element.17), channel_id=1, source_target_pairs={{3,0},{4,1},{5,2},{6,3},{7,4},{8,5},{9,6},{10,7},{11,8},{12,9},{13... | collective-permute-start | bytes 786440 | tf_op jit(solution)/shard_map/ppermute | solution.py:192
  179.1 1.9 collective-permute-start.7
  181.1 3.9 %collective-permute-done.5 = bf16[2,128,512]{2,1,0:T(8,128)(2,1)S(1)} collective-permute-done((bf16[2,128,512]{2,1,0:T(8,128)(2,1)S(1)}, bf16[2,128,512]{2,1,0:T(8,128)(2,1)S(1)}, u32[]{:S(2)}, u32[]{:S(2)}) %collective-permute-start.5) | collective-permute-done | bytes 262176 | tf_op jit(solution)/shard_map/ppermute | solution.py:192
  185.0 3.7 %collective-permute-done.6 = bf16[2,128,512]{2,1,0:T(8,128)(2,1)S(1)} collective-permute-done((bf16[2,128,512]{2,1,0:T(8,128)(2,1)S(1)}, bf16[2,128,512]{2,1,0:T(8,128)(2,1)S(1)}, u32[]{:S(2)}, u32[]{:S(2)}) %collective-permute-start.6) | collective-permute-done | bytes 262176 | tf_op jit(solution)/shard_map/ppermute | solution.py:192
  188.7 16.9 %collective-permute-done.7 = bf16[2,128,512]{2,1,0:T(8,128)(2,1)S(1)} collective-permute-done((bf16[2,128,512]{2,1,0:T(8,128)(2,1)S(1)}, bf16[2,128,512]{2,1,0:T(8,128)(2,1)S(1)}, u32[]{:S(2)}, u32[]{:S(2)}) %collective-permute-start.7) | collective-permute-done | bytes 262176 | tf_op jit(solution)/shard_map/ppermute | solution.py:192
  205.7 0.8 slice_bitcast_fusion
  206.6 1.6 bitcast_convert_fusion.1
  (31 shorter events, 0.7 us)
Async XLA Ops:
  7.2 1.7 copy-start.4
  7.2 1.7 copy-start.3
  7.2 74.5 %all-gather.3.cloned.1.call-start = ((), (), s32[]{:S(2)}) async-start(), calls=%async_computation.5 | async-start | bytes 5242880 | tf_op jit(solution)/shard_map/all_gather | solution.py:216
  9.5 4.9 %collective-permute-start.9 = (bf16[128,2048]{1,0:T(8,128)(2,1)S(1)}, bf16[128,2048]{1,0:T(8,128)(2,1)S(1)}, u32[]{:S(2)}, u32[]{:S(2)}) collective-permute-start(bf16[128,2048]{1,0:T(8,128)(2,1)S(1)} %bitcast.46), channel_id=1, source_target_pairs={{0,8},{8,0},{1,9},{9,1},{2,10},{10,2},{3,11},{11,3},{4,12},{12,4},... | collective-permute-start | bytes 1572872 | tf_op jit(solution)/shard_map/ppermute | solution.py:197
  12.8 2.7 %copy-start.5 = (bf16[128,512]{1,0:T(8,128)(2,1)S(1)}, bf16[128,512]{1,0:T(8,128)(2,1)}, u32[]{:S(2)}) copy-start(bf16[128,512]{1,0:T(8,128)(2,1)} %param.10) | copy-start | bytes 393220
  12.8 2.7 %copy-start.6 = (bf16[128,512]{1,0:T(8,128)(2,1)S(1)}, bf16[128,512]{1,0:T(8,128)(2,1)}, u32[]{:S(2)}) copy-start(bf16[128,512]{1,0:T(8,128)(2,1)} %param.9) | copy-start | bytes 393220
  13.1 22.2 %copy-start = (bf16[128,4096]{1,0:T(8,128)(2,1)S(1)}, bf16[128,4096]{1,0:T(8,128)(2,1)}, u32[]{:S(2)}) copy-start(bf16[128,4096]{1,0:T(8,128)(2,1)} %q_ref.3) | copy-start | bytes 3145732
  13.1 22.2 %copy-start.2 = (s32[128]{0:T(128)S(1)}, s32[128]{0:T(128)}, u32[]{:S(2)}) copy-start(s32[128]{0:T(128)} %param.15) | copy-start | bytes 1540
  15.4 140.5 %reduce-scatter.3.cloned.1.call-start = ((), (), s32[]{:S(2)}) async-start(), calls=%async_computation.3 | async-start | bytes 5242880 | tf_op jit(solution)/shard_map/reduce_scatter | solution.py:224
  15.5 13.6 %collective-permute-start.3 = (bf16[2,128,512]{2,1,0:T(8,128)(2,1)S(1)}, bf16[2,128,512]{2,1,0:T(8,128)(2,1)S(1)}, u32[]{:S(2)}, u32[]{:S(2)}) collective-permute-start(bf16[2,128,512]{2,1,0:T(8,128)(2,1)S(1)} %pad_maximum_fusion.1.refs_4_), channel_id=1, source_target_pairs={{0,1},{1,2},{2,3},{3,4},{4,5},{5,6},{6,7},{7,8},{8,9},{9,10},{10,1... | collective-permute-start | bytes 786440 | tf_op jit(solution)/shard_map/ppermute | solution.py:192
  17.5 12.5 %collective-permute-start.2 = (bf16[2,128,512]{2,1,0:T(8,128)(2,1)S(1)}, bf16[2,128,512]{2,1,0:T(8,128)(2,1)S(1)}, u32[]{:S(2)}, u32[]{:S(2)}) collective-permute-start(bf16[2,128,512]{2,1,0:T(8,128)(2,1)S(1)} %pad_maximum_fusion.1.refs_4_), channel_id=1, source_target_pairs={{0,2},{1,3},{2,4},{3,5},{4,6},{5,7},{6,8},{7,9},{8,10},{9,11},{10,... | collective-permute-start | bytes 786440 | tf_op jit(solution)/shard_map/ppermute | solution.py:192
  21.6 12.6 %collective-permute-start.1 = (bf16[2,128,512]{2,1,0:T(8,128)(2,1)S(1)}, bf16[2,128,512]{2,1,0:T(8,128)(2,1)S(1)}, u32[]{:S(2)}, u32[]{:S(2)}) collective-permute-start(bf16[2,128,512]{2,1,0:T(8,128)(2,1)S(1)} %pad_maximum_fusion.1.refs_4_), channel_id=1, source_target_pairs={{0,3},{1,4},{2,5},{3,6},{4,7},{5,8},{6,9},{7,10},{8,11},{9,12},{10... | collective-permute-start | bytes 786440 | tf_op jit(solution)/shard_map/ppermute | solution.py:192
  25.9 9.4 %collective-permute-start = (bf16[2,128,512]{2,1,0:T(8,128)(2,1)S(1)}, bf16[2,128,512]{2,1,0:T(8,128)(2,1)S(1)}, u32[]{:S(2)}, u32[]{:S(2)}) collective-permute-start(bf16[2,128,512]{2,1,0:T(8,128)(2,1)S(1)} %pad_maximum_fusion.1.refs_4_), channel_id=1, source_target_pairs={{0,4},{1,5},{2,6},{3,7},{4,8},{5,9},{6,10},{7,11},{8,12},{9,13},{1... | collective-permute-start | bytes 786440 | tf_op jit(solution)/shard_map/ppermute | solution.py:192
  78.7 3.1 %collective-permute-start.8 = (bf16[2,4,512,128]{3,2,1,0:T(8,128)(2,1)S(1)}, bf16[2,4,512,128]{3,2,1,0:T(8,128)(2,1)}, u32[]{:S(2)}, u32[]{:S(2)}) collective-permute-start(bf16[2,4,512,128]{3,2,1,0:T(8,128)(2,1)S(1)} %copy.42), channel_id=1, source_target_pairs={{0,8},{8,0},{1,9},{9,1},{2,10},{10,2},{3,11},{11,3},{4,12},{12,4},... | collective-permute-start | bytes 3145736 | tf_op jit(solution)/shard_map/ppermute | solution.py:197
  102.6 53.4 %copy-start.1 = (bf16[128,4096]{1,0:T(8,128)(2,1)S(1)}, bf16[128,4096]{1,0:T(8,128)(2,1)}, u32[]{:S(2)}) copy-start(bf16[128,4096]{1,0:T(8,128)(2,1)} %g_ref.1) | copy-start | bytes 3145732
  102.6 103.9 %reduce-scatter.5.cloned.1.call-start = ((), (), s32[]{:S(2)}) async-start(), calls=%async_computation.4 | async-start | bytes 1179648 | tf_op jit(solution)/shard_map/reduce_scatter | solution.py:226
  167.8 13.2 %collective-permute-start.4 = (bf16[2,128,512]{2,1,0:T(8,128)(2,1)S(1)}, bf16[2,128,512]{2,1,0:T(8,128)(2,1)S(1)}, u32[]{:S(2)}, u32[]{:S(2)}) collective-permute-start(bf16[2,128,512]{2,1,0:T(8,128)(2,1)S(1)} %get-tuple-element.15), channel_id=1, source_target_pairs={{1,0},{2,1},{3,2},{4,3},{5,4},{6,5},{7,6},{8,7},{9,8},{10,9},{11,1... | collective-permute-start | bytes 786440 | tf_op jit(solution)/shard_map/ppermute | solution.py:192
  173.7 11.3 %collective-permute-start.5 = (bf16[2,128,512]{2,1,0:T(8,128)(2,1)S(1)}, bf16[2,128,512]{2,1,0:T(8,128)(2,1)S(1)}, u32[]{:S(2)}, u32[]{:S(2)}) collective-permute-start(bf16[2,128,512]{2,1,0:T(8,128)(2,1)S(1)} %get-tuple-element.16), channel_id=1, source_target_pairs={{2,0},{3,1},{4,2},{5,3},{6,4},{7,5},{8,6},{9,7},{10,8},{11,9},{12,... | collective-permute-start | bytes 786440 | tf_op jit(solution)/shard_map/ppermute | solution.py:192
  176.4 12.2 %collective-permute-start.6 = (bf16[2,128,512]{2,1,0:T(8,128)(2,1)S(1)}, bf16[2,128,512]{2,1,0:T(8,128)(2,1)S(1)}, u32[]{:S(2)}, u32[]{:S(2)}) collective-permute-start(bf16[2,128,512]{2,1,0:T(8,128)(2,1)S(1)} %get-tuple-element.17), channel_id=1, source_target_pairs={{3,0},{4,1},{5,2},{6,3},{7,4},{8,5},{9,6},{10,7},{11,8},{12,9},{13... | collective-permute-start | bytes 786440 | tf_op jit(solution)/shard_map/ppermute | solution.py:192
  179.1 26.4 %collective-permute-start.7 = (bf16[2,128,512]{2,1,0:T(8,128)(2,1)S(1)}, bf16[2,128,512]{2,1,0:T(8,128)(2,1)S(1)}, u32[]{:S(2)}, u32[]{:S(2)}) collective-permute-start(bf16[2,128,512]{2,1,0:T(8,128)(2,1)S(1)} %get-tuple-element.18), channel_id=1, source_target_pairs={{4,0},{5,1},{6,2},{7,3},{8,4},{9,5},{10,6},{11,7},{12,8},{13,9},{1... | collective-permute-start | bytes 786440 | tf_op jit(solution)/shard_map/ppermute | solution.py:192
Sparse Core Ops, SparseCore 0:
  15.6 62.9 all-gather.2
  102.7 53.1 reduce-scatter.2
  158.7 35.4 reduce-scatter.4
where the time goes:
time: 215 us
  waiting for transfers between devices  87.7 us (41%)
  blocking collectives  34.3 us (16%)
  starting transfers between devices  30.8 us (14%)
  Pallas kernels  20.7 us (10%)
  local copies, waits for them, and re-layouts  16.2 us (8%)
  between operations  14 us (7%)
  matrix products  7.91 us (4%)
  other arithmetic  3.09 us (1%)
    reduce_scatter x1, waiting for transfers between devices, shards(): part = lax.psum_scatter(part, 'x', scatter_dimension=0, tiled=False)  53.3 us
    all_to_all x1, blocking collectives, shards(): lax.all_to_all(out_t.reshape(2, 4, 512, TOKENS), 'y', split_axis=1, conca...  34.3 us
    ppermute x8, waiting for transfers between devices, along_tokens(): lax.ppermute(v, FLAT, [(i, i + by) for i in range(count) if 0 <= i + by <...  30.6 us
    ppermute x8, starting transfers between devices, along_tokens(): lax.ppermute(v, FLAT, [(i, i + by) for i in range(count) if 0 <= i + by <...  26.7 us
    reshape x2, local copies, waits for them, and re-layouts, shards(): part = part.reshape(2, 512, 4, 4, 128).transpose(3, 2, 0, 1, 4)  13 us
    pallas_call x1, Pallas kernels, attention_backward(): pl.pallas_call(backward_kernel, grid_spec=pltpu.PrefetchScalarGridSpec(nu...  11.8 us
    pallas_call x1, Pallas kernels, attention_forward(): pl.pallas_call(forward_kernel, grid_spec=pltpu.PrefetchScalarGridSpec(num...  8.9 us
    dot_general x1, matrix products, shards(): jnp.einsum('zycrt,yctn->zrn', o_all, w_all.reshape(4, 2, TOKENS, -1), pre...  7.91 us
  transfers between devices with their start and end apart: 13, of which 9 were waited for; matrix products, arithmetic and copies ran while one was open for 1% of the time, Pallas kernels for 10%

commit v1 on v0

--- a/solution.py
+++ b/solution.py
@@ -1,3 +1,4 @@
+import itertools
 import math
 
 import jax
@@ -13,6 +14,8 @@
 SPAN = (BACK + 1) * TOKENS
 KV_HEADS = 4
 GROUP = 8
+ZH, ZL, RING = 4, 2, 4
+ROWS = 1024
 CLIP = 2.0
 NEG = -1e30
 SCALE = 1.0 / math.sqrt(HEAD)
@@ -157,7 +160,7 @@
             jax.ShapeDtypeStruct((rows, TOKENS), BF),
             jax.ShapeDtypeStruct((KV_HEADS, GROUP, TOKENS), F32),
         ],
-        compiler_params=params(32),
+        compiler_params=params(10),
         cost_estimate=pl.CostEstimate(flops=2 * 2 * 32 * 128 * 640 * 128, bytes_accessed=2**22, transcendentals=32 * 128 * 640),
         name="attention_forward",
     )(here, lengths, q, *kvs)
@@ -179,22 +182,100 @@
             jax.ShapeDtypeStruct(kv_shape, F32),
         ]
         + [jax.ShapeDtypeStruct(kv_shape, BF)] * BACK,
-        compiler_params=params(32),
+        compiler_params=params(14),
         cost_estimate=pl.CostEstimate(flops=5 * 2 * 32 * 128 * 640 * 128, bytes_accessed=2**23, transcendentals=32 * 128 * 640),
         name="attention_backward",
     )(here, lengths, old, new, q, g, logs, *kvs)
 
 
 def along_tokens(v, by):
-    count = 1
-    for axis in FLAT:
-        count *= lax.axis_size(axis)
+    count = math.prod(lax.axis_size(axis) for axis in FLAT)
     return lax.ppermute(v, FLAT, [(i, i + by) for i in range(count) if 0 <= i + by < count])
 
 
-def turn(v, axis, by):
-    size = lax.axis_size(axis)
-    return lax.ppermute(v, axis, [(i, (i + by) % size) for i in range(size)])
+def moved(v, to):
+    sizes = [lax.axis_size(axis) for axis in FLAT]
+    pairs = []
+    for i, at in enumerate(itertools.product(*map(range, sizes))):
+        there = to(*at)
+        if there is not None:
+            pairs.append((i, sum(c * math.prod(sizes[j + 1 :]) for j, c in enumerate(there))))
+    return lax.ppermute(v, FLAT, pairs)
+
+
+def core_swap(v):
+    return moved(v, lambda zh, x, c, zl, y: (zh, x, 1 - c, zl, y))
+
+
+def group_turn(v, by):
+    return moved(v, lambda zh, x, c, zl, y: (zh, (x + by * c) % RING, c, zl, (y + by * (1 - c)) % RING))
+
+
+def reduce_turn(v, by):
+    return moved(v, lambda zh, x, c, zl, y: (zh, (x + by * (1 - c)) % RING, c, zl, (y + by * c) % RING))
+
+
+def transposed(v):
+    return moved(v, lambda zh, x, c, zl, y: (zh, y, c, zl, x) if c == 1 and x != y else None)
+
+
+def weigh_kernel(core_ref, old_ref, new_ref, cot_ref, keep_ref, send_ref):
+    ratio = ratio_column(old_ref, new_ref)
+    for out_ref, half in ((keep_ref, core_ref[0]), (send_ref, 1 - core_ref[0])):
+        for chunk in range(RING):
+            for zh in range(ZH):
+                at = pl.multiple_of((zh * 2 * RING + chunk * 2 + half) * HEAD, HEAD)
+                to = (chunk * ZH + zh) * HEAD
+                part = cot_ref[:, pl.ds(at, HEAD)].astype(F32) * ratio
+                out_ref[:, to : to + HEAD] = part.astype(BF)
+
+
+def weigh(core, old, new, cotangent):
+    half = jax.ShapeDtypeStruct((TOKENS, cotangent.shape[1] // 2), BF)
+    smem = pl.BlockSpec(memory_space=pltpu.SMEM)
+    vmem = pl.BlockSpec(memory_space=pltpu.VMEM)
+    return pl.pallas_call(
+        weigh_kernel,
+        in_specs=[smem, vmem, vmem, vmem],
+        out_specs=[vmem, vmem],
+        out_shape=[half, half],
+        compiler_params=params(8),
+        cost_estimate=pl.CostEstimate(flops=2**20, bytes_accessed=2**21, transcendentals=0),
+        name="weigh",
+    )(core, old, new, cotangent)
+
+
+def product_kernel(first_ref, *refs):
+    o_refs, w_refs, out_refs = refs[:RING], refs[RING : 2 * RING], refs[2 * RING :]
+    lhs = jnp.concatenate([r[c].reshape(ROWS, TOKENS) for r in o_refs for c in range(2)], axis=1)
+    rhs = jnp.concatenate([r[...] for r in w_refs], axis=0)
+    part = dot(lhs, rhs).astype(BF)
+    for step, ref in enumerate(out_refs):
+
+        @pl.when(pl.program_id(0) == step)
+        def _(ref=ref):
+            for zh in range(ZH):
+                for zl in range(ZL):
+                    ref[zh * ZL + zl] = part[zl * ROWS // ZL : (zl + 1) * ROWS // ZL, zh * HEAD : (zh + 1) * HEAD]
+
+
+def product(first, count, outs, ws):
+    chunk = (ZH * ZL, ROWS // ZL, HEAD)
+    width = ZH * HEAD
+    return pl.pallas_call(
+        product_kernel,
+        grid_spec=pltpu.PrefetchScalarGridSpec(
+            num_scalar_prefetch=1,
+            grid=(count,),
+            in_specs=[pl.BlockSpec((2, ZL, ROWS // ZL, TOKENS), lambda i, f: (0, 0, 0, 0), pipeline_mode=pl.Buffered(1))] * RING
+            + [pl.BlockSpec((2 * TOKENS, width), lambda i, f: (0, lax.rem(f[0] + i, RING)))] * RING,
+            out_specs=[pl.BlockSpec(chunk, lambda i, f: (0, 0, 0), pipeline_mode=pl.Buffered(1))] * count,
+        ),
+        out_shape=[jax.ShapeDtypeStruct(chunk, BF)] * count,
+        compiler_params=params(22),
+        cost_estimate=pl.CostEstimate(flops=2 * ROWS * 1024 * width * count, bytes_accessed=2**21 * (1 + count), transcendentals=0),
+        name="product",
+    )(first, *outs, *ws)
 
 
 def shards(queries, keys, values, head_grads, cotangent, old, new, doc_lengths):
@@ -202,37 +283,46 @@
     lengths = doc_lengths.reshape(1, -1)
     old = old.reshape(1, -1)
     new = new.reshape(1, -1)
-    core = lax.axis_index("core")
+    core, x, y = (lax.axis_index(a).astype(jnp.int32) for a in ("core", "x", "y"))
+    in_group = jnp.where(core == 0, y, x)
+    in_reduce = jnp.where(core == 0, x, y)
 
     kv = jnp.stack([keys, values])
     kvs = [along_tokens(kv, by) for by in range(BACK, 0, -1)] + [kv]
 
-    ratios = jnp.minimum(jnp.exp(new - old), CLIP).reshape(-1, 1)
-    weighted = (ratios * cotangent.astype(F32)).astype(BF)
-    halves = weighted.reshape(TOKENS, 4, 4, 2, 128).transpose(3, 0, 1, 2, 4).reshape(2, TOKENS, -1)
-    keep = lax.dynamic_index_in_dim(halves, core, 0, keepdims=False)
-    send = lax.dynamic_index_in_dim(halves, 1 - core, 0, keepdims=False)
-    mine = jnp.concatenate([keep, turn(send, "core", 1)], axis=0)
-    w_all = lax.all_gather(mine, "y", axis=0, tiled=False)
-
-    out_t, logs = attention_forward(here, lengths, queries, kvs)
-    parts = lax.all_to_all(out_t.reshape(2, 4, 512, TOKENS), "y", split_axis=1, concat_axis=1, tiled=True)
-    other = turn(parts, "core", 1)
-    o_all = jnp.stack([parts, other], axis=2)
-    part = jnp.einsum("zycrt,yctn->zrn", o_all, w_all.reshape(4, 2, TOKENS, -1), preferred_element_type=F32).astype(BF)
-    part = part.reshape(2, 512, 4, 4, 128).transpose(3, 2, 0, 1, 4)
-    part = lax.psum_scatter(part, "x", scatter_dimension=0, tiled=False)
-    part = part.reshape(8, 512, 128)
-    grad_weight = lax.psum_scatter(part, ("zh", "zl"), scatter_dimension=0, tiled=False).astype(F32)
+    kv, cotangent = lax.optimization_barrier((kv, cotangent))
+    keep, send = weigh(core.reshape(1), old, new, cotangent)
+    w_mine = jnp.concatenate([keep, core_swap(send)], axis=0)
+    ws = [w_mine] + [group_turn(w_mine, by) for by in range(1, RING)]
+
+    here_after, ws[2] = lax.optimization_barrier((here, ws[2]))
+    out_t, logs = attention_forward(here_after, lengths, queries, kvs)
+    out_both = jnp.stack([out_t, core_swap(out_t)]).reshape(2, ZL, RING, ROWS // ZL, TOKENS)
+
+    def rows_of(by):
+        return lax.dynamic_index_in_dim(out_both, (in_group + by) % RING, 2, keepdims=False)
+
+    outs = [rows_of(0)] + [group_turn(rows_of(by), by) for by in range(1, RING)]
 
     dq, own, *backs = attention_backward(here, lengths, old, new, queries, head_grads, logs, kvs)
-    home = [along_tokens(b, -(j + 1)).astype(F32) for j, b in enumerate(backs)]
-    dkv = own + sum(home)
+    *outs, own = lax.optimization_barrier((*outs, own))
+    home = [along_tokens(b, -(j + 1)) for j, b in enumerate(backs)]
+
+    sent = product(((in_reduce + 1) % RING).reshape(1), RING - 1, outs, ws)
+    got = [reduce_turn(part, by) for by, part in enumerate(sent, 1)]
+    (mine,) = product(in_reduce.reshape(1), 1, outs, ws)
+    part = sum((g.astype(F32) for g in got), mine.astype(F32)).astype(BF)
+    *home, part = lax.optimization_barrier((*home, part))
+    part = lax.all_to_all(part, ("zh", "zl"), split_axis=0, concat_axis=0, tiled=True)
+    total = jnp.sum(part.astype(F32), axis=0).astype(BF)
+
+    dkv = own + sum(b.astype(F32) for b in home)
+    grad_weight = jnp.where((core == 1) & (x != y), transposed(total), total).astype(F32)
     return dq, dkv[0], dkv[1], grad_weight
 
 
 def solution(mesh):
-    mesh = Mesh(mesh.devices.reshape(4, 4, 2, 2, 4), FLAT)
+    mesh = Mesh(mesh.devices.reshape(ZH, RING, 2, ZL, RING), FLAT)
     tokens = P(FLAT, None)
     return jax.shard_map(
         shards,

time: 215 us -> 179 us (0.83)
  the two profiles are of different devices: /device:TPU:1 before, /device:TPU:17 now
where the time goes in v1:
time: 179 us; the launch traced here: 178 us
  starting transfers between devices  66.6 us (37%)
  waiting for transfers between devices  60 us (34%)
  Pallas kernels  29.3 us (16%)
  local copies, waits for them, and re-layouts  15.2 us (8%)
  other arithmetic  6.01 us (3%)
    ppermute x8, starting transfers between devices, along_tokens(): lax.ppermute(v, FLAT, [(i, i + by) for i in range(count) if 0 <= i + by <...  44.5 us
    all_to_all x1, waiting for transfers between devices, shards(): lax.all_to_all(part, ('zh', 'zl'), split_axis=0, concat_axis=0, tiled=True)  28.9 us
    ppermute x8, waiting for transfers between devices, along_tokens(): lax.ppermute(v, FLAT, [(i, i + by) for i in range(count) if 0 <= i + by <...  21.8 us
    ppermute x12, starting transfers between devices, moved(): return lax.ppermute(v, FLAT, pairs)  14.7 us
    unnamed x47, local copies, waits for them, and re-layouts  14.4 us
    pallas_call x1, Pallas kernels, attention_backward(): pl.pallas_call(backward_kernel, grid_spec=pltpu.PrefetchScalarGridSpec(nu...  11.8 us
    ppermute x12, waiting for transfers between devices, moved(): return lax.ppermute(v, FLAT, pairs)  9.32 us
    pallas_call x1, Pallas kernels, attention_forward(): pl.pallas_call(forward_kernel, grid_spec=pltpu.PrefetchScalarGridSpec(num...  8.89 us
  transfers between devices with their start and end apart: 21, of which 11 were waited for; matrix products, arithmetic and copies ran while one was open for 3% of the time, Pallas kernels for 8%

profile of v1, /device:TPU:17, one launch (start us, length us, event | category | flops | bytes accessed | tf_op | source)
XLA Modules:
  0.0 178.0 jit_solution(551533328707044220)
XLA Ops:
  1.7 1.2 copy-done
  5.4 1.5 collective-permute-done
  7.0 2.8 %collective-permute-start.1 = (bf16[256,2048]{1,0:T(8,128)(2,1)S(1)}, bf16[256,2048]{1,0:T(8,128)(2,1)S(1)}, u32[]{:S(2)}, u32[]{:S(2)}) collective-permute-start(bf16[256,2048]{1,0:T(8,128)(2,1)S(1)} %constant_dynamic-update-slice_fusion.refs_4_), channel_id=1, source_target_pairs={{0,2},{1,3},{2,0},{3,1},{4,6},{5,7},{6,4},{7,5},{8,40},{9,41},{10,... | collective-permute-start | bytes 3145736 | tf_op jit(solution)/shard_map/ppermute | solution.py:203
  9.8 2.9 %collective-permute-start.5 = (bf16[2,128,512]{2,1,0:T(8,128)(2,1)S(1)}, bf16[2,128,512]{2,1,0:T(8,128)(2,1)S(1)}, u32[]{:S(2)}, u32[]{:S(2)}) collective-permute-start(bf16[2,128,512]{2,1,0:T(8,128)(2,1)S(1)} %pad_maximum_fusion.refs_4_), channel_id=1, source_target_pairs={{0,1},{1,2},{2,3},{3,4},{4,5},{5,6},{6,7},{7,8},{8,9},{9,10},{10,1... | collective-permute-start | bytes 786440 | tf_op jit(solution)/shard_map/ppermute | solution.py:193
  12.7 3.6 %collective-permute-start.4 = (bf16[2,128,512]{2,1,0:T(8,128)(2,1)S(1)}, bf16[2,128,512]{2,1,0:T(8,128)(2,1)S(1)}, u32[]{:S(2)}, u32[]{:S(2)}) collective-permute-start(bf16[2,128,512]{2,1,0:T(8,128)(2,1)S(1)} %pad_maximum_fusion.refs_4_), channel_id=1, source_target_pairs={{0,2},{1,3},{2,4},{3,5},{4,6},{5,7},{6,8},{7,9},{8,10},{9,11},{10,... | collective-permute-start | bytes 786440 | tf_op jit(solution)/shard_map/ppermute | solution.py:193
  16.3 3.9 %collective-permute-start.3 = (bf16[2,128,512]{2,1,0:T(8,128)(2,1)S(1)}, bf16[2,128,512]{2,1,0:T(8,128)(2,1)S(1)}, u32[]{:S(2)}, u32[]{:S(2)}) collective-permute-start(bf16[2,128,512]{2,1,0:T(8,128)(2,1)S(1)} %pad_maximum_fusion.refs_4_), channel_id=1, source_target_pairs={{0,3},{1,4},{2,5},{3,6},{4,7},{5,8},{6,9},{7,10},{8,11},{9,12},{10... | collective-permute-start | bytes 786440 | tf_op jit(solution)/shard_map/ppermute | solution.py:193
  20.2 4.1 %collective-permute-start.2 = (bf16[2,128,512]{2,1,0:T(8,128)(2,1)S(1)}, bf16[2,128,512]{2,1,0:T(8,128)(2,1)S(1)}, u32[]{:S(2)}, u32[]{:S(2)}) collective-permute-start(bf16[2,128,512]{2,1,0:T(8,128)(2,1)S(1)} %pad_maximum_fusion.refs_4_), channel_id=1, source_target_pairs={{0,4},{1,5},{2,6},{3,7},{4,8},{5,9},{6,10},{7,11},{8,12},{9,13},{1... | collective-permute-start | bytes 786440 | tf_op jit(solution)/shard_map/ppermute | solution.py:193
  25.3 6.4 %collective-permute-done.5.refs_3_ = bf16[2,128,512]{2,1,0:T(8,128)(2,1)S(1)} collective-permute-done((bf16[2,128,512]{2,1,0:T(8,128)(2,1)S(1)}, bf16[2,128,512]{2,1,0:T(8,128)(2,1)S(1)}, u32[]{:S(2)}, u32[]{:S(2)}) %collective-permute-start.5) | collective-permute-done | bytes 262176 | tf_op jit(solution)/shard_map/ppermute | solution.py:193
  31.7 2.2 %collective-permute-done.3.refs_1_ = bf16[2,128,512]{2,1,0:T(8,128)(2,1)S(1)} collective-permute-done((bf16[2,128,512]{2,1,0:T(8,128)(2,1)S(1)}, bf16[2,128,512]{2,1,0:T(8,128)(2,1)S(1)}, u32[]{:S(2)}, u32[]{:S(2)}) %collective-permute-start.3) | collective-permute-done | bytes 262176 | tf_op jit(solution)/shard_map/ppermute | solution.py:193
  34.6 4.9 %collective-permute-done.2.refs_0_ = bf16[2,128,512]{2,1,0:T(8,128)(2,1)S(1)} collective-permute-done((bf16[2,128,512]{2,1,0:T(8,128)(2,1)S(1)}, bf16[2,128,512]{2,1,0:T(8,128)(2,1)S(1)}, u32[]{:S(2)}, u32[]{:S(2)}) %collective-permute-start.2) | collective-permute-done | bytes 262176 | tf_op jit(solution)/shard_map/ppermute | solution.py:193
  40.2 1.2 copy-done.7
  43.4 8.9 %attention_forward.1 = (bf16[4096,128]{1,0:T(8,128)(2,1)S(1)}, f32[4,8,128]{2,1,0:T(8,128)S(1)}) custom-call(s32[1]{0:T(128)} %bitcast.here_ref, s32[1,128]{1,0:T(1,128)S(1)} %bitcast.36, bf16[128,4096]{1,0:T(8,128)(2,1)S(1)} %copy-done.7, bf16[2,128,512]{2,1,0:T(8,128)(2,1)S(1)} %copy-done.18, bf16[2,128,512]{2,1,0:T(8,128)(2,1)S(1)} %copy-done.15, ...), custom_call_target="tpu_custom_call" | custom-call | flops 1342177280 | bytes 4194304 | tf_op jit(solution)/shard_map/attention_forward/pallas_call | solution.py:150
  53.4 1.5 collective-permute-start.14
  55.8 2.4 %fusion.1 = (bf16[2,2,512,128]{3,2,1,0:T(8,128)(2,1)}, bf16[2,2,512,128]{3,2,1,0:T(8,128)(2,1)S(1)}, bf16[2,2,512,128]{3,2,1,0:T(8,128)(2,1)}, bf16[2,2,512,128]{3,2,1,0:T(8,128)(2,1)}) fusion(s32[]{:T(128)S(6)} %select_n.58, bf16[1,2,4,512,128]{4,3,2,1,0:T(8,128)(2,1)S(1)} %bitcast.31, bf16[1,2,4,512,128]{4,3,2,1,0:T(8,128)(2,1)} %bitcast.8, ...), kind=kLoop, calls=%fused_computation.10 | loop fusion | flops 1048576 | bytes 4194320 | tf_op jit(solution)/shard_map/jit(dynamic_index_in_dim)/squeeze | solution.py:303
  59.7 1.2 copy-done.8
  60.9 1.2 copy-done.9
  66.0 11.8 %attention_backward.1 = (f32[128,4096]{1,0:T(8,128)}, f32[2,128,512]{2,1,0:T(8,128)S(1)}, bf16[2,128,512]{2,1,0:T(8,128)(2,1)S(1)}, bf16[2,128,512]{2,1,0:T(8,12...) custom-call(s32[1]{0:T(128)} %bitcast.here_ref, s32[1,128]{1,0:T(1,128)S(1)} %bitcast.37, ...), custom_call_target="tpu_custom_call" | custom-call | flops 3355443200 | bytes 8388608 | tf_op jit(solution)/shard_map/attention_backward/pallas_call | solution.py:171
  77.8 2.0 %collective-permute-done.7.refs_1_ = bf16[2,2,512,128]{3,2,1,0:T(8,128)(2,1)S(1)} collective-permute-done((bf16[2,2,512,128]{3,2,1,0:T(8,128)(2,1)}, bf16[2,2,512,128]{3,2,1,0:T(8,128)(2,1)S(1)}, u32[]{:S(2)}, u32[]{:S(2)}) %collective-permute-start.7) | collective-permute-done | bytes 524320 | tf_op jit(solution)/shard_map/ppermute | solution.py:203
  79.8 5.7 %product.3 = (bf16[8,512,128]{2,1,0:T(8,128)(2,1)S(1)}, bf16[8,512,128]{2,1,0:T(8,128)(2,1)S(1)}, bf16[8,512,128]{2,1,0:T(8,128)(2,1)S(1)}) custom-call(s32[1]{0:T(128)} %bitcast.14.first_ref, bf16[2,2,512,128]{3,2,1,0:T(8,128)(2,1)S(1)} %get-tuple-element.43.refs_0_, bf16[2,2,512,128]{3,2,1,0:T(8,128)(2,1)S(1)} %collective-permute-done.7.refs_1_, ...), custom_call_target="tpu_custom_call" | custom-call | flops 3221225472 | bytes 8388608 | tf_op jit(solution)/shard_map/product/pallas_call | solution.py:265
  85.5 1.6 collective-permute-start.16
  88.4 3.9 %collective-permute-start.10 = (bf16[2,128,512]{2,1,0:T(8,128)(2,1)S(1)}, bf16[2,128,512]{2,1,0:T(8,128)(2,1)S(1)}, u32[]{:S(2)}, u32[]{:S(2)}) collective-permute-start(bf16[2,128,512]{2,1,0:T(8,128)(2,1)S(1)} %get-tuple-element.39), channel_id=1, source_target_pairs={{1,0},{2,1},{3,2},{4,3},{5,4},{6,5},{7,6},{8,7},{9,8},{10,9},{11,1... | collective-permute-start | bytes 786440 | tf_op jit(solution)/shard_map/ppermute | solution.py:193
  92.3 6.4 %collective-permute-start.11 = (bf16[2,128,512]{2,1,0:T(8,128)(2,1)S(1)}, bf16[2,128,512]{2,1,0:T(8,128)(2,1)S(1)}, u32[]{:S(2)}, u32[]{:S(2)}) collective-permute-start(bf16[2,128,512]{2,1,0:T(8,128)(2,1)S(1)} %get-tuple-element.40), channel_id=1, source_target_pairs={{2,0},{3,1},{4,2},{5,3},{6,4},{7,5},{8,6},{9,7},{10,8},{11,9},{12,... | collective-permute-start | bytes 786440 | tf_op jit(solution)/shard_map/ppermute | solution.py:193
  98.7 2.5 %product.2 = bf16[8,512,128]{2,1,0:T(8,128)(2,1)S(1)} custom-call(s32[1]{0:T(128)} %bitcast.13.first_ref, bf16[2,2,512,128]{3,2,1,0:T(8,128)(2,1)S(1)} %get-tuple-element.43.refs_0_, bf16[2,2,512,128]{3,2,1,0:T(8,128)(2,1)S(1)} %collective-permute-done.7.refs_1_, bf16[2,2,512,128]{3,2,1,0:T(8,128)(2,1)} %collective-permute-done.8.refs_2_, ...), custom_call_target="tpu_custom_call" | custom-call | flops 1073741824 | bytes 4194304 | tf_op jit(solution)/shard_map/product/pallas_call | solution.py:265
  101.2 17.8 %collective-permute-start.12 = (bf16[2,128,512]{2,1,0:T(8,128)(2,1)S(1)}, bf16[2,128,512]{2,1,0:T(8,128)(2,1)S(1)}, u32[]{:S(2)}, u32[]{:S(2)}) collective-permute-start(bf16[2,128,512]{2,1,0:T(8,128)(2,1)S(1)} %get-tuple-element.41), channel_id=1, source_target_pairs={{3,0},{4,1},{5,2},{6,3},{7,4},{8,5},{9,6},{10,7},{11,8},{12,9},{13... | collective-permute-start | bytes 786440 | tf_op jit(solution)/shard_map/ppermute | solution.py:193
  119.3 1.9 %collective-permute-start.13 = (bf16[2,128,512]{2,1,0:T(8,128)(2,1)S(1)}, bf16[2,128,512]{2,1,0:T(8,128)(2,1)S(1)}, u32[]{:S(2)}, u32[]{:S(2)}) collective-permute-start(bf16[2,128,512]{2,1,0:T(8,128)(2,1)S(1)} %get-tuple-element.42), channel_id=1, source_target_pairs={{4,0},{5,1},{6,2},{7,3},{8,4},{9,5},{10,6},{11,7},{12,8},{13,9},{1... | collective-permute-start | bytes 786440 | tf_op jit(solution)/shard_map/ppermute | solution.py:193
  121.2 1.6 add_convert_fusion
  122.8 2.5 %collective-permute-done.12 = bf16[2,128,512]{2,1,0:T(8,128)(2,1)S(1)} collective-permute-done((bf16[2,128,512]{2,1,0:T(8,128)(2,1)S(1)}, bf16[2,128,512]{2,1,0:T(8,128)(2,1)S(1)}, u32[]{:S(2)}, u32[]{:S(2)}) %collective-permute-start.12) | collective-permute-done | bytes 262176 | tf_op jit(solution)/shard_map/ppermute | solution.py:193
  125.2 5.8 %collective-permute-done.13 = bf16[2,128,512]{2,1,0:T(8,128)(2,1)S(1)} collective-permute-done((bf16[2,128,512]{2,1,0:T(8,128)(2,1)S(1)}, bf16[2,128,512]{2,1,0:T(8,128)(2,1)S(1)}, u32[]{:S(2)}, u32[]{:S(2)}) %collective-permute-start.13) | collective-permute-done | bytes 262176 | tf_op jit(solution)/shard_map/ppermute | solution.py:193
  131.0 7.4 %all-to-all-start = ((bf16[8,512,128]{2,1,0:T(8,128)(2,1)}), bf16[8,512,128]{2,1,0:T(8,128)(2,1)S(1)}, u32[]{:S(2)}, u32[]{:S(2)}) async-start(bf16[8,512,128]{2,1,0:T(8,128)(2,1)} %add_convert_fusion), calls=%async_computation | async-start | bytes 2097152 | tf_op jit(solution)/shard_map/all_to_all | solution.py:316
  138.6 28.9 %all-to-all-done = bf16[8,512,128]{2,1,0:T(8,128)(2,1)S(1)} async-done(((bf16[8,512,128]{2,1,0:T(8,128)(2,1)}), bf16[8,512,128]{2,1,0:T(8,128)(2,1)S(1)}, u32[]{:S(2)}, u32[]{:S(2)}) %all-to-all-start) | async-done | bytes 1048608 | tf_op jit(solution)/shard_map/all_to_all | solution.py:316
  167.7 4.1 %collective-permute-start.19 = (bf16[512,128]{1,0:T(8,128)(2,1)S(1)}, bf16[512,128]{1,0:T(8,128)(2,1)S(1)}, u32[]{:S(2)}, u32[]{:S(2)}) collective-permute-start(bf16[512,128]{1,0:T(8,128)(2,1)S(1)} %reduce_sum.12), channel_id=1, source_target_pairs={{9,24},{10,40},{11,56},{13,28},{14,44},{15,60},{24,9},{26,41},{27,... | collective-permute-start | bytes 393224 | tf_op jit(solution)/shard_map/ppermute | solution.py:203
  172.7 4.6 %collective-permute-done.19 = bf16[512,128]{1,0:T(8,128)(2,1)S(1)} collective-permute-done((bf16[512,128]{1,0:T(8,128)(2,1)S(1)}, bf16[512,128]{1,0:T(8,128)(2,1)S(1)}, u32[]{:S(2)}, u32[]{:S(2)}) %collective-permute-start.19) | collective-permute-done | bytes 131104 | tf_op jit(solution)/shard_map/ppermute | solution.py:203
  (70 shorter events, 18.6 us)
Async XLA Ops:
  0.6 39.6 %copy-start.20 = (s32[128]{0:T(128)S(1)}, s32[128]{0:T(128)}, u32[]{:S(2)}) copy-start(s32[128]{0:T(128)} %param.15) | copy-start | bytes 1540
  1.6 1.2 copy-start
  4.6 2.3 %collective-permute-start = (bf16[128,2048]{1,0:T(8,128)(2,1)S(1)}, bf16[128,2048]{1,0:T(8,128)(2,1)S(1)}, u32[]{:S(2)}, u32[]{:S(2)}) collective-permute-start(bf16[128,2048]{1,0:T(8,128)(2,1)S(1)} %get-tuple-element.32), channel_id=1, source_target_pairs={{0,8},{1,9},{2,10},{3,11},{4,12},{5,13},{6,14},{7,15},{8,0},{9,1},... | collective-permute-start | bytes 1572872 | tf_op jit(solution)/shard_map/ppermute | solution.py:203
  7.0 17.4 %collective-permute-start.1 = (bf16[256,2048]{1,0:T(8,128)(2,1)S(1)}, bf16[256,2048]{1,0:T(8,128)(2,1)S(1)}, u32[]{:S(2)}, u32[]{:S(2)}) collective-permute-start(bf16[256,2048]{1,0:T(8,128)(2,1)S(1)} %constant_dynamic-update-slice_fusion.refs_4_), channel_id=1, source_target_pairs={{0,2},{1,3},{2,0},{3,1},{4,6},{5,7},{6,4},{7,5},{8,40},{9,41},{10,... | collective-permute-start | bytes 3145736 | tf_op jit(solution)/shard_map/ppermute | solution.py:203
  9.8 21.9 %collective-permute-start.5 = (bf16[2,128,512]{2,1,0:T(8,128)(2,1)S(1)}, bf16[2,128,512]{2,1,0:T(8,128)(2,1)S(1)}, u32[]{:S(2)}, u32[]{:S(2)}) collective-permute-start(bf16[2,128,512]{2,1,0:T(8,128)(2,1)S(1)} %pad_maximum_fusion.refs_4_), channel_id=1, source_target_pairs={{0,1},{1,2},{2,3},{3,4},{4,5},{5,6},{6,7},{7,8},{8,9},{9,10},{10,1... | collective-permute-start | bytes 786440 | tf_op jit(solution)/shard_map/ppermute | solution.py:193
  12.7 19.0 %collective-permute-start.4 = (bf16[2,128,512]{2,1,0:T(8,128)(2,1)S(1)}, bf16[2,128,512]{2,1,0:T(8,128)(2,1)S(1)}, u32[]{:S(2)}, u32[]{:S(2)}) collective-permute-start(bf16[2,128,512]{2,1,0:T(8,128)(2,1)S(1)} %pad_maximum_fusion.refs_4_), channel_id=1, source_target_pairs={{0,2},{1,3},{2,4},{3,5},{4,6},{5,7},{6,8},{7,9},{8,10},{9,11},{10,... | collective-permute-start | bytes 786440 | tf_op jit(solution)/shard_map/ppermute | solution.py:193
  16.3 17.6 %collective-permute-start.3 = (bf16[2,128,512]{2,1,0:T(8,128)(2,1)S(1)}, bf16[2,128,512]{2,1,0:T(8,128)(2,1)S(1)}, u32[]{:S(2)}, u32[]{:S(2)}) collective-permute-start(bf16[2,128,512]{2,1,0:T(8,128)(2,1)S(1)} %pad_maximum_fusion.refs_4_), channel_id=1, source_target_pairs={{0,3},{1,4},{2,5},{3,6},{4,7},{5,8},{6,9},{7,10},{8,11},{9,12},{10... | collective-permute-start | bytes 786440 | tf_op jit(solution)/shard_map/ppermute | solution.py:193
  20.2 19.3 %collective-permute-start.2 = (bf16[2,128,512]{2,1,0:T(8,128)(2,1)S(1)}, bf16[2,128,512]{2,1,0:T(8,128)(2,1)S(1)}, u32[]{:S(2)}, u32[]{:S(2)}) collective-permute-start(bf16[2,128,512]{2,1,0:T(8,128)(2,1)S(1)} %pad_maximum_fusion.refs_4_), channel_id=1, source_target_pairs={{0,4},{1,5},{2,6},{3,7},{4,8},{5,9},{6,10},{7,11},{8,12},{9,13},{1... | collective-permute-start | bytes 786440 | tf_op jit(solution)/shard_map/ppermute | solution.py:193
  31.7 20.6 %copy-start.10 = (bf16[2,128,512]{2,1,0:T(8,128)(2,1)}, bf16[2,128,512]{2,1,0:T(8,128)(2,1)S(1)}, u32[]{:S(2)}) copy-start(bf16[2,128,512]{2,1,0:T(8,128)(2,1)S(1)} %collective-permute-done.5.refs_3_) | copy-start | bytes 786436
  31.7 20.6 %copy-start.12 = (bf16[2,128,512]{2,1,0:T(8,128)(2,1)}, bf16[2,128,512]{2,1,0:T(8,128)(2,1)S(1)}, u32[]{:S(2)}) copy-start(bf16[2,128,512]{2,1,0:T(8,128)(2,1)S(1)} %collective-permute-done.4.refs_2_) | copy-start | bytes 786436
  40.2 1.2 copy-start.7
  52.3 3.5 %collective-permute-start.6 = (bf16[4096,128]{1,0:T(8,128)(2,1)S(1)}, bf16[4096,128]{1,0:T(8,128)(2,1)}, u32[]{:S(2)}, u32[]{:S(2)}) collective-permute-start(bf16[4096,128]{1,0:T(8,128)(2,1)S(1)} %get-tuple-element.36), channel_id=1, source_target_pairs={{0,8},{1,9},{2,10},{3,11},{4,12},{5,13},{6,14},{7,15},{8,0},{9,1},... | collective-permute-start | bytes 3145736 | tf_op jit(solution)/shard_map/ppermute | solution.py:203
  53.4 26.3 %collective-permute-start.15 = (bf16[256,2048]{1,0:T(8,128)(2,1)S(1)}, bf16[256,2048]{1,0:T(8,128)(2,1)}, u32[]{:S(2)}, u32[]{:S(2)}) collective-permute-start(bf16[256,2048]{1,0:T(8,128)(2,1)S(1)} %constant_dynamic-update-slice_fusion.refs_4_), channel_id=1, source_target_pairs={{0,3},{1,0},{2,1},{3,2},{4,7},{5,4},{6,5},{7,6},{8,56},{9,57},{10,... | collective-permute-start | bytes 3145736 | tf_op jit(solution)/shard_map/ppermute | solution.py:203
  53.4 26.3 %collective-permute-start.14 = (bf16[256,2048]{1,0:T(8,128)(2,1)S(1)}, bf16[256,2048]{1,0:T(8,128)(2,1)}, u32[]{:S(2)}, u32[]{:S(2)}) collective-permute-start(bf16[256,2048]{1,0:T(8,128)(2,1)S(1)} %constant_dynamic-update-slice_fusion.refs_4_), channel_id=1, source_target_pairs={{0,1},{1,2},{2,3},{3,0},{4,5},{5,6},{6,7},{7,4},{8,24},{9,25},{10,... | collective-permute-start | bytes 3145736 | tf_op jit(solution)/shard_map/ppermute | solution.py:203
  55.8 3.9 %copy-start.4 = (f32[128]{0:T(128)S(1)}, f32[128]{0:T(128)}, u32[]{:S(2)}) copy-start(f32[128]{0:T(128)} %param.13) | copy-start | bytes 1540
  55.8 3.9 %copy-start.6 = (f32[128]{0:T(128)S(1)}, f32[128]{0:T(128)}, u32[]{:S(2)}) copy-start(f32[128]{0:T(128)} %param.14) | copy-start | bytes 1540
  58.2 19.5 %collective-permute-start.9 = (bf16[2,2,512,128]{3,2,1,0:T(8,128)(2,1)}, bf16[2,2,512,128]{3,2,1,0:T(8,128)(2,1)S(1)}, u32[]{:S(2)}, u32[]{:S(2)}) collective-permute-start(bf16[2,2,512,128]{3,2,1,0:T(8,128)(2,1)} %get-tuple-element.56), channel_id=1, source_target_pairs={{0,3},{1,0},{2,1},{3,2},{4,7},{5,4},{6,5},{7,6},{8,56},{9,57},{10,... | collective-permute-start | bytes 1572872 | tf_op jit(solution)/shard_map/ppermute | solution.py:203
  58.5 21.2 %collective-permute-start.7 = (bf16[2,2,512,128]{3,2,1,0:T(8,128)(2,1)}, bf16[2,2,512,128]{3,2,1,0:T(8,128)(2,1)S(1)}, u32[]{:S(2)}, u32[]{:S(2)}) collective-permute-start(bf16[2,2,512,128]{3,2,1,0:T(8,128)(2,1)} %get-tuple-element.58), channel_id=1, source_target_pairs={{0,1},{1,2},{2,3},{3,0},{4,5},{5,6},{6,7},{7,4},{8,24},{9,25},{10,... | collective-permute-start | bytes 1572872 | tf_op jit(solution)/shard_map/ppermute | solution.py:203
  59.7 20.0 %collective-permute-start.8 = (bf16[2,2,512,128]{3,2,1,0:T(8,128)(2,1)}, bf16[2,2,512,128]{3,2,1,0:T(8,128)(2,1)}, u32[]{:S(2)}, u32[]{:S(2)}) collective-permute-start(bf16[2,2,512,128]{3,2,1,0:T(8,128)(2,1)} %get-tuple-element.59), channel_id=1, source_target_pairs={{0,2},{1,3},{2,0},{3,1},{4,6},{5,7},{6,4},{7,5},{8,40},{9,41},{10,... | collective-permute-start | bytes 1572872 | tf_op jit(solution)/shard_map/ppermute | solution.py:203
  59.7 1.2 copy-start.8
  66.0 13.8 %copy-start.2 = (bf16[256,2048]{1,0:T(8,128)(2,1)S(1)}, bf16[256,2048]{1,0:T(8,128)(2,1)}, u32[]{:S(2)}) copy-start(bf16[256,2048]{1,0:T(8,128)(2,1)} %copy-done.1) | copy-start | bytes 3145732
  85.5 15.7 %collective-permute-start.16 = (bf16[8,512,128]{2,1,0:T(8,128)(2,1)S(1)}, bf16[8,512,128]{2,1,0:T(8,128)(2,1)S(1)}, u32[]{:S(2)}, u32[]{:S(2)}) collective-permute-start(bf16[8,512,128]{2,1,0:T(8,128)(2,1)S(1)} %get-tuple-element.48), channel_id=1, source_target_pairs={{0,16},{1,17},{2,18},{3,19},{4,20},{5,21},{6,22},{7,23},{8,9},{9,1... | collective-permute-start | bytes 3145736 | tf_op jit(solution)/shard_map/ppermute | solution.py:203
  87.1 32.1 %collective-permute-start.17 = (bf16[8,512,128]{2,1,0:T(8,128)(2,1)S(1)}, bf16[8,512,128]{2,1,0:T(8,128)(2,1)S(1)}, u32[]{:S(2)}, u32[]{:S(2)}) collective-permute-start(bf16[8,512,128]{2,1,0:T(8,128)(2,1)S(1)} %get-tuple-element.49), channel_id=1, source_target_pairs={{0,32},{1,33},{2,34},{3,35},{4,36},{5,37},{6,38},{7,39},{8,10},{9,... | collective-permute-start | bytes 3145736 | tf_op jit(solution)/shard_map/ppermute | solution.py:203
  87.4 33.8 %collective-permute-start.18 = (bf16[8,512,128]{2,1,0:T(8,128)(2,1)S(1)}, bf16[8,512,128]{2,1,0:T(8,128)(2,1)S(1)}, u32[]{:S(2)}, u32[]{:S(2)}) collective-permute-start(bf16[8,512,128]{2,1,0:T(8,128)(2,1)S(1)} %get-tuple-element.50), channel_id=1, source_target_pairs={{0,48},{1,49},{2,50},{3,51},{4,52},{5,53},{6,54},{7,55},{8,11},{9,... | collective-permute-start | bytes 3145736 | tf_op jit(solution)/shard_map/ppermute | solution.py:203
  88.4 34.3 %collective-permute-start.10 = (bf16[2,128,512]{2,1,0:T(8,128)(2,1)S(1)}, bf16[2,128,512]{2,1,0:T(8,128)(2,1)S(1)}, u32[]{:S(2)}, u32[]{:S(2)}) collective-permute-start(bf16[2,128,512]{2,1,0:T(8,128)(2,1)S(1)} %get-tuple-element.39), channel_id=1, source_target_pairs={{1,0},{2,1},{3,2},{4,3},{5,4},{6,5},{7,6},{8,7},{9,8},{10,9},{11,1... | collective-permute-start | bytes 786440 | tf_op jit(solution)/shard_map/ppermute | solution.py:193
  92.3 30.5 %collective-permute-start.11 = (bf16[2,128,512]{2,1,0:T(8,128)(2,1)S(1)}, bf16[2,128,512]{2,1,0:T(8,128)(2,1)S(1)}, u32[]{:S(2)}, u32[]{:S(2)}) collective-permute-start(bf16[2,128,512]{2,1,0:T(8,128)(2,1)S(1)} %get-tuple-element.40), channel_id=1, source_target_pairs={{2,0},{3,1},{4,2},{5,3},{6,4},{7,5},{8,6},{9,7},{10,8},{11,9},{12,... | collective-permute-start | bytes 786440 | tf_op jit(solution)/shard_map/ppermute | solution.py:193
  101.2 24.0 %collective-permute-start.12 = (bf16[2,128,512]{2,1,0:T(8,128)(2,1)S(1)}, bf16[2,128,512]{2,1,0:T(8,128)(2,1)S(1)}, u32[]{:S(2)}, u32[]{:S(2)}) collective-permute-start(bf16[2,128,512]{2,1,0:T(8,128)(2,1)S(1)} %get-tuple-element.41), channel_id=1, source_target_pairs={{3,0},{4,1},{5,2},{6,3},{7,4},{8,5},{9,6},{10,7},{11,8},{12,9},{13... | collective-permute-start | bytes 786440 | tf_op jit(solution)/shard_map/ppermute | solution.py:193
  119.3 11.8 %collective-permute-start.13 = (bf16[2,128,512]{2,1,0:T(8,128)(2,1)S(1)}, bf16[2,128,512]{2,1,0:T(8,128)(2,1)S(1)}, u32[]{:S(2)}, u32[]{:S(2)}) collective-permute-start(bf16[2,128,512]{2,1,0:T(8,128)(2,1)S(1)} %get-tuple-element.42), channel_id=1, source_target_pairs={{4,0},{5,1},{6,2},{7,3},{8,4},{9,5},{10,6},{11,7},{12,8},{13,9},{1... | collective-permute-start | bytes 786440 | tf_op jit(solution)/shard_map/ppermute | solution.py:193
  122.8 2.5 %copy-start.21 = (bf16[2,128,512]{2,1,0:T(8,128)(2,1)}, bf16[2,128,512]{2,1,0:T(8,128)(2,1)S(1)}, u32[]{:S(2)}) copy-start(bf16[2,128,512]{2,1,0:T(8,128)(2,1)S(1)} %collective-permute-done.11) | copy-start | bytes 786436
  131.0 7.4 %copy-start.22 = (bf16[2,128,512]{2,1,0:T(8,128)(2,1)S(1)}, bf16[2,128,512]{2,1,0:T(8,128)(2,1)}, u32[]{:S(2)}) copy-start(bf16[2,128,512]{2,1,0:T(8,128)(2,1)} %copy-done.21) | copy-start | bytes 786436
  131.0 36.5 %all-to-all-start = ((bf16[8,512,128]{2,1,0:T(8,128)(2,1)}), bf16[8,512,128]{2,1,0:T(8,128)(2,1)S(1)}, u32[]{:S(2)}, u32[]{:S(2)}) async-start(bf16[8,512,128]{2,1,0:T(8,128)(2,1)} %add_convert_fusion), calls=%async_computation | async-start | bytes 2097152 | tf_op jit(solution)/shard_map/all_to_all | solution.py:316
  167.7 9.6 %collective-permute-start.19 = (bf16[512,128]{1,0:T(8,128)(2,1)S(1)}, bf16[512,128]{1,0:T(8,128)(2,1)S(1)}, u32[]{:S(2)}, u32[]{:S(2)}) collective-permute-start(bf16[512,128]{1,0:T(8,128)(2,1)S(1)} %reduce_sum.12), channel_id=1, source_target_pairs={{9,24},{10,40},{11,56},{13,28},{14,44},{15,60},{24,9},{26,41},{27,... | collective-permute-start | bytes 393224 | tf_op jit(solution)/shard_map/ppermute | solution.py:203
  (12 other events, 10.6 us)

commit v2 on v1

--- a/solution.py
+++ b/solution.py
@@ -16,6 +16,8 @@
 GROUP = 8
 ZH, ZL, RING = 4, 2, 4
 ROWS = 1024
+FORWARD_MIB, BACKWARD_MIB, PREPARE_MIB, PRODUCT_MIB = 56, 56, 56, 56
+AFTER = 3
 CLIP = 2.0
 NEG = -1e30
 SCALE = 1.0 / math.sqrt(HEAD)
@@ -62,15 +64,21 @@
 
 
 def forward_kernel(here_ref, len_ref, q_ref, *refs):
-    kv_refs, (out_ref, log_ref, bias_ref) = refs[: BACK + 1], refs[BACK + 1 :]
-
-    @pl.when(pl.program_id(0) == 0)
+    kv_refs = refs[: BACK + 1]
+    own_refs = refs[BACK + 1 : BACK + 1 + RING]
+    cross_refs = refs[BACK + 1 + RING : BACK + 1 + 2 * RING]
+    log_ref, bias_ref = refs[BACK + 1 + 2 * RING :]
+    g = pl.program_id(0)
+
+    @pl.when(g == 0)
     def _():
         bias_ref[...] = mask_bias(here_ref[0], len_ref[...])
 
     keys = jnp.concatenate([r[0] for r in kv_refs], axis=0)
     values_t = jnp.concatenate([r[1] for r in kv_refs], axis=0).T
     bias = jnp.concatenate([bias_ref[...]] * 2, axis=1)
+    zl = g // 2
+    quads = []
     for pair in range(GROUP // 2):
         s = scores_of(keys, pair_rows(q_ref, pair), bias)
         top = jnp.max(s, axis=0, keepdims=True)
@@ -80,8 +88,18 @@
         log_total = top + jnp.log2(total)
         for i in range(2):
             h = 2 * pair + i
-            out_ref[h * HEAD : (h + 1) * HEAD, :] = out_t[:, i * TOKENS : (i + 1) * TOKENS]
+            quads.append(out_t[:, i * TOKENS : (i + 1) * TOKENS])
             log_ref[0, h : h + 1, :] = log_total[:, i * TOKENS : (i + 1) * TOKENS]
+    for u in range(2):
+        quad = jnp.concatenate(quads[4 * u : 4 * u + 4], axis=0)
+        row_group = lax.rem(2 * g + u, RING)
+        for group, out_refs in ((here_ref[1], own_refs), (here_ref[2], cross_refs)):
+            away = lax.rem(row_group - group + RING, RING)
+            for k, ref in enumerate(out_refs):
+
+                @pl.when(away == k)
+                def _(ref=ref, quad=quad):
+                    ref[zl] = quad
 
 
 def column_of(row):
@@ -145,25 +163,24 @@
 LOG_SPEC = pl.BlockSpec((1, GROUP, TOKENS), lambda g, *_: (g, 0, 0))
 
 
-def attention_forward(here, lengths, q, kvs):
-    rows = q.shape[1]
-    return pl.pallas_call(
+def attention_forward(place, lengths, q, kvs):
+    piece = (ZL, ROWS // ZL, TOKENS)
+    out = pl.pallas_call(
         forward_kernel,
         grid_spec=pltpu.PrefetchScalarGridSpec(
             num_scalar_prefetch=1,
             grid=(KV_HEADS,),
             in_specs=[ROW_SPEC, Q_SPEC] + [KV_SPEC] * (BACK + 1),
-            out_specs=[pl.BlockSpec((GROUP * HEAD, TOKENS), lambda g, *_: (g, 0)), LOG_SPEC],
+            out_specs=[pl.BlockSpec(piece, lambda g, *_: (0, 0, 0))] * (2 * RING) + [LOG_SPEC],
             scratch_shapes=[pltpu.VMEM((SPAN, TOKENS), F32)],
         ),
-        out_shape=[
-            jax.ShapeDtypeStruct((rows, TOKENS), BF),
-            jax.ShapeDtypeStruct((KV_HEADS, GROUP, TOKENS), F32),
-        ],
-        compiler_params=params(10),
+        out_shape=[jax.ShapeDtypeStruct(piece, BF)] * (2 * RING)
+        + [jax.ShapeDtypeStruct((KV_HEADS, GROUP, TOKENS), F32)],
+        compiler_params=params(FORWARD_MIB),
         cost_estimate=pl.CostEstimate(flops=2 * 2 * 32 * 128 * 640 * 128, bytes_accessed=2**22, transcendentals=32 * 128 * 640),
         name="attention_forward",
-    )(here, lengths, q, *kvs)
+    )(place, lengths, q, *kvs)
+    return out[:RING], out[RING : 2 * RING], out[2 * RING]
 
 
 def attention_backward(here, lengths, old, new, q, g, logs, kvs):
@@ -182,7 +199,7 @@
             jax.ShapeDtypeStruct(kv_shape, F32),
         ]
         + [jax.ShapeDtypeStruct(kv_shape, BF)] * BACK,
-        compiler_params=params(14),
+        compiler_params=params(BACKWARD_MIB),
         cost_estimate=pl.CostEstimate(flops=5 * 2 * 32 * 128 * 640 * 128, bytes_accessed=2**23, transcendentals=32 * 128 * 640),
         name="attention_backward",
     )(here, lengths, old, new, q, g, logs, *kvs)
@@ -211,6 +228,10 @@
     return moved(v, lambda zh, x, c, zl, y: (zh, (x + by * c) % RING, c, zl, (y + by * (1 - c)) % RING))
 
 
+def cross_turn(v, by):
+    return moved(v, lambda zh, x, c, zl, y: (zh, (x + by * (1 - c)) % RING, 1 - c, zl, (y + by * c) % RING))
+
+
 def reduce_turn(v, by):
     return moved(v, lambda zh, x, c, zl, y: (zh, (x + by * (1 - c)) % RING, c, zl, (y + by * c) % RING))
 
@@ -219,9 +240,22 @@
     return moved(v, lambda zh, x, c, zl, y: (zh, y, c, zl, x) if c == 1 and x != y else None)
 
 
-def weigh_kernel(core_ref, old_ref, new_ref, cot_ref, keep_ref, send_ref):
+def brought_home(own, backs, y):
+    before = backs[RING - 1].astype(F32)
+    for by in range(1, RING):
+        part = moved(backs[by - 1], lambda zh, x, c, zl, y: (zh, x, c, zl, (y - by) % RING)).astype(F32)
+        here = y + by < RING
+        own = own + jnp.where(here, part, 0.0)
+        before = before + jnp.where(here, 0.0, part)
+    return own + along_tokens(before.astype(BF), -RING).astype(F32)
+
+
+def prepare_kernel(place_ref, old_ref, new_ref, keys_ref, values_ref, cot_ref, kv_ref, keep_ref, send_ref):
+    kv_ref[0] = keys_ref[...]
+    kv_ref[1] = values_ref[...]
     ratio = ratio_column(old_ref, new_ref)
-    for out_ref, half in ((keep_ref, core_ref[0]), (send_ref, 1 - core_ref[0])):
+    core = place_ref[3]
+    for out_ref, half in ((keep_ref, core), (send_ref, 1 - core)):
         for chunk in range(RING):
             for zh in range(ZH):
                 at = pl.multiple_of((zh * 2 * RING + chunk * 2 + half) * HEAD, HEAD)
@@ -230,24 +264,25 @@
                 out_ref[:, to : to + HEAD] = part.astype(BF)
 
 
-def weigh(core, old, new, cotangent):
+def prepare(place, old, new, keys, values, cotangent):
     half = jax.ShapeDtypeStruct((TOKENS, cotangent.shape[1] // 2), BF)
     smem = pl.BlockSpec(memory_space=pltpu.SMEM)
     vmem = pl.BlockSpec(memory_space=pltpu.VMEM)
     return pl.pallas_call(
-        weigh_kernel,
-        in_specs=[smem, vmem, vmem, vmem],
-        out_specs=[vmem, vmem],
-        out_shape=[half, half],
-        compiler_params=params(8),
-        cost_estimate=pl.CostEstimate(flops=2**20, bytes_accessed=2**21, transcendentals=0),
-        name="weigh",
-    )(core, old, new, cotangent)
+        prepare_kernel,
+        in_specs=[smem] + [vmem] * 5,
+        out_specs=[vmem] * 3,
+        out_shape=[jax.ShapeDtypeStruct((2,) + keys.shape, BF), half, half],
+        compiler_params=params(PREPARE_MIB),
+        cost_estimate=pl.CostEstimate(flops=2**20, bytes_accessed=2**22, transcendentals=0),
+        name="prepare",
+    )(place, old, new, keys, values, cotangent)
 
 
 def product_kernel(first_ref, *refs):
-    o_refs, w_refs, out_refs = refs[:RING], refs[RING : 2 * RING], refs[2 * RING :]
-    lhs = jnp.concatenate([r[c].reshape(ROWS, TOKENS) for r in o_refs for c in range(2)], axis=1)
+    o_refs, w_refs, out_refs = refs[: 2 * RING], refs[2 * RING : 3 * RING], refs[3 * RING :]
+    rows = o_refs[0].shape[1]
+    lhs = jnp.concatenate([r[...].reshape(ZL * rows, TOKENS) for r in o_refs], axis=1)
     rhs = jnp.concatenate([r[...] for r in w_refs], axis=0)
     part = dot(lhs, rhs).astype(BF)
     for step, ref in enumerate(out_refs):
@@ -256,67 +291,66 @@
         def _(ref=ref):
             for zh in range(ZH):
                 for zl in range(ZL):
-                    ref[zh * ZL + zl] = part[zl * ROWS // ZL : (zl + 1) * ROWS // ZL, zh * HEAD : (zh + 1) * HEAD]
+                    ref[zh * ZL + zl] = part[zl * rows : (zl + 1) * rows, zh * HEAD : (zh + 1) * HEAD]
 
 
 def product(first, count, outs, ws):
-    chunk = (ZH * ZL, ROWS // ZL, HEAD)
+    rows = ROWS // ZL
+    chunk = (ZH * ZL, rows, HEAD)
     width = ZH * HEAD
     return pl.pallas_call(
         product_kernel,
         grid_spec=pltpu.PrefetchScalarGridSpec(
             num_scalar_prefetch=1,
             grid=(count,),
-            in_specs=[pl.BlockSpec((2, ZL, ROWS // ZL, TOKENS), lambda i, f: (0, 0, 0, 0), pipeline_mode=pl.Buffered(1))] * RING
+            in_specs=[pl.BlockSpec((ZL, rows, TOKENS), lambda i, f: (0, 0, 0), pipeline_mode=pl.Buffered(1))] * (2 * RING)
             + [pl.BlockSpec((2 * TOKENS, width), lambda i, f: (0, lax.rem(f[0] + i, RING)))] * RING,
             out_specs=[pl.BlockSpec(chunk, lambda i, f: (0, 0, 0), pipeline_mode=pl.Buffered(1))] * count,
         ),
         out_shape=[jax.ShapeDtypeStruct(chunk, BF)] * count,
-        compiler_params=params(22),
-        cost_estimate=pl.CostEstimate(flops=2 * ROWS * 1024 * width * count, bytes_accessed=2**21 * (1 + count), transcendentals=0),
+        compiler_params=params(PRODUCT_MIB),
+        cost_estimate=pl.CostEstimate(flops=2 * ZL * rows * 1024 * width * count, bytes_accessed=2**21 * (1 + count), transcendentals=0),
         name="product",
     )(first, *outs, *ws)
 
 
 def shards(queries, keys, values, head_grads, cotangent, old, new, doc_lengths):
-    here = lax.axis_index(FLAT).astype(jnp.int32).reshape(1)
+    here = lax.axis_index(FLAT).astype(jnp.int32)
     lengths = doc_lengths.reshape(1, -1)
     old = old.reshape(1, -1)
     new = new.reshape(1, -1)
     core, x, y = (lax.axis_index(a).astype(jnp.int32) for a in ("core", "x", "y"))
     in_group = jnp.where(core == 0, y, x)
     in_reduce = jnp.where(core == 0, x, y)
-
-    kv = jnp.stack([keys, values])
+    place = jnp.stack([here, in_group, in_reduce, core])
+
+    kv, keep, send = prepare(place, old, new, keys, values, cotangent)
     kvs = [along_tokens(kv, by) for by in range(BACK, 0, -1)] + [kv]
-
-    kv, cotangent = lax.optimization_barrier((kv, cotangent))
-    keep, send = weigh(core.reshape(1), old, new, cotangent)
     w_mine = jnp.concatenate([keep, core_swap(send)], axis=0)
-    ws = [w_mine] + [group_turn(w_mine, by) for by in range(1, RING)]
-
-    here_after, ws[2] = lax.optimization_barrier((here, ws[2]))
-    out_t, logs = attention_forward(here_after, lengths, queries, kvs)
-    out_both = jnp.stack([out_t, core_swap(out_t)]).reshape(2, ZL, RING, ROWS // ZL, TOKENS)
-
-    def rows_of(by):
-        return lax.dynamic_index_in_dim(out_both, (in_group + by) % RING, 2, keepdims=False)
-
-    outs = [rows_of(0)] + [group_turn(rows_of(by), by) for by in range(1, RING)]
-
-    dq, own, *backs = attention_backward(here, lengths, old, new, queries, head_grads, logs, kvs)
-    *outs, own = lax.optimization_barrier((*outs, own))
-    home = [along_tokens(b, -(j + 1)) for j, b in enumerate(backs)]
-
-    sent = product(((in_reduce + 1) % RING).reshape(1), RING - 1, outs, ws)
+    kvs[AFTER], w_soon = lax.optimization_barrier((kvs[AFTER], w_mine))
+    *kvs, w_late = lax.optimization_barrier((*kvs, w_mine))
+    ws = [w_mine] + [group_turn(w_soon if by == 2 else w_late, by) for by in range(1, RING)]
+
+    same, cross, logs = attention_forward(place, lengths, queries, kvs)
+    dq, own, *backs = attention_backward(place, lengths, old, new, queries, head_grads, logs, kvs)
+    *pieces, ws[1], ws[2], ws[3], own = lax.optimization_barrier((*same, *cross, *ws[1:], own))
+    same, cross = pieces[:RING], pieces[RING:]
+    outs = []
+    for by in range(RING):
+        outs.append(group_turn(same[by], by) if by else same[0])
+        outs.append(cross_turn(cross[by], by))
+
+    first = ((in_reduce + 1) % RING).reshape(1)
+    sent = product(first, RING - 1, outs, ws)
     got = [reduce_turn(part, by) for by, part in enumerate(sent, 1)]
+
     (mine,) = product(in_reduce.reshape(1), 1, outs, ws)
     part = sum((g.astype(F32) for g in got), mine.astype(F32)).astype(BF)
-    *home, part = lax.optimization_barrier((*home, part))
+    dkv = brought_home(own, backs, y)
+    dkv, part = lax.optimization_barrier((dkv, part))
     part = lax.all_to_all(part, ("zh", "zl"), split_axis=0, concat_axis=0, tiled=True)
     total = jnp.sum(part.astype(F32), axis=0).astype(BF)
 
-    dkv = own + sum(b.astype(F32) for b in home)
     grad_weight = jnp.where((core == 1) & (x != y), transposed(total), total).astype(F32)
     return dq, dkv[0], dkv[1], grad_weight
 

time: 179 us -> 168 us (0.939)
  Pallas kernels: 29.3 us -> 40.3 us
  local copies, waits for them, and re-layouts: 15.2 us -> 4.68 us
  starting transfers between devices: 66.6 us -> 59.3 us
  waiting for transfers between devices: 60 us -> 55 us
    ppermute x8 -> x5, starting transfers between devices: 44.5 us -> 22.7 us  [along_tokens(): lax.ppermute(v, FLAT, [(i, i + by) for i in range(count) if 0 <= i + by <...]
    ppermute x12 -> x18, starting transfers between devices: 14.7 us -> 28.2 us  [moved(): return lax.ppermute(v, FLAT, pairs)]
    unnamed x47 -> x41, local copies, waits for them, and re-layouts: 14.4 us -> 3.81 us
    ppermute x8 -> x5, waiting for transfers between devices: 21.8 us -> 15.5 us  [along_tokens(): lax.ppermute(v, FLAT, [(i, i + by) for i in range(count) if 0 <= i + by <...]
    ppermute x12 -> x18, waiting for transfers between devices: 9.32 us -> 14.3 us  [moved(): return lax.ppermute(v, FLAT, pairs)]
    pallas_call x2, Pallas kernels: 8.2 us -> 12.1 us  [product(): pl.pallas_call(product_kernel, grid_spec=pltpu.PrefetchScalarGridSpec(num...]
    all_to_all x1, waiting for transfers between devices: 28.9 us -> 25.1 us  [shards(): lax.all_to_all(part, ('zh', 'zl'), split_axis=0, concat_axis=0, tiled=True)]
    pallas_call x1, Pallas kernels: 8.89 us -> 12.3 us  [attention_forward(): pl.pallas_call(forward_kernel, grid_spec=pltpu.PrefetchScalarGridSpec(num...]
  transfers between devices with their start and end apart: 21 -> 24, of which waited for: 11 -> 10; matrix products, arithmetic and copies ran while one was open for 3% -> 2% of each run, Pallas kernels for 8% -> 23%
where the time goes in v2:
time: 168 us; the launch traced here: 166 us
  starting transfers between devices  59.3 us (35%)
  waiting for transfers between devices  55 us (33%)
  Pallas kernels  40.3 us (24%)
  other arithmetic  5.96 us (4%)
  local copies, waits for them, and re-layouts  4.68 us (3%)
    ppermute x18, starting transfers between devices, moved(): return lax.ppermute(v, FLAT, pairs)  28.2 us
    all_to_all x1, waiting for transfers between devices, shards(): lax.all_to_all(part, ('zh', 'zl'), split_axis=0, concat_axis=0, tiled=True)  25.1 us
    ppermute x5, starting transfers between devices, along_tokens(): lax.ppermute(v, FLAT, [(i, i + by) for i in range(count) if 0 <= i + by <...  22.7 us
    ppermute x5, waiting for transfers between devices, along_tokens(): lax.ppermute(v, FLAT, [(i, i + by) for i in range(count) if 0 <= i + by <...  15.5 us
    ppermute x18, waiting for transfers between devices, moved(): return lax.ppermute(v, FLAT, pairs)  14.3 us
    pallas_call x1, Pallas kernels, attention_backward(): pl.pallas_call(backward_kernel, grid_spec=pltpu.PrefetchScalarGridSpec(nu...  13.2 us
    pallas_call x1, Pallas kernels, attention_forward(): pl.pallas_call(forward_kernel, grid_spec=pltpu.PrefetchScalarGridSpec(num...  12.3 us
    pallas_call x2, Pallas kernels, product(): pl.pallas_call(product_kernel, grid_spec=pltpu.PrefetchScalarGridSpec(num...  12.1 us
  transfers between devices with their start and end apart: 24, of which 10 were waited for; matrix products, arithmetic and copies ran while one was open for 2% of the time, Pallas kernels for 23%

profile of v2, /device:TPU:17, one launch (start us, length us, event | category | flops | bytes accessed | tf_op | source)
XLA Modules:
  0.0 166.2 jit_solution(12251154454794697781)
XLA Ops:
  1.3 2.7 %prepare.1 = (bf16[2,128,512]{2,1,0:T(8,128)(2,1)}, bf16[128,2048]{1,0:T(8,128)(2,1)}, bf16[128,2048]{1,0:T(8,128)(2,1)}) custom-call(s32[4]{0:T(128)} %pad_add_fusion.place_ref.here_ref, f32[1,128]{1,0:T(1,128)} %bitcast.12, f32[1,128]{1,0:T(1,128)} %bitcast.14, bf16[128,512]{1,0:T(8,128)(2,1)} %keys_ref.1, bf16[128,512]{1,0:T(8,128)(2,1)} %values_ref.1, ...), custom_call_target="tpu_custom_call" | custom-call | flops 1048576 | bytes 4194304 | tf_op jit(solution)/shard_map/prepare/pallas_call | solution.py:271
  4.7 2.9 %collective-permute-start.3 = (bf16[2,128,512]{2,1,0:T(8,128)(2,1)}, bf16[2,128,512]{2,1,0:T(8,128)(2,1)S(1)}, u32[]{:S(2)}, u32[]{:S(2)}) collective-permute-start(bf16[2,128,512]{2,1,0:T(8,128)(2,1)} %get-tuple-element.55.refs_4_), channel_id=1, source_target_pairs={{0,1},{1,2},{2,3},{3,4},{4,5},{5,6},{6,7},{7,8},{8,9},{9,10},{10,1... | collective-permute-start | bytes 786440 | tf_op jit(solution)/shard_map/ppermute | solution.py:210
  7.6 3.6 %collective-permute-start.2 = (bf16[2,128,512]{2,1,0:T(8,128)(2,1)}, bf16[2,128,512]{2,1,0:T(8,128)(2,1)S(1)}, u32[]{:S(2)}, u32[]{:S(2)}) collective-permute-start(bf16[2,128,512]{2,1,0:T(8,128)(2,1)} %get-tuple-element.55.refs_4_), channel_id=1, source_target_pairs={{0,2},{1,3},{2,4},{3,5},{4,6},{5,7},{6,8},{7,9},{8,10},{9,11},{10,... | collective-permute-start | bytes 786440 | tf_op jit(solution)/shard_map/ppermute | solution.py:210
  11.2 3.0 %collective-permute-start.1 = (bf16[2,128,512]{2,1,0:T(8,128)(2,1)}, bf16[2,128,512]{2,1,0:T(8,128)(2,1)S(1)}, u32[]{:S(2)}, u32[]{:S(2)}) collective-permute-start(bf16[2,128,512]{2,1,0:T(8,128)(2,1)} %get-tuple-element.55.refs_4_), channel_id=1, source_target_pairs={{0,3},{1,4},{2,5},{3,6},{4,7},{5,8},{6,9},{7,10},{8,11},{9,12},{10... | collective-permute-start | bytes 786440 | tf_op jit(solution)/shard_map/ppermute | solution.py:210
  14.3 4.1 %collective-permute-start = (bf16[2,128,512]{2,1,0:T(8,128)(2,1)}, bf16[2,128,512]{2,1,0:T(8,128)(2,1)S(1)}, u32[]{:S(2)}, u32[]{:S(2)}) collective-permute-start(bf16[2,128,512]{2,1,0:T(8,128)(2,1)} %get-tuple-element.55.refs_4_), channel_id=1, source_target_pairs={{0,4},{1,5},{2,6},{3,7},{4,8},{5,9},{6,10},{7,11},{8,12},{9,13},{1... | collective-permute-start | bytes 786440 | tf_op jit(solution)/shard_map/ppermute | solution.py:210
  19.6 1.5 collective-permute-done.2.refs_2_
  21.1 7.2 %collective-permute-done.1.refs_1_ = bf16[2,128,512]{2,1,0:T(8,128)(2,1)S(1)} collective-permute-done((bf16[2,128,512]{2,1,0:T(8,128)(2,1)}, bf16[2,128,512]{2,1,0:T(8,128)(2,1)S(1)}, u32[]{:S(2)}, u32[]{:S(2)}) %collective-permute-start.1) | collective-permute-done | bytes 262176 | tf_op jit(solution)/shard_map/ppermute | solution.py:210
  28.3 3.5 %collective-permute-done.refs_0_ = bf16[2,128,512]{2,1,0:T(8,128)(2,1)S(1)} collective-permute-done((bf16[2,128,512]{2,1,0:T(8,128)(2,1)}, bf16[2,128,512]{2,1,0:T(8,128)(2,1)S(1)}, u32[]{:S(2)}, u32[]{:S(2)}) %collective-permute-start) | collective-permute-done | bytes 262176 | tf_op jit(solution)/shard_map/ppermute | solution.py:210
  31.8 2.5 %collective-permute-start.7 = (bf16[256,2048]{1,0:T(8,128)(2,1)S(1)}, bf16[256,2048]{1,0:T(8,128)(2,1)S(1)}, u32[]{:S(2)}, u32[]{:S(2)}) collective-permute-start(bf16[256,2048]{1,0:T(8,128)(2,1)S(1)} %constant_dynamic-update-slice_fusion.refs_8_), channel_id=1, source_target_pairs={{0,3},{1,0},{2,1},{3,2},{4,7},{5,4},{6,5},{7,6},{8,56},{9,57},{10,... | collective-permute-start | bytes 3145736 | tf_op jit(solution)/shard_map/ppermute | solution.py:220
  34.3 1.7 %collective-permute-start.6 = (bf16[256,2048]{1,0:T(8,128)(2,1)S(1)}, bf16[256,2048]{1,0:T(8,128)(2,1)S(1)}, u32[]{:S(2)}, u32[]{:S(2)}) collective-permute-start(bf16[256,2048]{1,0:T(8,128)(2,1)S(1)} %constant_dynamic-update-slice_fusion.refs_8_), channel_id=1, source_target_pairs={{0,2},{1,3},{2,0},{3,1},{4,6},{5,7},{6,4},{7,5},{8,40},{9,41},{10,... | collective-permute-start | bytes 3145736 | tf_op jit(solution)/shard_map/ppermute | solution.py:220
  36.1 12.3 %attention_forward.1 = (bf16[2,512,128]{2,1,0:T(8,128)(2,1)}, bf16[2,512,128]{2,1,0:T(8,128)(2,1)}, bf16[2,512,128]{2,1,0:T(8,128)(2,1)}, bf16[2,512,128]{2,1,0:...) custom-call(s32[4]{0:T(128)} %pad_add_fusion.place_ref.here_ref, ...), custom_call_target="tpu_custom_call" | custom-call | flops 1342177280 | bytes 4194304 | tf_op jit(solution)/shard_map/attention_forward/pallas_call | solution.py:168
  48.4 13.2 %attention_backward.1 = (f32[128,4096]{1,0:T(8,128)}, f32[2,128,512]{2,1,0:T(8,128)}, bf16[2,128,512]{2,1,0:T(8,128)(2,1)}, bf16[2,128,512]{2,1,0:T(8,128)(2,1)}...) custom-call(s32[4]{0:T(128)} %pad_add_fusion.place_ref.here_ref, s32[1,128]{1,0:T(1,128)} %bitcast.17, ...), custom_call_target="tpu_custom_call" | custom-call | flops 3355443200 | bytes 8388608 | tf_op jit(solution)/shard_map/attention_backward/pallas_call | solution.py:188
  63.6 1.6 collective-permute-start.13
  65.2 1.7 %collective-permute-start.14 = (bf16[2,512,128]{2,1,0:T(8,128)(2,1)S(1)}, bf16[2,512,128]{2,1,0:T(8,128)(2,1)S(1)}, u32[]{:S(2)}, u32[]{:S(2)}) collective-permute-start(bf16[2,512,128]{2,1,0:T(8,128)(2,1)S(1)} %copy-done.13), channel_id=1, source_target_pairs={{0,24},{1,25},{2,26},{3,27},{4,28},{5,29},{6,30},{7,31},{8,1},{9,2... | collective-permute-start | bytes 786440 | tf_op jit(solution)/shard_map/ppermute | solution.py:220
  66.9 2.7 %collective-permute-start.15 = (bf16[2,512,128]{2,1,0:T(8,128)(2,1)S(1)}, bf16[2,512,128]{2,1,0:T(8,128)(2,1)S(1)}, u32[]{:S(2)}, u32[]{:S(2)}) collective-permute-start(bf16[2,512,128]{2,1,0:T(8,128)(2,1)S(1)} %copy-done.12), channel_id=1, source_target_pairs={{0,2},{1,3},{2,0},{3,1},{4,6},{5,7},{6,4},{7,5},{8,40},{9,41},{10,... | collective-permute-start | bytes 786440 | tf_op jit(solution)/shard_map/ppermute | solution.py:220
  69.7 1.8 %collective-permute-start.17 = (bf16[2,512,128]{2,1,0:T(8,128)(2,1)}, bf16[2,512,128]{2,1,0:T(8,128)(2,1)S(1)}, u32[]{:S(2)}, u32[]{:S(2)}) collective-permute-start(bf16[2,512,128]{2,1,0:T(8,128)(2,1)} %get-tuple-element.80), channel_id=1, source_target_pairs={{0,3},{1,0},{2,1},{3,2},{4,7},{5,4},{6,5},{7,6},{8,56},{9,57},{10,... | collective-permute-start | bytes 786440 | tf_op jit(solution)/shard_map/ppermute | solution.py:220
  71.4 3.6 %collective-permute-start.18 = (bf16[2,512,128]{2,1,0:T(8,128)(2,1)}, bf16[2,512,128]{2,1,0:T(8,128)(2,1)}, u32[]{:S(2)}, u32[]{:S(2)}) collective-permute-start(bf16[2,512,128]{2,1,0:T(8,128)(2,1)} %get-tuple-element.81), channel_id=1, source_target_pairs={{0,56},{1,57},{2,58},{3,59},{4,60},{5,61},{6,62},{7,63},{8,3},{9,0... | collective-permute-start | bytes 786440 | tf_op jit(solution)/shard_map/ppermute | solution.py:220
  75.3 3.3 %collective-permute-done.15.refs_4_ = bf16[2,512,128]{2,1,0:T(8,128)(2,1)S(1)} collective-permute-done((bf16[2,512,128]{2,1,0:T(8,128)(2,1)S(1)}, bf16[2,512,128]{2,1,0:T(8,128)(2,1)S(1)}, u32[]{:S(2)}, u32[]{:S(2)}) %collective-permute-start.15) | collective-permute-done | bytes 262176 | tf_op jit(solution)/shard_map/ppermute | solution.py:220
  78.6 2.3 %collective-permute-start.9 = (bf16[2,128,512]{2,1,0:T(8,128)(2,1)}, bf16[2,128,512]{2,1,0:T(8,128)(2,1)S(1)}, u32[]{:S(2)}, u32[]{:S(2)}) collective-permute-start(bf16[2,128,512]{2,1,0:T(8,128)(2,1)} %get-tuple-element.71), channel_id=1, source_target_pairs={{0,2},{1,3},{2,0},{3,1},{4,6},{5,7},{6,4},{7,5},{8,10},{9,11},{10,... | collective-permute-start | bytes 786440 | tf_op jit(solution)/shard_map/ppermute | solution.py:220
  80.9 2.0 %collective-permute-start.10 = (bf16[2,128,512]{2,1,0:T(8,128)(2,1)}, bf16[2,128,512]{2,1,0:T(8,128)(2,1)S(1)}, u32[]{:S(2)}, u32[]{:S(2)}) collective-permute-start(bf16[2,128,512]{2,1,0:T(8,128)(2,1)} %get-tuple-element.72), channel_id=1, source_target_pairs={{0,1},{1,2},{2,3},{3,0},{4,5},{5,6},{6,7},{7,4},{8,9},{9,10},{10,1... | collective-permute-start | bytes 786440 | tf_op jit(solution)/shard_map/ppermute | solution.py:220
  83.6 8.1 %product.3 = (bf16[8,512,128]{2,1,0:T(8,128)(2,1)}, bf16[8,512,128]{2,1,0:T(8,128)(2,1)}, bf16[8,512,128]{2,1,0:T(8,128)(2,1)}) custom-call(s32[1]{0:T(128)} %bitcast.7.first_ref, bf16[2,512,128]{2,1,0:T(8,128)(2,1)} %get-tuple-element.74.refs_0_, bf16[2,512,128]{2,1,0:T(8,128)(2,1)} %copy-done.5, bf16[2,512,128]{2,1,0:T(8,128)(2,1)} %copy-done.6, ...), custom_call_target="tpu_custom_call" | custom-call | flops 3221225472 | bytes 8388608 | tf_op jit(solution)/shard_map/product/pallas_call | solution.py:301
  92.3 1.5 collective-permute-start.21
  94.3 9.0 %collective-permute-start.11 = (bf16[2,128,512]{2,1,0:T(8,128)(2,1)S(1)}, bf16[2,128,512]{2,1,0:T(8,128)(2,1)S(1)}, u32[]{:S(2)}, u32[]{:S(2)}) collective-permute-start(bf16[2,128,512]{2,1,0:T(8,128)(2,1)S(1)} %fusion.7), channel_id=1, source_target_pairs={{4,0},{5,1},{6,2},{7,3},{8,4},{9,5},{10,6},{11,7},{12,8},{13,9},{1... | collective-permute-start | bytes 786440 | tf_op jit(solution)/shard_map/ppermute | solution.py:210
  103.4 3.3 %collective-permute-done.11 = bf16[2,128,512]{2,1,0:T(8,128)(2,1)S(1)} collective-permute-done((bf16[2,128,512]{2,1,0:T(8,128)(2,1)S(1)}, bf16[2,128,512]{2,1,0:T(8,128)(2,1)S(1)}, u32[]{:S(2)}, u32[]{:S(2)}) %collective-permute-start.11) | collective-permute-done | bytes 262176 | tf_op jit(solution)/shard_map/ppermute | solution.py:210
  107.9 4.0 %product.2 = bf16[8,512,128]{2,1,0:T(8,128)(2,1)} custom-call(s32[1]{0:T(128)} %bitcast.2.first_ref, bf16[2,512,128]{2,1,0:T(8,128)(2,1)} %get-tuple-element.74.refs_0_, bf16[2,512,128]{2,1,0:T(8,128)(2,1)} %copy-done.5, bf16[2,512,128]{2,1,0:T(8,128)(2,1)} %copy-done.6, bf16[2,512,128]{2,1,0:T(8,128)(2,1)} %copy-done.7, bf16[2,512,128]{2,1,0:T(8,128)(2,1)} %copy-done.8, ...), custom_call_target="tpu_custom_call" | custom-call | flops 1073741824 | bytes 4194304 | tf_op jit(solution)/shard_map/product/pallas_call | solution.py:301
  111.9 5.2 %collective-permute-done.19 = bf16[8,512,128]{2,1,0:T(8,128)(2,1)S(1)} collective-permute-done((bf16[8,512,128]{2,1,0:T(8,128)(2,1)}, bf16[8,512,128]{2,1,0:T(8,128)(2,1)S(1)}, u32[]{:S(2)}, u32[]{:S(2)}) %collective-permute-start.19) | collective-permute-done | bytes 1048608 | tf_op jit(solution)/shard_map/ppermute | solution.py:220
  117.2 1.8 %collective-permute-done.21 = bf16[8,512,128]{2,1,0:T(8,128)(2,1)} collective-permute-done((bf16[8,512,128]{2,1,0:T(8,128)(2,1)}, bf16[8,512,128]{2,1,0:T(8,128)(2,1)}, u32[]{:S(2)}, u32[]{:S(2)}) %collective-permute-start.21) | collective-permute-done | bytes 1048608 | tf_op jit(solution)/shard_map/ppermute | solution.py:220
  119.0 3.0 %add_convert_fusion = bf16[8,512,128]{2,1,0:T(8,128)(2,1)} fusion(bf16[8,512,128]{2,1,0:T(8,128)(2,1)} %collective-permute-done.21, bf16[8,512,128]{2,1,0:T(8,128)(2,1)S(1)} %collective-permute-done.20, bf16[8,512,128]{2,1,0:T(8,128)(2,1)S(1)} %collective-permute-done.19, bf16[8,512,128]{2,1,0:T(8,128)(2,1)} %product.2), kind=kLoop, calls=%fused_computation | loop fusion | flops 4194304 | bytes 5242880 | tf_op jit(solution)/shard_map/convert_element_type | solution.py:348
  122.1 8.4 %all-to-all-start = ((bf16[8,512,128]{2,1,0:T(8,128)(2,1)}), bf16[8,512,128]{2,1,0:T(8,128)(2,1)S(1)}, u32[]{:S(2)}, u32[]{:S(2)}) async-start(bf16[8,512,128]{2,1,0:T(8,128)(2,1)} %add_convert_fusion), calls=%async_computation | async-start | bytes 2097152 | tf_op jit(solution)/shard_map/all_to_all | solution.py:351
  130.5 25.1 %all-to-all-done = bf16[8,512,128]{2,1,0:T(8,128)(2,1)S(1)} async-done(((bf16[8,512,128]{2,1,0:T(8,128)(2,1)}), bf16[8,512,128]{2,1,0:T(8,128)(2,1)S(1)}, u32[]{:S(2)}, u32[]{:S(2)}) %all-to-all-start) | async-done | bytes 1048608 | tf_op jit(solution)/shard_map/all_to_all | solution.py:351
  155.8 5.2 %collective-permute-start.22 = (bf16[512,128]{1,0:T(8,128)(2,1)S(1)}, bf16[512,128]{1,0:T(8,128)(2,1)S(1)}, u32[]{:S(2)}, u32[]{:S(2)}) collective-permute-start(bf16[512,128]{1,0:T(8,128)(2,1)S(1)} %reduce_sum.12), channel_id=1, source_target_pairs={{9,24},{10,40},{11,56},{13,28},{14,44},{15,60},{24,9},{26,41},{27,... | collective-permute-start | bytes 393224 | tf_op jit(solution)/shard_map/ppermute | solution.py:220
  161.8 3.7 %collective-permute-done.22 = bf16[512,128]{1,0:T(8,128)(2,1)S(1)} collective-permute-done((bf16[512,128]{1,0:T(8,128)(2,1)S(1)}, bf16[512,128]{1,0:T(8,128)(2,1)S(1)}, u32[]{:S(2)}, u32[]{:S(2)}) %collective-permute-start.22) | collective-permute-done | bytes 131104 | tf_op jit(solution)/shard_map/ppermute | solution.py:220
  (70 shorter events, 9.5 us)
Async XLA Ops:
  4.0 15.5 %collective-permute-start.4 = (bf16[128,2048]{1,0:T(8,128)(2,1)}, bf16[128,2048]{1,0:T(8,128)(2,1)S(1)}, u32[]{:S(2)}, u32[]{:S(2)}) collective-permute-start(bf16[128,2048]{1,0:T(8,128)(2,1)} %get-tuple-element.49), channel_id=1, source_target_pairs={{0,8},{1,9},{2,10},{3,11},{4,12},{5,13},{6,14},{7,15},{8,0},{9,1},... | collective-permute-start | bytes 1572872 | tf_op jit(solution)/shard_map/ppermute | solution.py:220
  4.7 14.8 %collective-permute-start.3 = (bf16[2,128,512]{2,1,0:T(8,128)(2,1)}, bf16[2,128,512]{2,1,0:T(8,128)(2,1)S(1)}, u32[]{:S(2)}, u32[]{:S(2)}) collective-permute-start(bf16[2,128,512]{2,1,0:T(8,128)(2,1)} %get-tuple-element.55.refs_4_), channel_id=1, source_target_pairs={{0,1},{1,2},{2,3},{3,4},{4,5},{5,6},{6,7},{7,8},{8,9},{9,10},{10,1... | collective-permute-start | bytes 786440 | tf_op jit(solution)/shard_map/ppermute | solution.py:210
  7.6 13.5 %collective-permute-start.2 = (bf16[2,128,512]{2,1,0:T(8,128)(2,1)}, bf16[2,128,512]{2,1,0:T(8,128)(2,1)S(1)}, u32[]{:S(2)}, u32[]{:S(2)}) collective-permute-start(bf16[2,128,512]{2,1,0:T(8,128)(2,1)} %get-tuple-element.55.refs_4_), channel_id=1, source_target_pairs={{0,2},{1,3},{2,4},{3,5},{4,6},{5,7},{6,8},{7,9},{8,10},{9,11},{10,... | collective-permute-start | bytes 786440 | tf_op jit(solution)/shard_map/ppermute | solution.py:210
  11.2 17.1 %collective-permute-start.1 = (bf16[2,128,512]{2,1,0:T(8,128)(2,1)}, bf16[2,128,512]{2,1,0:T(8,128)(2,1)S(1)}, u32[]{:S(2)}, u32[]{:S(2)}) collective-permute-start(bf16[2,128,512]{2,1,0:T(8,128)(2,1)} %get-tuple-element.55.refs_4_), channel_id=1, source_target_pairs={{0,3},{1,4},{2,5},{3,6},{4,7},{5,8},{6,9},{7,10},{8,11},{9,12},{10... | collective-permute-start | bytes 786440 | tf_op jit(solution)/shard_map/ppermute | solution.py:210
  14.3 17.5 %collective-permute-start = (bf16[2,128,512]{2,1,0:T(8,128)(2,1)}, bf16[2,128,512]{2,1,0:T(8,128)(2,1)S(1)}, u32[]{:S(2)}, u32[]{:S(2)}) collective-permute-start(bf16[2,128,512]{2,1,0:T(8,128)(2,1)} %get-tuple-element.55.refs_4_), channel_id=1, source_target_pairs={{0,4},{1,5},{2,6},{3,7},{4,8},{5,9},{6,10},{7,11},{8,12},{9,13},{1... | collective-permute-start | bytes 786440 | tf_op jit(solution)/shard_map/ppermute | solution.py:210
  19.5 28.8 %copy-start = (bf16[256,2048]{1,0:T(8,128)(2,1)}, bf16[256,2048]{1,0:T(8,128)(2,1)S(1)}, u32[]{:S(2)}) copy-start(bf16[256,2048]{1,0:T(8,128)(2,1)S(1)} %constant_dynamic-update-slice_fusion.refs_8_) | copy-start | bytes 3145732
  19.6 16.5 %copy-start.14 = (bf16[2,128,512]{2,1,0:T(8,128)(2,1)}, bf16[2,128,512]{2,1,0:T(8,128)(2,1)S(1)}, u32[]{:S(2)}) copy-start(bf16[2,128,512]{2,1,0:T(8,128)(2,1)S(1)} %collective-permute-done.3.refs_3_) | copy-start | bytes 786436
  31.8 29.7 %collective-permute-start.7 = (bf16[256,2048]{1,0:T(8,128)(2,1)S(1)}, bf16[256,2048]{1,0:T(8,128)(2,1)S(1)}, u32[]{:S(2)}, u32[]{:S(2)}) collective-permute-start(bf16[256,2048]{1,0:T(8,128)(2,1)S(1)} %constant_dynamic-update-slice_fusion.refs_8_), channel_id=1, source_target_pairs={{0,3},{1,0},{2,1},{3,2},{4,7},{5,4},{6,5},{7,6},{8,56},{9,57},{10,... | collective-permute-start | bytes 3145736 | tf_op jit(solution)/shard_map/ppermute | solution.py:220
  34.3 27.3 %collective-permute-start.5 = (bf16[256,2048]{1,0:T(8,128)(2,1)S(1)}, bf16[256,2048]{1,0:T(8,128)(2,1)S(1)}, u32[]{:S(2)}, u32[]{:S(2)}) collective-permute-start(bf16[256,2048]{1,0:T(8,128)(2,1)S(1)} %constant_dynamic-update-slice_fusion.refs_8_), channel_id=1, source_target_pairs={{0,1},{1,2},{2,3},{3,0},{4,5},{5,6},{6,7},{7,4},{8,24},{9,25},{10,... | collective-permute-start | bytes 3145736 | tf_op jit(solution)/shard_map/ppermute | solution.py:220
  34.3 27.3 %collective-permute-start.6 = (bf16[256,2048]{1,0:T(8,128)(2,1)S(1)}, bf16[256,2048]{1,0:T(8,128)(2,1)S(1)}, u32[]{:S(2)}, u32[]{:S(2)}) collective-permute-start(bf16[256,2048]{1,0:T(8,128)(2,1)S(1)} %constant_dynamic-update-slice_fusion.refs_8_), channel_id=1, source_target_pairs={{0,2},{1,3},{2,0},{3,1},{4,6},{5,7},{6,4},{7,5},{8,40},{9,41},{10,... | collective-permute-start | bytes 3145736 | tf_op jit(solution)/shard_map/ppermute | solution.py:220
  48.4 15.2 %copy-start.19 = (bf16[2,512,128]{2,1,0:T(8,128)(2,1)S(1)}, bf16[2,512,128]{2,1,0:T(8,128)(2,1)}, u32[]{:S(2)}) copy-start(bf16[2,512,128]{2,1,0:T(8,128)(2,1)} %get-tuple-element.75) | copy-start | bytes 786436
  48.4 15.2 %copy-start.17 = (bf16[2,512,128]{2,1,0:T(8,128)(2,1)S(1)}, bf16[2,512,128]{2,1,0:T(8,128)(2,1)}, u32[]{:S(2)}) copy-start(bf16[2,512,128]{2,1,0:T(8,128)(2,1)} %get-tuple-element.76) | copy-start | bytes 786436
  48.4 16.8 %copy-start.13 = (bf16[2,512,128]{2,1,0:T(8,128)(2,1)S(1)}, bf16[2,512,128]{2,1,0:T(8,128)(2,1)}, u32[]{:S(2)}) copy-start(bf16[2,512,128]{2,1,0:T(8,128)(2,1)} %get-tuple-element.77) | copy-start | bytes 786436
  48.4 18.5 %copy-start.12 = (bf16[2,512,128]{2,1,0:T(8,128)(2,1)S(1)}, bf16[2,512,128]{2,1,0:T(8,128)(2,1)}, u32[]{:S(2)}) copy-start(bf16[2,512,128]{2,1,0:T(8,128)(2,1)} %get-tuple-element.78) | copy-start | bytes 786436
  48.4 21.2 %copy-start.11 = (bf16[2,512,128]{2,1,0:T(8,128)(2,1)S(1)}, bf16[2,512,128]{2,1,0:T(8,128)(2,1)}, u32[]{:S(2)}) copy-start(bf16[2,512,128]{2,1,0:T(8,128)(2,1)} %get-tuple-element.79) | copy-start | bytes 786436
  61.6 22.0 %copy-start.1 = (bf16[256,2048]{1,0:T(8,128)(2,1)}, bf16[256,2048]{1,0:T(8,128)(2,1)S(1)}, u32[]{:S(2)}) copy-start(bf16[256,2048]{1,0:T(8,128)(2,1)S(1)} %collective-permute-done.7.refs_11_) | copy-start | bytes 3145732
  63.6 6.1 %collective-permute-start.12 = (bf16[2,512,128]{2,1,0:T(8,128)(2,1)S(1)}, bf16[2,512,128]{2,1,0:T(8,128)(2,1)S(1)}, u32[]{:S(2)}, u32[]{:S(2)}) collective-permute-start(bf16[2,512,128]{2,1,0:T(8,128)(2,1)S(1)} %copy-done.19), channel_id=1, source_target_pairs={{0,8},{1,9},{2,10},{3,11},{4,12},{5,13},{6,14},{7,15},{8,0},{9,1},... | collective-permute-start | bytes 786440 | tf_op jit(solution)/shard_map/ppermute | solution.py:220
  63.6 7.8 %collective-permute-start.13 = (bf16[2,512,128]{2,1,0:T(8,128)(2,1)S(1)}, bf16[2,512,128]{2,1,0:T(8,128)(2,1)S(1)}, u32[]{:S(2)}, u32[]{:S(2)}) collective-permute-start(bf16[2,512,128]{2,1,0:T(8,128)(2,1)S(1)} %copy-done.17), channel_id=1, source_target_pairs={{0,1},{1,2},{2,3},{3,0},{4,5},{5,6},{6,7},{7,4},{8,24},{9,25},{10,... | collective-permute-start | bytes 786440 | tf_op jit(solution)/shard_map/ppermute | solution.py:220
  65.2 9.8 %collective-permute-start.14 = (bf16[2,512,128]{2,1,0:T(8,128)(2,1)S(1)}, bf16[2,512,128]{2,1,0:T(8,128)(2,1)S(1)}, u32[]{:S(2)}, u32[]{:S(2)}) collective-permute-start(bf16[2,512,128]{2,1,0:T(8,128)(2,1)S(1)} %copy-done.13), channel_id=1, source_target_pairs={{0,24},{1,25},{2,26},{3,27},{4,28},{5,29},{6,30},{7,31},{8,1},{9,2... | collective-permute-start | bytes 786440 | tf_op jit(solution)/shard_map/ppermute | solution.py:220
  66.9 11.7 %collective-permute-start.15 = (bf16[2,512,128]{2,1,0:T(8,128)(2,1)S(1)}, bf16[2,512,128]{2,1,0:T(8,128)(2,1)S(1)}, u32[]{:S(2)}, u32[]{:S(2)}) collective-permute-start(bf16[2,512,128]{2,1,0:T(8,128)(2,1)S(1)} %copy-done.12), channel_id=1, source_target_pairs={{0,2},{1,3},{2,0},{3,1},{4,6},{5,7},{6,4},{7,5},{8,40},{9,41},{10,... | collective-permute-start | bytes 786440 | tf_op jit(solution)/shard_map/ppermute | solution.py:220
  69.6 11.2 %collective-permute-start.16 = (bf16[2,512,128]{2,1,0:T(8,128)(2,1)S(1)}, bf16[2,512,128]{2,1,0:T(8,128)(2,1)S(1)}, u32[]{:S(2)}, u32[]{:S(2)}) collective-permute-start(bf16[2,512,128]{2,1,0:T(8,128)(2,1)S(1)} %copy-done.11), channel_id=1, source_target_pairs={{0,40},{1,41},{2,42},{3,43},{4,44},{5,45},{6,46},{7,47},{8,2},{9,3... | collective-permute-start | bytes 786440 | tf_op jit(solution)/shard_map/ppermute | solution.py:220
  69.7 13.2 %collective-permute-start.17 = (bf16[2,512,128]{2,1,0:T(8,128)(2,1)}, bf16[2,512,128]{2,1,0:T(8,128)(2,1)S(1)}, u32[]{:S(2)}, u32[]{:S(2)}) collective-permute-start(bf16[2,512,128]{2,1,0:T(8,128)(2,1)} %get-tuple-element.80), channel_id=1, source_target_pairs={{0,3},{1,0},{2,1},{3,2},{4,7},{5,4},{6,5},{7,6},{8,56},{9,57},{10,... | collective-permute-start | bytes 786440 | tf_op jit(solution)/shard_map/ppermute | solution.py:220
  71.4 11.4 %collective-permute-start.18 = (bf16[2,512,128]{2,1,0:T(8,128)(2,1)}, bf16[2,512,128]{2,1,0:T(8,128)(2,1)}, u32[]{:S(2)}, u32[]{:S(2)}) collective-permute-start(bf16[2,512,128]{2,1,0:T(8,128)(2,1)} %get-tuple-element.81), channel_id=1, source_target_pairs={{0,56},{1,57},{2,58},{3,59},{4,60},{5,61},{6,62},{7,63},{8,3},{9,0... | collective-permute-start | bytes 786440 | tf_op jit(solution)/shard_map/ppermute | solution.py:220
  75.0 17.3 %collective-permute-start.8 = (bf16[2,128,512]{2,1,0:T(8,128)(2,1)}, bf16[2,128,512]{2,1,0:T(8,128)(2,1)S(1)}, u32[]{:S(2)}, u32[]{:S(2)}) collective-permute-start(bf16[2,128,512]{2,1,0:T(8,128)(2,1)} %get-tuple-element.70), channel_id=1, source_target_pairs={{0,3},{1,0},{2,1},{3,2},{4,7},{5,4},{6,5},{7,6},{8,11},{9,8},{10,9... | collective-permute-start | bytes 786440 | tf_op jit(solution)/shard_map/ppermute | solution.py:220
  78.6 15.3 %collective-permute-start.9 = (bf16[2,128,512]{2,1,0:T(8,128)(2,1)}, bf16[2,128,512]{2,1,0:T(8,128)(2,1)S(1)}, u32[]{:S(2)}, u32[]{:S(2)}) collective-permute-start(bf16[2,128,512]{2,1,0:T(8,128)(2,1)} %get-tuple-element.71), channel_id=1, source_target_pairs={{0,2},{1,3},{2,0},{3,1},{4,6},{5,7},{6,4},{7,5},{8,10},{9,11},{10,... | collective-permute-start | bytes 786440 | tf_op jit(solution)/shard_map/ppermute | solution.py:220
  80.9 13.3 %collective-permute-start.10 = (bf16[2,128,512]{2,1,0:T(8,128)(2,1)}, bf16[2,128,512]{2,1,0:T(8,128)(2,1)S(1)}, u32[]{:S(2)}, u32[]{:S(2)}) collective-permute-start(bf16[2,128,512]{2,1,0:T(8,128)(2,1)} %get-tuple-element.72), channel_id=1, source_target_pairs={{0,1},{1,2},{2,3},{3,0},{4,5},{5,6},{6,7},{7,4},{8,9},{9,10},{10,1... | collective-permute-start | bytes 786440 | tf_op jit(solution)/shard_map/ppermute | solution.py:220
  91.7 25.5 %collective-permute-start.19 = (bf16[8,512,128]{2,1,0:T(8,128)(2,1)}, bf16[8,512,128]{2,1,0:T(8,128)(2,1)S(1)}, u32[]{:S(2)}, u32[]{:S(2)}) collective-permute-start(bf16[8,512,128]{2,1,0:T(8,128)(2,1)} %get-tuple-element.85), channel_id=1, source_target_pairs={{0,16},{1,17},{2,18},{3,19},{4,20},{5,21},{6,22},{7,23},{8,9},{9,1... | collective-permute-start | bytes 3145736 | tf_op jit(solution)/shard_map/ppermute | solution.py:220
  92.1 25.1 %collective-permute-start.20 = (bf16[8,512,128]{2,1,0:T(8,128)(2,1)}, bf16[8,512,128]{2,1,0:T(8,128)(2,1)S(1)}, u32[]{:S(2)}, u32[]{:S(2)}) collective-permute-start(bf16[8,512,128]{2,1,0:T(8,128)(2,1)} %get-tuple-element.86), channel_id=1, source_target_pairs={{0,32},{1,33},{2,34},{3,35},{4,36},{5,37},{6,38},{7,39},{8,10},{9,... | collective-permute-start | bytes 3145736 | tf_op jit(solution)/shard_map/ppermute | solution.py:220
  92.3 26.7 %collective-permute-start.21 = (bf16[8,512,128]{2,1,0:T(8,128)(2,1)}, bf16[8,512,128]{2,1,0:T(8,128)(2,1)}, u32[]{:S(2)}, u32[]{:S(2)}) collective-permute-start(bf16[8,512,128]{2,1,0:T(8,128)(2,1)} %get-tuple-element.87), channel_id=1, source_target_pairs={{0,48},{1,49},{2,50},{3,51},{4,52},{5,53},{6,54},{7,55},{8,11},{9,... | collective-permute-start | bytes 3145736 | tf_op jit(solution)/shard_map/ppermute | solution.py:220
  94.3 12.3 %collective-permute-start.11 = (bf16[2,128,512]{2,1,0:T(8,128)(2,1)S(1)}, bf16[2,128,512]{2,1,0:T(8,128)(2,1)S(1)}, u32[]{:S(2)}, u32[]{:S(2)}) collective-permute-start(bf16[2,128,512]{2,1,0:T(8,128)(2,1)S(1)} %fusion.7), channel_id=1, source_target_pairs={{4,0},{5,1},{6,2},{7,3},{8,4},{9,5},{10,6},{11,7},{12,8},{13,9},{1... | collective-permute-start | bytes 786440 | tf_op jit(solution)/shard_map/ppermute | solution.py:210
  122.1 33.5 %all-to-all-start = ((bf16[8,512,128]{2,1,0:T(8,128)(2,1)}), bf16[8,512,128]{2,1,0:T(8,128)(2,1)S(1)}, u32[]{:S(2)}, u32[]{:S(2)}) async-start(bf16[8,512,128]{2,1,0:T(8,128)(2,1)} %add_convert_fusion), calls=%async_computation | async-start | bytes 2097152 | tf_op jit(solution)/shard_map/all_to_all | solution.py:351
  155.8 9.7 %collective-permute-start.22 = (bf16[512,128]{1,0:T(8,128)(2,1)S(1)}, bf16[512,128]{1,0:T(8,128)(2,1)S(1)}, u32[]{:S(2)}, u32[]{:S(2)}) collective-permute-start(bf16[512,128]{1,0:T(8,128)(2,1)S(1)} %reduce_sum.12), channel_id=1, source_target_pairs={{9,24},{10,40},{11,56},{13,28},{14,44},{15,60},{24,9},{26,41},{27,... | collective-permute-start | bytes 393224 | tf_op jit(solution)/shard_map/ppermute | solution.py:220
  (12 other events, 82.5 us)

commit v3 on v2

--- a/solution.py
+++ b/solution.py
@@ -14,6 +14,7 @@
 SPAN = (BACK + 1) * TOKENS
 KV_HEADS = 4
 GROUP = 8
+HEADS_AT_ONCE = 8
 ZH, ZL, RING = 4, 2, 4
 ROWS = 1024
 FORWARD_MIB, BACKWARD_MIB, PREPARE_MIB, PRODUCT_MIB = 56, 56, 56, 56
@@ -57,10 +58,8 @@
     return dot_nt(keys, q_pair) * (SCALE * LOG2E) + bias
 
 
-def pair_rows(ref_or_val, pair):
-    a = ref_or_val[:, (2 * pair) * HEAD : (2 * pair + 1) * HEAD]
-    b = ref_or_val[:, (2 * pair + 1) * HEAD : (2 * pair + 2) * HEAD]
-    return jnp.concatenate([a, b], axis=0)
+def rows_of_heads(ref, at, count):
+    return jnp.concatenate([ref[:, h * HEAD : (h + 1) * HEAD] for h in range(at, at + count)], axis=0)
 
 
 def forward_kernel(here_ref, len_ref, q_ref, *refs):
@@ -76,18 +75,18 @@
 
     keys = jnp.concatenate([r[0] for r in kv_refs], axis=0)
     values_t = jnp.concatenate([r[1] for r in kv_refs], axis=0).T
-    bias = jnp.concatenate([bias_ref[...]] * 2, axis=1)
+    bias = jnp.concatenate([bias_ref[...]] * HEADS_AT_ONCE, axis=1)
     zl = g // 2
     quads = []
-    for pair in range(GROUP // 2):
-        s = scores_of(keys, pair_rows(q_ref, pair), bias)
+    for at in range(0, GROUP, HEADS_AT_ONCE):
+        s = scores_of(keys, rows_of_heads(q_ref, at, HEADS_AT_ONCE), bias)
         top = jnp.max(s, axis=0, keepdims=True)
         p = jnp.exp2(s - top)
         total = jnp.sum(p, axis=0, keepdims=True)
         out_t = (dot(values_t, p.astype(BF)) / total).astype(BF)
         log_total = top + jnp.log2(total)
-        for i in range(2):
-            h = 2 * pair + i
+        for i in range(HEADS_AT_ONCE):
+            h = at + i
             quads.append(out_t[:, i * TOKENS : (i + 1) * TOKENS])
             log_ref[0, h : h + 1, :] = log_total[:, i * TOKENS : (i + 1) * TOKENS]
     for u in range(2):
@@ -126,14 +125,14 @@
     keys = jnp.concatenate([r[0] for r in kv_refs], axis=0)
     values = jnp.concatenate([r[1] for r in kv_refs], axis=0)
     keys_t = keys.T
-    bias = jnp.concatenate([bias_ref[...]] * 2, axis=1)
-    ratio = jnp.concatenate([ratio_ref[...]] * 2, axis=0)
+    bias = jnp.concatenate([bias_ref[...]] * HEADS_AT_ONCE, axis=1)
+    ratio = jnp.concatenate([ratio_ref[...]] * HEADS_AT_ONCE, axis=0)
     dk = jnp.zeros((SPAN, HEAD), F32)
     dv = jnp.zeros((SPAN, HEAD), F32)
-    for pair in range(GROUP // 2):
-        q = pair_rows(q_ref, pair)
-        grad = (pair_rows(g_ref, pair).astype(F32) * ratio).astype(BF)
-        logs = jnp.concatenate([log_ref[0, 2 * pair : 2 * pair + 1, :], log_ref[0, 2 * pair + 1 : 2 * pair + 2, :]], axis=1)
+    for at in range(0, GROUP, HEADS_AT_ONCE):
+        q = rows_of_heads(q_ref, at, HEADS_AT_ONCE)
+        grad = (rows_of_heads(g_ref, at, HEADS_AT_ONCE).astype(F32) * ratio).astype(BF)
+        logs = jnp.concatenate([log_ref[0, h : h + 1, :] for h in range(at, at + HEADS_AT_ONCE)], axis=1)
         p = jnp.exp2(scores_of(keys, q, bias) - logs)
         dp = dot_nt(values, grad)
         delta = jnp.sum(p * dp, axis=0, keepdims=True)
@@ -141,8 +140,8 @@
         dv = dv + dot(p.astype(BF), grad)
         dk = dk + dot(ds, q)
         dq_t = dot(keys_t, ds) * SCALE
-        for i in range(2):
-            h = 2 * pair + i
+        for i in range(HEADS_AT_ONCE):
+            h = at + i
             dq_ref[:, h * HEAD : (h + 1) * HEAD] = dq_t[:, i * TOKENS : (i + 1) * TOKENS].T
     dk = dk * SCALE
     own_ref[0] = dk[BACK * TOKENS :]
@@ -240,6 +239,15 @@
     return moved(v, lambda zh, x, c, zl, y: (zh, y, c, zl, x) if c == 1 and x != y else None)
 
 
+def y_turn(v, by):
+    return moved(v, lambda zh, x, c, zl, y: (zh, x, c, zl, (y + by) % RING))
+
+
+def from_predecessors(kv, y):
+    before = along_tokens(kv, BACK)
+    return [before] + [y_turn(jnp.where(y + by < RING, kv, before), by) for by in range(BACK - 1, 0, -1)]
+
+
 def brought_home(own, backs, y):
     before = backs[RING - 1].astype(F32)
     for by in range(1, RING):
@@ -325,7 +333,7 @@
     place = jnp.stack([here, in_group, in_reduce, core])
 
     kv, keep, send = prepare(place, old, new, keys, values, cotangent)
-    kvs = [along_tokens(kv, by) for by in range(BACK, 0, -1)] + [kv]
+    kvs = from_predecessors(kv, y) + [kv]
     w_mine = jnp.concatenate([keep, core_swap(send)], axis=0)
     kvs[AFTER], w_soon = lax.optimization_barrier((kvs[AFTER], w_mine))
     *kvs, w_late = lax.optimization_barrier((*kvs, w_mine))
@@ -333,12 +341,15 @@
 
     same, cross, logs = attention_forward(place, lengths, queries, kvs)
     dq, own, *backs = attention_backward(place, lengths, old, new, queries, head_grads, logs, kvs)
-    *pieces, ws[1], ws[2], ws[3], own = lax.optimization_barrier((*same, *cross, *ws[1:], own))
+    pieces = [*same, *cross]
+    pieces[2] = group_turn(same[2], 2)
+    pieces[RING + 2] = cross_turn(cross[2], 2)
+    *pieces, ws[1], ws[2], ws[3], own = lax.optimization_barrier((*pieces, *ws[1:], own))
     same, cross = pieces[:RING], pieces[RING:]
     outs = []
     for by in range(RING):
-        outs.append(group_turn(same[by], by) if by else same[0])
-        outs.append(cross_turn(cross[by], by))
+        outs.append(group_turn(same[by], by) if by % 2 else same[by])
+        outs.append(cross[by] if by == 2 else cross_turn(cross[by], by))
 
     first = ((in_reduce + 1) % RING).reshape(1)
     sent = product(first, RING - 1, outs, ws)

time: 168 us -> 162 us (0.964)
  waiting for transfers between devices: 55 us -> 68.9 us
  starting transfers between devices: 59.3 us -> 46.2 us
  Pallas kernels: 40.3 us -> 34.8 us
    ppermute x18 -> x21, waiting for transfers between devices: 14.3 us -> 34.4 us  [moved(): return lax.ppermute(v, FLAT, pairs)]
    ppermute x5 -> x2, starting transfers between devices: 22.7 us -> 9.53 us  [along_tokens(): lax.ppermute(v, FLAT, [(i, i + by) for i in range(count) if 0 <= i + by <...]
    ppermute x5 -> x2, waiting for transfers between devices: 15.5 us -> 9.49 us  [along_tokens(): lax.ppermute(v, FLAT, [(i, i + by) for i in range(count) if 0 <= i + by <...]
    pallas_call x1, Pallas kernels: 12.3 us -> 8.45 us  [attention_forward(): pl.pallas_call(forward_kernel, grid_spec=pltpu.PrefetchScalarGridSpec(num...]
    pallas_call x1, Pallas kernels: 13.2 us -> 11.4 us  [attention_backward(): pl.pallas_call(backward_kernel, grid_spec=pltpu.PrefetchScalarGridSpec(nu...]
    ppermute x18 -> x21, starting transfers between devices: 28.2 us -> 29.2 us  [moved(): return lax.ppermute(v, FLAT, pairs)]
    unnamed x41 -> x39, local copies, waits for them, and re-layouts: 3.81 us -> 3.8 us
  transfers between devices with their start and end apart: 24 -> 24, of which waited for: 10 -> 13; matrix products, arithmetic and copies ran while one was open for 2% -> 2% of each run, Pallas kernels for 23% -> 20%
where the time goes in v3:
time: 162 us; the launch traced here: 161 us
  waiting for transfers between devices  68.9 us (43%)
  starting transfers between devices  46.2 us (29%)
  Pallas kernels  34.8 us (21%)
  other arithmetic  5.76 us (4%)
  local copies, waits for them, and re-layouts  4.66 us (3%)
    ppermute x21, waiting for transfers between devices, moved(): return lax.ppermute(v, FLAT, pairs)  34.4 us
    ppermute x21, starting transfers between devices, moved(): return lax.ppermute(v, FLAT, pairs)  29.2 us
    all_to_all x1, waiting for transfers between devices, shards(): lax.all_to_all(part, ('zh', 'zl'), split_axis=0, concat_axis=0, tiled=True)  25.1 us
    pallas_call x2, Pallas kernels, product(): pl.pallas_call(product_kernel, grid_spec=pltpu.PrefetchScalarGridSpec(num...  12.2 us
    pallas_call x1, Pallas kernels, attention_backward(): pl.pallas_call(backward_kernel, grid_spec=pltpu.PrefetchScalarGridSpec(nu...  11.4 us
    ppermute x2, starting transfers between devices, along_tokens(): lax.ppermute(v, FLAT, [(i, i + by) for i in range(count) if 0 <= i + by <...  9.53 us
    ppermute x2, waiting for transfers between devices, along_tokens(): lax.ppermute(v, FLAT, [(i, i + by) for i in range(count) if 0 <= i + by <...  9.49 us
    pallas_call x1, Pallas kernels, attention_forward(): pl.pallas_call(forward_kernel, grid_spec=pltpu.PrefetchScalarGridSpec(num...  8.45 us
  transfers between devices with their start and end apart: 24, of which 13 were waited for; matrix products, arithmetic and copies ran while one was open for 2% of the time, Pallas kernels for 20%

profile of v3, /device:TPU:17, one launch (start us, length us, event | category | flops | bytes accessed | tf_op | source)
XLA Modules:
  0.0 161.3 jit_solution(9867722932847585702)
XLA Ops:
  1.2 2.7 %prepare.1 = (bf16[2,128,512]{2,1,0:T(8,128)(2,1)}, bf16[128,2048]{1,0:T(8,128)(2,1)}, bf16[128,2048]{1,0:T(8,128)(2,1)}) custom-call(s32[4]{0:T(128)} %pad_add_fusion.place_ref.here_ref, f32[1,128]{1,0:T(1,128)} %bitcast.12, f32[1,128]{1,0:T(1,128)} %bitcast.14, bf16[128,512]{1,0:T(8,128)(2,1)} %keys_ref.1, bf16[128,512]{1,0:T(8,128)(2,1)} %values_ref.1, ...), custom_call_target="tpu_custom_call" | custom-call | flops 1048576 | bytes 4194304 | tf_op jit(solution)/shard_map/prepare/pallas_call | solution.py:279
  4.0 3.5 %collective-permute-start = (bf16[2,128,512]{2,1,0:T(8,128)(2,1)}, bf16[2,128,512]{2,1,0:T(8,128)(2,1)S(1)}, u32[]{:S(2)}, u32[]{:S(2)}) collective-permute-start(bf16[2,128,512]{2,1,0:T(8,128)(2,1)} %get-tuple-element.55.refs_4_), channel_id=1, source_target_pairs={{0,4},{1,5},{2,6},{3,7},{4,8},{5,9},{6,10},{7,11},{8,12},{9,13},{1... | collective-permute-start | bytes 786440 | tf_op jit(solution)/shard_map/ppermute | solution.py:209
  8.6 6.2 %collective-permute-done.refs_0_ = bf16[2,128,512]{2,1,0:T(8,128)(2,1)S(1)} collective-permute-done((bf16[2,128,512]{2,1,0:T(8,128)(2,1)}, bf16[2,128,512]{2,1,0:T(8,128)(2,1)S(1)}, u32[]{:S(2)}, u32[]{:S(2)}) %collective-permute-start) | collective-permute-done | bytes 262176 | tf_op jit(solution)/shard_map/ppermute | solution.py:209
  14.8 1.1 broadcast_select_fusion
  15.9 1.1 collective-permute-start.3
  18.3 1.1 constant_dynamic-update-slice_fusion.1
  19.4 4.9 %collective-permute-done.3.refs_3_ = bf16[2,128,512]{2,1,0:T(8,128)(2,1)S(1)} collective-permute-done((bf16[2,128,512]{2,1,0:T(8,128)(2,1)S(1)}, bf16[2,128,512]{2,1,0:T(8,128)(2,1)S(1)}, u32[]{:S(2)}, u32[]{:S(2)}) %collective-permute-start.3) | collective-permute-done | bytes 262176 | tf_op jit(solution)/shard_map/ppermute | solution.py:219
  24.3 5.5 %collective-permute-done.2.refs_2_ = bf16[2,128,512]{2,1,0:T(8,128)(2,1)S(1)} collective-permute-done((bf16[2,128,512]{2,1,0:T(8,128)(2,1)S(1)}, bf16[2,128,512]{2,1,0:T(8,128)(2,1)S(1)}, u32[]{:S(2)}, u32[]{:S(2)}) %collective-permute-start.2) | collective-permute-done | bytes 262176 | tf_op jit(solution)/shard_map/ppermute | solution.py:219
  29.8 1.6 %collective-permute-done.1.refs_1_ = bf16[2,128,512]{2,1,0:T(8,128)(2,1)S(1)} collective-permute-done((bf16[2,128,512]{2,1,0:T(8,128)(2,1)S(1)}, bf16[2,128,512]{2,1,0:T(8,128)(2,1)S(1)}, u32[]{:S(2)}, u32[]{:S(2)}) %collective-permute-start.1) | collective-permute-done | bytes 262176 | tf_op jit(solution)/shard_map/ppermute | solution.py:219
  31.4 1.5 collective-permute-start.7
  32.9 2.3 %collective-permute-start.8 = (bf16[256,2048]{1,0:T(8,128)(2,1)S(1)}, bf16[256,2048]{1,0:T(8,128)(2,1)S(1)}, u32[]{:S(2)}, u32[]{:S(2)}) collective-permute-start(bf16[256,2048]{1,0:T(8,128)(2,1)S(1)} %constant_dynamic-update-slice_fusion.refs_8_), channel_id=1, source_target_pairs={{0,2},{1,3},{2,0},{3,1},{4,6},{5,7},{6,4},{7,5},{8,40},{9,41},{10,... | collective-permute-start | bytes 3145736 | tf_op jit(solution)/shard_map/ppermute | solution.py:219
  35.2 8.5 %attention_forward.1 = (bf16[2,512,128]{2,1,0:T(8,128)(2,1)}, bf16[2,512,128]{2,1,0:T(8,128)(2,1)}, bf16[2,512,128]{2,1,0:T(8,128)(2,1)}, bf16[2,512,128]{2,1,0:...) custom-call(s32[4]{0:T(128)} %pad_add_fusion.place_ref.here_ref, ...), custom_call_target="tpu_custom_call" | custom-call | flops 1342177280 | bytes 4194304 | tf_op jit(solution)/shard_map/attention_forward/pallas_call | solution.py:167
  44.4 2.5 %collective-permute-start.6 = (bf16[2,512,128]{2,1,0:T(8,128)(2,1)}, bf16[2,512,128]{2,1,0:T(8,128)(2,1)S(1)}, u32[]{:S(2)}, u32[]{:S(2)}) collective-permute-start(bf16[2,512,128]{2,1,0:T(8,128)(2,1)} %get-tuple-element.64), channel_id=1, source_target_pairs={{0,40},{1,41},{2,42},{3,43},{4,44},{5,45},{6,46},{7,47},{8,2},{9,3... | collective-permute-start | bytes 786440 | tf_op jit(solution)/shard_map/ppermute | solution.py:219
  47.0 11.4 %attention_backward.1 = (f32[128,4096]{1,0:T(8,128)}, f32[2,128,512]{2,1,0:T(8,128)}, bf16[2,128,512]{2,1,0:T(8,128)(2,1)}, bf16[2,128,512]{2,1,0:T(8,128)(2,1)}...) custom-call(s32[4]{0:T(128)} %pad_add_fusion.place_ref.here_ref, s32[1,128]{1,0:T(1,128)} %bitcast.17, ...), custom_call_target="tpu_custom_call" | custom-call | flops 3355443200 | bytes 8388608 | tf_op jit(solution)/shard_map/attention_backward/pallas_call | solution.py:187
  58.4 5.9 %collective-permute-done.5.refs_4_ = bf16[2,512,128]{2,1,0:T(8,128)(2,1)S(1)} collective-permute-done((bf16[2,512,128]{2,1,0:T(8,128)(2,1)}, bf16[2,512,128]{2,1,0:T(8,128)(2,1)S(1)}, u32[]{:S(2)}, u32[]{:S(2)}) %collective-permute-start.5) | collective-permute-done | bytes 262176 | tf_op jit(solution)/shard_map/ppermute | solution.py:219
  66.9 1.5 collective-permute-start.15
  68.5 2.4 %collective-permute-start.16 = (bf16[2,512,128]{2,1,0:T(8,128)(2,1)}, bf16[2,512,128]{2,1,0:T(8,128)(2,1)S(1)}, u32[]{:S(2)}, u32[]{:S(2)}) collective-permute-start(bf16[2,512,128]{2,1,0:T(8,128)(2,1)} %get-tuple-element.77), channel_id=1, source_target_pairs={{0,24},{1,25},{2,26},{3,27},{4,28},{5,29},{6,30},{7,31},{8,1},{9,2... | collective-permute-start | bytes 786440 | tf_op jit(solution)/shard_map/ppermute | solution.py:219
  71.4 2.2 %collective-permute-start.18 = (bf16[2,512,128]{2,1,0:T(8,128)(2,1)S(1)}, bf16[2,512,128]{2,1,0:T(8,128)(2,1)S(1)}, u32[]{:S(2)}, u32[]{:S(2)}) collective-permute-start(bf16[2,512,128]{2,1,0:T(8,128)(2,1)S(1)} %copy-done.14), channel_id=1, source_target_pairs={{0,56},{1,57},{2,58},{3,59},{4,60},{5,61},{6,62},{7,63},{8,3},{9,0... | collective-permute-start | bytes 786440 | tf_op jit(solution)/shard_map/ppermute | solution.py:219
  74.3 3.2 %collective-permute-start.11 = (bf16[2,128,512]{2,1,0:T(8,128)(2,1)}, bf16[2,128,512]{2,1,0:T(8,128)(2,1)S(1)}, u32[]{:S(2)}, u32[]{:S(2)}) collective-permute-start(bf16[2,128,512]{2,1,0:T(8,128)(2,1)} %get-tuple-element.71), channel_id=1, source_target_pairs={{0,2},{1,3},{2,0},{3,1},{4,6},{5,7},{6,4},{7,5},{8,10},{9,11},{10,... | collective-permute-start | bytes 786440 | tf_op jit(solution)/shard_map/ppermute | solution.py:219
  80.0 8.1 %product.3 = (bf16[8,512,128]{2,1,0:T(8,128)(2,1)}, bf16[8,512,128]{2,1,0:T(8,128)(2,1)}, bf16[8,512,128]{2,1,0:T(8,128)(2,1)}) custom-call(s32[1]{0:T(128)} %bitcast.7.first_ref, bf16[2,512,128]{2,1,0:T(8,128)(2,1)} %get-tuple-element.74.refs_0_, bf16[2,512,128]{2,1,0:T(8,128)(2,1)} %copy-done.9, bf16[2,512,128]{2,1,0:T(8,128)(2,1)} %copy-done.10, ...), custom_call_target="tpu_custom_call" | custom-call | flops 3221225472 | bytes 8388608 | tf_op jit(solution)/shard_map/product/pallas_call | solution.py:309
  88.1 1.2 collective-permute-start.19
  89.3 1.4 collective-permute-start.21
  90.9 6.0 %collective-permute-start.13 = (bf16[2,128,512]{2,1,0:T(8,128)(2,1)S(1)}, bf16[2,128,512]{2,1,0:T(8,128)(2,1)S(1)}, u32[]{:S(2)}, u32[]{:S(2)}) collective-permute-start(bf16[2,128,512]{2,1,0:T(8,128)(2,1)S(1)} %fusion.7), channel_id=1, source_target_pairs={{4,0},{5,1},{6,2},{7,3},{8,4},{9,5},{10,6},{11,7},{12,8},{13,9},{1... | collective-permute-start | bytes 786440 | tf_op jit(solution)/shard_map/ppermute | solution.py:209
  96.9 3.3 %collective-permute-done.13 = bf16[2,128,512]{2,1,0:T(8,128)(2,1)S(1)} collective-permute-done((bf16[2,128,512]{2,1,0:T(8,128)(2,1)S(1)}, bf16[2,128,512]{2,1,0:T(8,128)(2,1)S(1)}, u32[]{:S(2)}, u32[]{:S(2)}) %collective-permute-start.13) | collective-permute-done | bytes 262176 | tf_op jit(solution)/shard_map/ppermute | solution.py:209
  100.4 4.1 %product.2 = bf16[8,512,128]{2,1,0:T(8,128)(2,1)} custom-call(s32[1]{0:T(128)} %bitcast.2.first_ref, bf16[2,512,128]{2,1,0:T(8,128)(2,1)} %get-tuple-element.74.refs_0_, bf16[2,512,128]{2,1,0:T(8,128)(2,1)} %copy-done.9, bf16[2,512,128]{2,1,0:T(8,128)(2,1)} %copy-done.10, bf16[2,512,128]{2,1,0:T(8,128)(2,1)} %copy-done.11, bf16[2,512,128]{2,1,0:T(8,128)(2,1)} %copy-done.7, ...), custom_call_target="tpu_custom_call" | custom-call | flops 1073741824 | bytes 4194304 | tf_op jit(solution)/shard_map/product/pallas_call | solution.py:309
  104.6 8.9 %collective-permute-done.19 = bf16[8,512,128]{2,1,0:T(8,128)(2,1)S(1)} collective-permute-done((bf16[8,512,128]{2,1,0:T(8,128)(2,1)}, bf16[8,512,128]{2,1,0:T(8,128)(2,1)S(1)}, u32[]{:S(2)}, u32[]{:S(2)}) %collective-permute-start.19) | collective-permute-done | bytes 1048608 | tf_op jit(solution)/shard_map/ppermute | solution.py:219
  113.5 1.8 %collective-permute-done.21 = bf16[8,512,128]{2,1,0:T(8,128)(2,1)S(1)} collective-permute-done((bf16[8,512,128]{2,1,0:T(8,128)(2,1)}, bf16[8,512,128]{2,1,0:T(8,128)(2,1)S(1)}, u32[]{:S(2)}, u32[]{:S(2)}) %collective-permute-start.21) | collective-permute-done | bytes 1048608 | tf_op jit(solution)/shard_map/ppermute | solution.py:219
  115.3 2.8 %add_convert_fusion = bf16[8,512,128]{2,1,0:T(8,128)(2,1)} fusion(bf16[8,512,128]{2,1,0:T(8,128)(2,1)S(1)} %collective-permute-done.21, bf16[8,512,128]{2,1,0:T(8,128)(2,1)S(1)} %collective-permute-done.20, bf16[8,512,128]{2,1,0:T(8,128)(2,1)S(1)} %collective-permute-done.19, bf16[8,512,128]{2,1,0:T(8,128)(2,1)} %product.2), kind=kLoop, calls=%fused_computation | loop fusion | flops 4194304 | bytes 5242880 | tf_op jit(solution)/shard_map/convert_element_type | solution.py:359
  118.1 7.4 %all-to-all-start = ((bf16[8,512,128]{2,1,0:T(8,128)(2,1)}), bf16[8,512,128]{2,1,0:T(8,128)(2,1)S(1)}, u32[]{:S(2)}, u32[]{:S(2)}) async-start(bf16[8,512,128]{2,1,0:T(8,128)(2,1)} %add_convert_fusion), calls=%async_computation | async-start | bytes 2097152 | tf_op jit(solution)/shard_map/all_to_all | solution.py:362
  125.6 25.1 %all-to-all-done = bf16[8,512,128]{2,1,0:T(8,128)(2,1)S(1)} async-done(((bf16[8,512,128]{2,1,0:T(8,128)(2,1)}), bf16[8,512,128]{2,1,0:T(8,128)(2,1)S(1)}, u32[]{:S(2)}, u32[]{:S(2)}) %all-to-all-start) | async-done | bytes 1048608 | tf_op jit(solution)/shard_map/all_to_all | solution.py:362
  150.8 5.1 %collective-permute-start.22 = (bf16[512,128]{1,0:T(8,128)(2,1)S(1)}, bf16[512,128]{1,0:T(8,128)(2,1)S(1)}, u32[]{:S(2)}, u32[]{:S(2)}) collective-permute-start(bf16[512,128]{1,0:T(8,128)(2,1)S(1)} %reduce_sum.12), channel_id=1, source_target_pairs={{9,24},{10,40},{11,56},{13,28},{14,44},{15,60},{24,9},{26,41},{27,... | collective-permute-start | bytes 393224 | tf_op jit(solution)/shard_map/ppermute | solution.py:219
  156.8 3.8 %collective-permute-done.22 = bf16[512,128]{1,0:T(8,128)(2,1)S(1)} collective-permute-done((bf16[512,128]{1,0:T(8,128)(2,1)S(1)}, bf16[512,128]{1,0:T(8,128)(2,1)S(1)}, u32[]{:S(2)}, u32[]{:S(2)}) %collective-permute-start.22) | collective-permute-done | bytes 131104 | tf_op jit(solution)/shard_map/ppermute | solution.py:219
  (69 shorter events, 12.2 us)
Async XLA Ops:
  4.0 10.8 %collective-permute-start = (bf16[2,128,512]{2,1,0:T(8,128)(2,1)}, bf16[2,128,512]{2,1,0:T(8,128)(2,1)S(1)}, u32[]{:S(2)}, u32[]{:S(2)}) collective-permute-start(bf16[2,128,512]{2,1,0:T(8,128)(2,1)} %get-tuple-element.55.refs_4_), channel_id=1, source_target_pairs={{0,4},{1,5},{2,6},{3,7},{4,8},{5,9},{6,10},{7,11},{8,12},{9,13},{1... | collective-permute-start | bytes 786440 | tf_op jit(solution)/shard_map/ppermute | solution.py:209
  7.5 11.8 %collective-permute-start.4 = (bf16[128,2048]{1,0:T(8,128)(2,1)}, bf16[128,2048]{1,0:T(8,128)(2,1)S(1)}, u32[]{:S(2)}, u32[]{:S(2)}) collective-permute-start(bf16[128,2048]{1,0:T(8,128)(2,1)} %get-tuple-element.49), channel_id=1, source_target_pairs={{0,8},{1,9},{2,10},{3,11},{4,12},{5,13},{6,14},{7,15},{8,0},{9,1},... | collective-permute-start | bytes 1572872 | tf_op jit(solution)/shard_map/ppermute | solution.py:219
  14.8 20.4 %copy-start.6 = (bf16[2,128,512]{2,1,0:T(8,128)(2,1)}, bf16[2,128,512]{2,1,0:T(8,128)(2,1)S(1)}, u32[]{:S(2)}) copy-start(bf16[2,128,512]{2,1,0:T(8,128)(2,1)S(1)} %collective-permute-done.refs_0_) | copy-start | bytes 786436
  15.9 8.4 %collective-permute-start.3 = (bf16[2,128,512]{2,1,0:T(8,128)(2,1)S(1)}, bf16[2,128,512]{2,1,0:T(8,128)(2,1)S(1)}, u32[]{:S(2)}, u32[]{:S(2)}) collective-permute-start(bf16[2,128,512]{2,1,0:T(8,128)(2,1)S(1)} %get-tuple-element.92), channel_id=1, source_target_pairs={{0,1},{1,2},{2,3},{3,0},{4,5},{5,6},{6,7},{7,4},{8,9},{9,10},{10,1... | collective-permute-start | bytes 786440 | tf_op jit(solution)/shard_map/ppermute | solution.py:219
  17.0 12.8 %collective-permute-start.2 = (bf16[2,128,512]{2,1,0:T(8,128)(2,1)S(1)}, bf16[2,128,512]{2,1,0:T(8,128)(2,1)S(1)}, u32[]{:S(2)}, u32[]{:S(2)}) collective-permute-start(bf16[2,128,512]{2,1,0:T(8,128)(2,1)S(1)} %get-tuple-element.93), channel_id=1, source_target_pairs={{0,2},{1,3},{2,0},{3,1},{4,6},{5,7},{6,4},{7,5},{8,10},{9,11},{10,... | collective-permute-start | bytes 786440 | tf_op jit(solution)/shard_map/ppermute | solution.py:219
  17.3 14.1 %collective-permute-start.1 = (bf16[2,128,512]{2,1,0:T(8,128)(2,1)S(1)}, bf16[2,128,512]{2,1,0:T(8,128)(2,1)S(1)}, u32[]{:S(2)}, u32[]{:S(2)}) collective-permute-start(bf16[2,128,512]{2,1,0:T(8,128)(2,1)S(1)} %get-tuple-element.94), channel_id=1, source_target_pairs={{0,3},{1,0},{2,1},{3,2},{4,7},{5,4},{6,5},{7,6},{8,11},{9,8},{10,9... | collective-permute-start | bytes 786440 | tf_op jit(solution)/shard_map/ppermute | solution.py:219
  19.4 24.3 %copy-start = (bf16[256,2048]{1,0:T(8,128)(2,1)}, bf16[256,2048]{1,0:T(8,128)(2,1)S(1)}, u32[]{:S(2)}) copy-start(bf16[256,2048]{1,0:T(8,128)(2,1)S(1)} %constant_dynamic-update-slice_fusion.refs_8_) | copy-start | bytes 3145732
  31.4 32.8 %collective-permute-start.9 = (bf16[256,2048]{1,0:T(8,128)(2,1)S(1)}, bf16[256,2048]{1,0:T(8,128)(2,1)S(1)}, u32[]{:S(2)}, u32[]{:S(2)}) collective-permute-start(bf16[256,2048]{1,0:T(8,128)(2,1)S(1)} %constant_dynamic-update-slice_fusion.refs_8_), channel_id=1, source_target_pairs={{0,3},{1,0},{2,1},{3,2},{4,7},{5,4},{6,5},{7,6},{8,56},{9,57},{10,... | collective-permute-start | bytes 3145736 | tf_op jit(solution)/shard_map/ppermute | solution.py:219
  31.4 32.8 %collective-permute-start.7 = (bf16[256,2048]{1,0:T(8,128)(2,1)S(1)}, bf16[256,2048]{1,0:T(8,128)(2,1)S(1)}, u32[]{:S(2)}, u32[]{:S(2)}) collective-permute-start(bf16[256,2048]{1,0:T(8,128)(2,1)S(1)} %constant_dynamic-update-slice_fusion.refs_8_), channel_id=1, source_target_pairs={{0,1},{1,2},{2,3},{3,0},{4,5},{5,6},{6,7},{7,4},{8,24},{9,25},{10,... | collective-permute-start | bytes 3145736 | tf_op jit(solution)/shard_map/ppermute | solution.py:219
  32.9 31.4 %collective-permute-start.8 = (bf16[256,2048]{1,0:T(8,128)(2,1)S(1)}, bf16[256,2048]{1,0:T(8,128)(2,1)S(1)}, u32[]{:S(2)}, u32[]{:S(2)}) collective-permute-start(bf16[256,2048]{1,0:T(8,128)(2,1)S(1)} %constant_dynamic-update-slice_fusion.refs_8_), channel_id=1, source_target_pairs={{0,2},{1,3},{2,0},{3,1},{4,6},{5,7},{6,4},{7,5},{8,40},{9,41},{10,... | collective-permute-start | bytes 3145736 | tf_op jit(solution)/shard_map/ppermute | solution.py:219
  43.7 20.6 %collective-permute-start.5 = (bf16[2,512,128]{2,1,0:T(8,128)(2,1)}, bf16[2,512,128]{2,1,0:T(8,128)(2,1)S(1)}, u32[]{:S(2)}, u32[]{:S(2)}) collective-permute-start(bf16[2,512,128]{2,1,0:T(8,128)(2,1)} %get-tuple-element.60), channel_id=1, source_target_pairs={{0,2},{1,3},{2,0},{3,1},{4,6},{5,7},{6,4},{7,5},{8,40},{9,41},{10,... | collective-permute-start | bytes 786440 | tf_op jit(solution)/shard_map/ppermute | solution.py:219
  44.4 19.8 %collective-permute-start.6 = (bf16[2,512,128]{2,1,0:T(8,128)(2,1)}, bf16[2,512,128]{2,1,0:T(8,128)(2,1)S(1)}, u32[]{:S(2)}, u32[]{:S(2)}) collective-permute-start(bf16[2,512,128]{2,1,0:T(8,128)(2,1)} %get-tuple-element.64), channel_id=1, source_target_pairs={{0,40},{1,41},{2,42},{3,43},{4,44},{5,45},{6,46},{7,47},{8,2},{9,3... | collective-permute-start | bytes 786440 | tf_op jit(solution)/shard_map/ppermute | solution.py:219
  47.0 23.9 %copy-start.15 = (bf16[2,512,128]{2,1,0:T(8,128)(2,1)S(1)}, bf16[2,512,128]{2,1,0:T(8,128)(2,1)}, u32[]{:S(2)}) copy-start(bf16[2,512,128]{2,1,0:T(8,128)(2,1)} %get-tuple-element.80) | copy-start | bytes 786436
  47.0 24.4 %copy-start.14 = (bf16[2,512,128]{2,1,0:T(8,128)(2,1)S(1)}, bf16[2,512,128]{2,1,0:T(8,128)(2,1)}, u32[]{:S(2)}) copy-start(bf16[2,512,128]{2,1,0:T(8,128)(2,1)} %get-tuple-element.81) | copy-start | bytes 786436
  64.2 15.0 %copy-start.7 = (bf16[2,512,128]{2,1,0:T(8,128)(2,1)}, bf16[2,512,128]{2,1,0:T(8,128)(2,1)S(1)}, u32[]{:S(2)}) copy-start(bf16[2,512,128]{2,1,0:T(8,128)(2,1)S(1)} %collective-permute-done.5.refs_4_) | copy-start | bytes 786436
  64.3 15.0 %copy-start.8 = (bf16[2,512,128]{2,1,0:T(8,128)(2,1)}, bf16[2,512,128]{2,1,0:T(8,128)(2,1)S(1)}, u32[]{:S(2)}) copy-start(bf16[2,512,128]{2,1,0:T(8,128)(2,1)S(1)} %collective-permute-done.6.refs_5_) | copy-start | bytes 786436
  64.3 15.0 %copy-start.1 = (bf16[256,2048]{1,0:T(8,128)(2,1)}, bf16[256,2048]{1,0:T(8,128)(2,1)S(1)}, u32[]{:S(2)}) copy-start(bf16[256,2048]{1,0:T(8,128)(2,1)S(1)} %collective-permute-done.9.refs_11_) | copy-start | bytes 3145732
  66.3 7.3 %collective-permute-start.14 = (bf16[2,512,128]{2,1,0:T(8,128)(2,1)}, bf16[2,512,128]{2,1,0:T(8,128)(2,1)S(1)}, u32[]{:S(2)}, u32[]{:S(2)}) collective-permute-start(bf16[2,512,128]{2,1,0:T(8,128)(2,1)} %get-tuple-element.75), channel_id=1, source_target_pairs={{0,8},{1,9},{2,10},{3,11},{4,12},{5,13},{6,14},{7,15},{8,0},{9,1},... | collective-permute-start | bytes 786440 | tf_op jit(solution)/shard_map/ppermute | solution.py:219
  66.9 7.3 %collective-permute-start.15 = (bf16[2,512,128]{2,1,0:T(8,128)(2,1)}, bf16[2,512,128]{2,1,0:T(8,128)(2,1)S(1)}, u32[]{:S(2)}, u32[]{:S(2)}) collective-permute-start(bf16[2,512,128]{2,1,0:T(8,128)(2,1)} %get-tuple-element.76), channel_id=1, source_target_pairs={{0,1},{1,2},{2,3},{3,0},{4,5},{5,6},{6,7},{7,4},{8,24},{9,25},{10,... | collective-permute-start | bytes 786440 | tf_op jit(solution)/shard_map/ppermute | solution.py:219
  68.5 9.0 %collective-permute-start.16 = (bf16[2,512,128]{2,1,0:T(8,128)(2,1)}, bf16[2,512,128]{2,1,0:T(8,128)(2,1)S(1)}, u32[]{:S(2)}, u32[]{:S(2)}) collective-permute-start(bf16[2,512,128]{2,1,0:T(8,128)(2,1)} %get-tuple-element.77), channel_id=1, source_target_pairs={{0,24},{1,25},{2,26},{3,27},{4,28},{5,29},{6,30},{7,31},{8,1},{9,2... | collective-permute-start | bytes 786440 | tf_op jit(solution)/shard_map/ppermute | solution.py:219
  70.9 7.3 %collective-permute-start.17 = (bf16[2,512,128]{2,1,0:T(8,128)(2,1)S(1)}, bf16[2,512,128]{2,1,0:T(8,128)(2,1)S(1)}, u32[]{:S(2)}, u32[]{:S(2)}) collective-permute-start(bf16[2,512,128]{2,1,0:T(8,128)(2,1)S(1)} %copy-done.15), channel_id=1, source_target_pairs={{0,3},{1,0},{2,1},{3,2},{4,7},{5,4},{6,5},{7,6},{8,56},{9,57},{10,... | collective-permute-start | bytes 786440 | tf_op jit(solution)/shard_map/ppermute | solution.py:219
  71.4 7.9 %collective-permute-start.18 = (bf16[2,512,128]{2,1,0:T(8,128)(2,1)S(1)}, bf16[2,512,128]{2,1,0:T(8,128)(2,1)S(1)}, u32[]{:S(2)}, u32[]{:S(2)}) collective-permute-start(bf16[2,512,128]{2,1,0:T(8,128)(2,1)S(1)} %copy-done.14), channel_id=1, source_target_pairs={{0,56},{1,57},{2,58},{3,59},{4,60},{5,61},{6,62},{7,63},{8,3},{9,0... | collective-permute-start | bytes 786440 | tf_op jit(solution)/shard_map/ppermute | solution.py:219
  73.6 15.7 %collective-permute-start.10 = (bf16[2,128,512]{2,1,0:T(8,128)(2,1)}, bf16[2,128,512]{2,1,0:T(8,128)(2,1)S(1)}, u32[]{:S(2)}, u32[]{:S(2)}) collective-permute-start(bf16[2,128,512]{2,1,0:T(8,128)(2,1)} %get-tuple-element.70), channel_id=1, source_target_pairs={{0,3},{1,0},{2,1},{3,2},{4,7},{5,4},{6,5},{7,6},{8,11},{9,8},{10,9... | collective-permute-start | bytes 786440 | tf_op jit(solution)/shard_map/ppermute | solution.py:219
  74.3 16.5 %collective-permute-start.11 = (bf16[2,128,512]{2,1,0:T(8,128)(2,1)}, bf16[2,128,512]{2,1,0:T(8,128)(2,1)S(1)}, u32[]{:S(2)}, u32[]{:S(2)}) collective-permute-start(bf16[2,128,512]{2,1,0:T(8,128)(2,1)} %get-tuple-element.71), channel_id=1, source_target_pairs={{0,2},{1,3},{2,0},{3,1},{4,6},{5,7},{6,4},{7,5},{8,10},{9,11},{10,... | collective-permute-start | bytes 786440 | tf_op jit(solution)/shard_map/ppermute | solution.py:219
  77.4 13.3 %collective-permute-start.12 = (bf16[2,128,512]{2,1,0:T(8,128)(2,1)}, bf16[2,128,512]{2,1,0:T(8,128)(2,1)S(1)}, u32[]{:S(2)}, u32[]{:S(2)}) collective-permute-start(bf16[2,128,512]{2,1,0:T(8,128)(2,1)} %get-tuple-element.72), channel_id=1, source_target_pairs={{0,1},{1,2},{2,3},{3,0},{4,5},{5,6},{6,7},{7,4},{8,9},{9,10},{10,1... | collective-permute-start | bytes 786440 | tf_op jit(solution)/shard_map/ppermute | solution.py:219
  80.0 20.3 %copy-start.4 = (f32[2,128,512]{2,1,0:T(8,128)S(1)}, f32[2,128,512]{2,1,0:T(8,128)}, u32[]{:S(2)}) copy-start(f32[2,128,512]{2,1,0:T(8,128)} %get-tuple-element.69) | copy-start | bytes 1572868
  88.1 25.4 %collective-permute-start.19 = (bf16[8,512,128]{2,1,0:T(8,128)(2,1)}, bf16[8,512,128]{2,1,0:T(8,128)(2,1)S(1)}, u32[]{:S(2)}, u32[]{:S(2)}) collective-permute-start(bf16[8,512,128]{2,1,0:T(8,128)(2,1)} %get-tuple-element.85), channel_id=1, source_target_pairs={{0,16},{1,17},{2,18},{3,19},{4,20},{5,21},{6,22},{7,23},{8,9},{9,1... | collective-permute-start | bytes 3145736 | tf_op jit(solution)/shard_map/ppermute | solution.py:219
  89.3 24.1 %collective-permute-start.20 = (bf16[8,512,128]{2,1,0:T(8,128)(2,1)}, bf16[8,512,128]{2,1,0:T(8,128)(2,1)S(1)}, u32[]{:S(2)}, u32[]{:S(2)}) collective-permute-start(bf16[8,512,128]{2,1,0:T(8,128)(2,1)} %get-tuple-element.86), channel_id=1, source_target_pairs={{0,32},{1,33},{2,34},{3,35},{4,36},{5,37},{6,38},{7,39},{8,10},{9,... | collective-permute-start | bytes 3145736 | tf_op jit(solution)/shard_map/ppermute | solution.py:219
  89.3 26.0 %collective-permute-start.21 = (bf16[8,512,128]{2,1,0:T(8,128)(2,1)}, bf16[8,512,128]{2,1,0:T(8,128)(2,1)S(1)}, u32[]{:S(2)}, u32[]{:S(2)}) collective-permute-start(bf16[8,512,128]{2,1,0:T(8,128)(2,1)} %get-tuple-element.87), channel_id=1, source_target_pairs={{0,48},{1,49},{2,50},{3,51},{4,52},{5,53},{6,54},{7,55},{8,11},{9,... | collective-permute-start | bytes 3145736 | tf_op jit(solution)/shard_map/ppermute | solution.py:219
  90.9 9.3 %collective-permute-start.13 = (bf16[2,128,512]{2,1,0:T(8,128)(2,1)S(1)}, bf16[2,128,512]{2,1,0:T(8,128)(2,1)S(1)}, u32[]{:S(2)}, u32[]{:S(2)}) collective-permute-start(bf16[2,128,512]{2,1,0:T(8,128)(2,1)S(1)} %fusion.7), channel_id=1, source_target_pairs={{4,0},{5,1},{6,2},{7,3},{8,4},{9,5},{10,6},{11,7},{12,8},{13,9},{1... | collective-permute-start | bytes 786440 | tf_op jit(solution)/shard_map/ppermute | solution.py:209
  118.1 32.5 %all-to-all-start = ((bf16[8,512,128]{2,1,0:T(8,128)(2,1)}), bf16[8,512,128]{2,1,0:T(8,128)(2,1)S(1)}, u32[]{:S(2)}, u32[]{:S(2)}) async-start(bf16[8,512,128]{2,1,0:T(8,128)(2,1)} %add_convert_fusion), calls=%async_computation | async-start | bytes 2097152 | tf_op jit(solution)/shard_map/all_to_all | solution.py:362
  150.8 9.7 %collective-permute-start.22 = (bf16[512,128]{1,0:T(8,128)(2,1)S(1)}, bf16[512,128]{1,0:T(8,128)(2,1)S(1)}, u32[]{:S(2)}, u32[]{:S(2)}) collective-permute-start(bf16[512,128]{1,0:T(8,128)(2,1)S(1)} %reduce_sum.12), channel_id=1, source_target_pairs={{9,24},{10,40},{11,56},{13,28},{14,44},{15,60},{24,9},{26,41},{27,... | collective-permute-start | bytes 393224 | tf_op jit(solution)/shard_map/ppermute | solution.py:219
  (11 other events, 47.2 us)

commit v4 on v3

--- a/solution.py
+++ b/solution.py
@@ -17,7 +17,7 @@
 HEADS_AT_ONCE = 8
 ZH, ZL, RING = 4, 2, 4
 ROWS = 1024
-FORWARD_MIB, BACKWARD_MIB, PREPARE_MIB, PRODUCT_MIB = 56, 56, 56, 56
+FORWARD_MIB, BACKWARD_MIB, PREPARE_MIB, PRODUCT_MIB = 28, 56, 12, 44
 AFTER = 3
 CLIP = 2.0
 NEG = -1e30
@@ -258,9 +258,7 @@
     return own + along_tokens(before.astype(BF), -RING).astype(F32)
 
 
-def prepare_kernel(place_ref, old_ref, new_ref, keys_ref, values_ref, cot_ref, kv_ref, keep_ref, send_ref):
-    kv_ref[0] = keys_ref[...]
-    kv_ref[1] = values_ref[...]
+def prepare_kernel(place_ref, old_ref, new_ref, cot_ref, keep_ref, send_ref):
     ratio = ratio_column(old_ref, new_ref)
     core = place_ref[3]
     for out_ref, half in ((keep_ref, core), (send_ref, 1 - core)):
@@ -272,19 +270,19 @@
                 out_ref[:, to : to + HEAD] = part.astype(BF)
 
 
-def prepare(place, old, new, keys, values, cotangent):
+def prepare(place, old, new, cotangent):
     half = jax.ShapeDtypeStruct((TOKENS, cotangent.shape[1] // 2), BF)
     smem = pl.BlockSpec(memory_space=pltpu.SMEM)
     vmem = pl.BlockSpec(memory_space=pltpu.VMEM)
     return pl.pallas_call(
         prepare_kernel,
-        in_specs=[smem] + [vmem] * 5,
-        out_specs=[vmem] * 3,
-        out_shape=[jax.ShapeDtypeStruct((2,) + keys.shape, BF), half, half],
+        in_specs=[smem] + [vmem] * 3,
+        out_specs=[vmem] * 2,
+        out_shape=[half, half],
         compiler_params=params(PREPARE_MIB),
         cost_estimate=pl.CostEstimate(flops=2**20, bytes_accessed=2**22, transcendentals=0),
         name="prepare",
-    )(place, old, new, keys, values, cotangent)
+    )(place, old, new, cotangent)
 
 
 def product_kernel(first_ref, *refs):
@@ -332,24 +330,26 @@
     in_reduce = jnp.where(core == 0, x, y)
     place = jnp.stack([here, in_group, in_reduce, core])
 
-    kv, keep, send = prepare(place, old, new, keys, values, cotangent)
+    kv = jnp.stack([keys, values])
+    kv, prepare_place = lax.optimization_barrier((kv, place))
+    keep, send = prepare(prepare_place, old, new, cotangent)
     kvs = from_predecessors(kv, y) + [kv]
     w_mine = jnp.concatenate([keep, core_swap(send)], axis=0)
-    kvs[AFTER], w_soon = lax.optimization_barrier((kvs[AFTER], w_mine))
+    w_soon = w_mine
     *kvs, w_late = lax.optimization_barrier((*kvs, w_mine))
     ws = [w_mine] + [group_turn(w_soon if by == 2 else w_late, by) for by in range(1, RING)]
 
     same, cross, logs = attention_forward(place, lengths, queries, kvs)
     dq, own, *backs = attention_backward(place, lengths, old, new, queries, head_grads, logs, kvs)
     pieces = [*same, *cross]
-    pieces[2] = group_turn(same[2], 2)
+    pieces[RING] = cross_turn(cross[0], 0)
     pieces[RING + 2] = cross_turn(cross[2], 2)
     *pieces, ws[1], ws[2], ws[3], own = lax.optimization_barrier((*pieces, *ws[1:], own))
     same, cross = pieces[:RING], pieces[RING:]
     outs = []
     for by in range(RING):
-        outs.append(group_turn(same[by], by) if by % 2 else same[by])
-        outs.append(cross[by] if by == 2 else cross_turn(cross[by], by))
+        outs.append(same[by] if by in (0,) else group_turn(same[by], by))
+        outs.append(cross[by] if by in (0, 2) else cross_turn(cross[by], by))
 
     first = ((in_reduce + 1) % RING).reshape(1)
     sent = product(first, RING - 1, outs, ws)

time: 162 us -> 154 us (0.951)
  waiting for transfers between devices: 68.9 us -> 54.5 us
  starting transfers between devices: 46.2 us -> 53.4 us
  local copies, waits for them, and re-layouts: 4.66 us -> 11.5 us
  Pallas kernels: 34.8 us -> 28 us
    unnamed x39 -> x51, local copies, waits for them, and re-layouts: 3.8 us -> 10.6 us
    ppermute x21, waiting for transfers between devices: 34.4 us -> 27.9 us  [moved(): return lax.ppermute(v, FLAT, pairs)]
    ppermute x2, starting transfers between devices: 9.53 us -> 14.7 us  [along_tokens(): lax.ppermute(v, FLAT, [(i, i + by) for i in range(count) if 0 <= i + by <...]
    all_to_all x1, waiting for transfers between devices: 25.1 us -> 20.9 us  [shards(): lax.all_to_all(part, ('zh', 'zl'), split_axis=0, concat_axis=0, tiled=True)]
    pallas_call x2, Pallas kernels: 12.2 us -> 8.47 us  [product(): pl.pallas_call(product_kernel, grid_spec=pltpu.PrefetchScalarGridSpec(num...]
    ppermute x2, waiting for transfers between devices: 9.49 us -> 5.77 us  [along_tokens(): lax.ppermute(v, FLAT, [(i, i + by) for i in range(count) if 0 <= i + by <...]
    ppermute x21, starting transfers between devices: 29.2 us -> 31.1 us  [moved(): return lax.ppermute(v, FLAT, pairs)]
    pallas_call x1, Pallas kernels: 2.75 us -> 0.95 us  [prepare(): pl.pallas_call(prepare_kernel, in_specs=[smem] + [vmem] * 3, out_specs=[v...]
  transfers between devices with their start and end apart: 24 -> 24, of which waited for: 13 -> 12; matrix products, arithmetic and copies ran while one was open for 2% -> 1% of each run, Pallas kernels for 20% -> 18%
where the time goes in v4:
time: 154 us; the launch traced here: 153 us
  waiting for transfers between devices  54.5 us (35%)
  starting transfers between devices  53.4 us (35%)
  Pallas kernels  28 us (18%)
  local copies, waits for them, and re-layouts  11.5 us (7%)
  other arithmetic  4.74 us (3%)
    ppermute x21, starting transfers between devices, moved(): return lax.ppermute(v, FLAT, pairs)  31.1 us
    ppermute x21, waiting for transfers between devices, moved(): return lax.ppermute(v, FLAT, pairs)  27.9 us
    all_to_all x1, waiting for transfers between devices, shards(): lax.all_to_all(part, ('zh', 'zl'), split_axis=0, concat_axis=0, tiled=True)  20.9 us
    ppermute x2, starting transfers between devices, along_tokens(): lax.ppermute(v, FLAT, [(i, i + by) for i in range(count) if 0 <= i + by <...  14.7 us
    pallas_call x1, Pallas kernels, attention_backward(): pl.pallas_call(backward_kernel, grid_spec=pltpu.PrefetchScalarGridSpec(nu...  11.4 us
    unnamed x51, local copies, waits for them, and re-layouts  10.6 us
    pallas_call x2, Pallas kernels, product(): pl.pallas_call(product_kernel, grid_spec=pltpu.PrefetchScalarGridSpec(num...  8.47 us
    all_to_all x1, starting transfers between devices, shards(): lax.all_to_all(part, ('zh', 'zl'), split_axis=0, concat_axis=0, tiled=True)  7.53 us
  transfers between devices with their start and end apart: 24, of which 12 were waited for; matrix products, arithmetic and copies ran while one was open for 1% of the time, Pallas kernels for 18%

profile of v4, /device:TPU:17, one launch (start us, length us, event | category | flops | bytes accessed | tf_op | source)
XLA Modules:
  0.0 153.1 jit_solution(1073678412831740184)
XLA Ops:
  1.7 3.5 %collective-permute-start = (bf16[2,128,512]{2,1,0:T(8,128)(2,1)S(1)}, bf16[2,128,512]{2,1,0:T(8,128)(2,1)S(1)}, u32[]{:S(2)}, u32[]{:S(2)}) collective-permute-start(bf16[2,128,512]{2,1,0:T(8,128)(2,1)S(1)} %pad_maximum_fusion.refs_4_), channel_id=1, source_target_pairs={{0,4},{1,5},{2,6},{3,7},{4,8},{5,9},{6,10},{7,11},{8,12},{9,13},{1... | collective-permute-start | bytes 786440 | tf_op jit(solution)/shard_map/ppermute | solution.py:209
  5.3 1.2 copy-done
  9.9 2.5 %collective-permute-done.refs_0_ = bf16[2,128,512]{2,1,0:T(8,128)(2,1)S(1)} collective-permute-done((bf16[2,128,512]{2,1,0:T(8,128)(2,1)S(1)}, bf16[2,128,512]{2,1,0:T(8,128)(2,1)S(1)}, u32[]{:S(2)}, u32[]{:S(2)}) %collective-permute-start) | collective-permute-done | bytes 262176 | tf_op jit(solution)/shard_map/ppermute | solution.py:209
  12.4 1.1 collective-permute-start.3
  14.9 11.5 %collective-permute-done.3.refs_3_ = bf16[2,128,512]{2,1,0:T(8,128)(2,1)S(1)} collective-permute-done((bf16[2,128,512]{2,1,0:T(8,128)(2,1)S(1)}, bf16[2,128,512]{2,1,0:T(8,128)(2,1)S(1)}, u32[]{:S(2)}, u32[]{:S(2)}) %collective-permute-start.3) | collective-permute-done | bytes 262176 | tf_op jit(solution)/shard_map/ppermute | solution.py:219
  26.3 1.7 %collective-permute-done.1.refs_1_ = bf16[2,128,512]{2,1,0:T(8,128)(2,1)S(1)} collective-permute-done((bf16[2,128,512]{2,1,0:T(8,128)(2,1)S(1)}, bf16[2,128,512]{2,1,0:T(8,128)(2,1)S(1)}, u32[]{:S(2)}, u32[]{:S(2)}) %collective-permute-start.1) | collective-permute-done | bytes 262176 | tf_op jit(solution)/shard_map/ppermute | solution.py:219
  28.0 1.5 collective-permute-start.7
  29.5 2.2 %collective-permute-start.8 = (bf16[256,2048]{1,0:T(8,128)(2,1)S(1)}, bf16[256,2048]{1,0:T(8,128)(2,1)S(1)}, u32[]{:S(2)}, u32[]{:S(2)}) collective-permute-start(bf16[256,2048]{1,0:T(8,128)(2,1)S(1)} %constant_dynamic-update-slice_fusion.refs_8_), channel_id=1, source_target_pairs={{0,2},{1,3},{2,0},{3,1},{4,6},{5,7},{6,4},{7,5},{8,40},{9,41},{10,... | collective-permute-start | bytes 3145736 | tf_op jit(solution)/shard_map/ppermute | solution.py:219
  31.7 1.2 copy-done.16
  33.0 7.2 %attention_forward.1 = (bf16[2,512,128]{2,1,0:T(8,128)(2,1)S(1)}, bf16[2,512,128]{2,1,0:T(8,128)(2,1)}, bf16[2,512,128]{2,1,0:T(8,128)(2,1)}, bf16[2,512,128]{2,...) custom-call(s32[4]{0:T(128)S(1)} %pad_add_fusion.place_ref.here_ref,, ...), custom_call_target="tpu_custom_call" | custom-call | flops 1342177280 | bytes 4194304 | tf_op jit(solution)/shard_map/attention_forward/pallas_call | solution.py:167
  41.5 2.0 %collective-permute-start.6 = (bf16[2,512,128]{2,1,0:T(8,128)(2,1)S(1)}, bf16[2,512,128]{2,1,0:T(8,128)(2,1)S(1)}, u32[]{:S(2)}, u32[]{:S(2)}) collective-permute-start(bf16[2,512,128]{2,1,0:T(8,128)(2,1)S(1)} %get-tuple-element.63), channel_id=1, source_target_pairs={{0,40},{1,41},{2,42},{3,43},{4,44},{5,45},{6,46},{7,47},{8,2},{9,3... | collective-permute-start | bytes 786440 | tf_op jit(solution)/shard_map/ppermute | solution.py:219
  43.5 11.4 %attention_backward.1 = (f32[128,4096]{1,0:T(8,128)}, f32[2,128,512]{2,1,0:T(8,128)}, bf16[2,128,512]{2,1,0:T(8,128)(2,1)}, bf16[2,128,512]{2,1,0:T(8,128)(2,1)}...) custom-call(s32[4]{0:T(128)} %copy-done.13, s32[1,128]{1,0:T(1,128)} %bitcast.18, f32[1,128]{1,0:T(1,128)} %bitcast.14, ...), custom_call_target="tpu_custom_call" | custom-call | flops 3355443200 | bytes 8388608 | tf_op jit(solution)/shard_map/attention_backward/pallas_call | solution.py:187
  56.3 1.6 %collective-permute-done.8.refs_10_ = bf16[256,2048]{1,0:T(8,128)(2,1)S(1)} collective-permute-done((bf16[256,2048]{1,0:T(8,128)(2,1)S(1)}, bf16[256,2048]{1,0:T(8,128)(2,1)S(1)}, u32[]{:S(2)}, u32[]{:S(2)}) %collective-permute-start.8) | collective-permute-done | bytes 1048608 | tf_op jit(solution)/shard_map/ppermute | solution.py:219
  58.9 4.7 %collective-permute-start.15 = (bf16[2,512,128]{2,1,0:T(8,128)(2,1)}, bf16[2,512,128]{2,1,0:T(8,128)(2,1)}, u32[]{:S(2)}, u32[]{:S(2)}) collective-permute-start(bf16[2,512,128]{2,1,0:T(8,128)(2,1)} %get-tuple-element.75), channel_id=1, source_target_pairs={{0,24},{1,25},{2,26},{3,27},{4,28},{5,29},{6,30},{7,31},{8,1},{9,2... | collective-permute-start | bytes 786440 | tf_op jit(solution)/shard_map/ppermute | solution.py:219
  63.6 3.3 %collective-permute-start.16 = (bf16[2,512,128]{2,1,0:T(8,128)(2,1)}, bf16[2,512,128]{2,1,0:T(8,128)(2,1)}, u32[]{:S(2)}, u32[]{:S(2)}) collective-permute-start(bf16[2,512,128]{2,1,0:T(8,128)(2,1)} %get-tuple-element.76), channel_id=1, source_target_pairs={{0,2},{1,3},{2,0},{3,1},{4,6},{5,7},{6,4},{7,5},{8,40},{9,41},{10,... | collective-permute-start | bytes 786440 | tf_op jit(solution)/shard_map/ppermute | solution.py:219
  67.9 3.1 %collective-permute-start.10 = (bf16[2,128,512]{2,1,0:T(8,128)(2,1)}, bf16[2,128,512]{2,1,0:T(8,128)(2,1)S(1)}, u32[]{:S(2)}, u32[]{:S(2)}) collective-permute-start(bf16[2,128,512]{2,1,0:T(8,128)(2,1)} %get-tuple-element.68), channel_id=1, source_target_pairs={{0,3},{1,0},{2,1},{3,2},{4,7},{5,4},{6,5},{7,6},{8,11},{9,8},{10,9... | collective-permute-start | bytes 786440 | tf_op jit(solution)/shard_map/ppermute | solution.py:219
  71.4 2.7 %collective-permute-start.11 = (bf16[2,128,512]{2,1,0:T(8,128)(2,1)}, bf16[2,128,512]{2,1,0:T(8,128)(2,1)S(1)}, u32[]{:S(2)}, u32[]{:S(2)}) collective-permute-start(bf16[2,128,512]{2,1,0:T(8,128)(2,1)} %get-tuple-element.69), channel_id=1, source_target_pairs={{0,2},{1,3},{2,0},{3,1},{4,6},{5,7},{6,4},{7,5},{8,10},{9,11},{10,... | collective-permute-start | bytes 786440 | tf_op jit(solution)/shard_map/ppermute | solution.py:219
  74.2 1.2 collective-permute-done.18.refs_7_
  75.4 1.2 copy-done.3
  78.5 6.0 %product.3 = (bf16[8,512,128]{2,1,0:T(8,128)(2,1)S(1)}, bf16[8,512,128]{2,1,0:T(8,128)(2,1)S(1)}, bf16[8,512,128]{2,1,0:T(8,128)(2,1)S(1)}) custom-call(s32[1]{0:T(128)} %bitcast.9.first_ref, bf16[2,512,128]{2,1,0:T(8,128)(2,1)S(1)} %copy-done.7, bf16[2,512,128]{2,1,0:T(8,128)(2,1)S(1)} %copy-done.9, bf16[2,512,128]{2,1,0:T(8,128)(2,1)} %collective-permute-done.14.refs_2_, ...), custom_call_target="tpu_custom_call" | custom-call | flops 3221225472 | bytes 8388608 | tf_op jit(solution)/shard_map/product/pallas_call | solution.py:307
  84.6 1.4 collective-permute-start.20
  86.0 1.2 collective-permute-start.21
  87.4 11.2 %collective-permute-start.13 = (bf16[2,128,512]{2,1,0:T(8,128)(2,1)S(1)}, bf16[2,128,512]{2,1,0:T(8,128)(2,1)S(1)}, u32[]{:S(2)}, u32[]{:S(2)}) collective-permute-start(bf16[2,128,512]{2,1,0:T(8,128)(2,1)S(1)} %fusion.7), channel_id=1, source_target_pairs={{4,0},{5,1},{6,2},{7,3},{8,4},{9,5},{10,6},{11,7},{12,8},{13,9},{1... | collective-permute-start | bytes 786440 | tf_op jit(solution)/shard_map/ppermute | solution.py:209
  98.6 3.3 %collective-permute-done.13 = bf16[2,128,512]{2,1,0:T(8,128)(2,1)S(1)} collective-permute-done((bf16[2,128,512]{2,1,0:T(8,128)(2,1)S(1)}, bf16[2,128,512]{2,1,0:T(8,128)(2,1)S(1)}, u32[]{:S(2)}, u32[]{:S(2)}) %collective-permute-start.13) | collective-permute-done | bytes 262176 | tf_op jit(solution)/shard_map/ppermute | solution.py:209
  102.9 2.5 %product.2 = bf16[8,512,128]{2,1,0:T(8,128)(2,1)S(1)} custom-call(s32[1]{0:T(128)} %bitcast.2.first_ref, bf16[2,512,128]{2,1,0:T(8,128)(2,1)S(1)} %copy-done.7, bf16[2,512,128]{2,1,0:T(8,128)(2,1)S(1)} %copy-done.9, bf16[2,512,128]{2,1,0:T(8,128)(2,1)} %collective-permute-done.14.refs_2_, bf16[2,512,128]{2,1,0:T(8,128)(2,1)} %collective-permute-done.15.refs_3_, ...), custom_call_target="tpu_custom_call" | custom-call | flops 1073741824 | bytes 4194304 | tf_op jit(solution)/shard_map/product/pallas_call | solution.py:307
  105.4 4.3 %collective-permute-done.20 = bf16[8,512,128]{2,1,0:T(8,128)(2,1)S(1)} collective-permute-done((bf16[8,512,128]{2,1,0:T(8,128)(2,1)S(1)}, bf16[8,512,128]{2,1,0:T(8,128)(2,1)S(1)}, u32[]{:S(2)}, u32[]{:S(2)}) %collective-permute-start.20) | collective-permute-done | bytes 1048608 | tf_op jit(solution)/shard_map/ppermute | solution.py:219
  109.7 1.9 %collective-permute-done.21 = bf16[8,512,128]{2,1,0:T(8,128)(2,1)S(1)} collective-permute-done((bf16[8,512,128]{2,1,0:T(8,128)(2,1)S(1)}, bf16[8,512,128]{2,1,0:T(8,128)(2,1)S(1)}, u32[]{:S(2)}, u32[]{:S(2)}) %collective-permute-start.21) | collective-permute-done | bytes 1048608 | tf_op jit(solution)/shard_map/ppermute | solution.py:219
  111.6 1.5 %add_convert_fusion = bf16[8,512,128]{2,1,0:T(8,128)(2,1)} fusion(bf16[8,512,128]{2,1,0:T(8,128)(2,1)S(1)} %collective-permute-done.21, bf16[8,512,128]{2,1,0:T(8,128)(2,1)S(1)} %collective-permute-done.20, bf16[8,512,128]{2,1,0:T(8,128)(2,1)S(1)} %collective-permute-done.19, bf16[8,512,128]{2,1,0:T(8,128)(2,1)S(1)} %product.2), kind=kLoop, calls=%fused_computation | loop fusion | flops 4194304 | bytes 5242880 | tf_op jit(solution)/shard_map/convert_element_type | solution.py:359
  113.1 7.5 %all-to-all-start = ((bf16[8,512,128]{2,1,0:T(8,128)(2,1)}), bf16[8,512,128]{2,1,0:T(8,128)(2,1)S(1)}, u32[]{:S(2)}, u32[]{:S(2)}) async-start(bf16[8,512,128]{2,1,0:T(8,128)(2,1)} %add_convert_fusion), calls=%async_computation | async-start | bytes 2097152 | tf_op jit(solution)/shard_map/all_to_all | solution.py:362
  120.7 20.9 %all-to-all-done = bf16[8,512,128]{2,1,0:T(8,128)(2,1)S(1)} async-done(((bf16[8,512,128]{2,1,0:T(8,128)(2,1)}), bf16[8,512,128]{2,1,0:T(8,128)(2,1)S(1)}, u32[]{:S(2)}, u32[]{:S(2)}) %all-to-all-start) | async-done | bytes 1048608 | tf_op jit(solution)/shard_map/all_to_all | solution.py:362
  141.7 4.9 %collective-permute-start.22 = (bf16[512,128]{1,0:T(8,128)(2,1)S(1)}, bf16[512,128]{1,0:T(8,128)(2,1)S(1)}, u32[]{:S(2)}, u32[]{:S(2)}) collective-permute-start(bf16[512,128]{1,0:T(8,128)(2,1)S(1)} %reduce_sum.12), channel_id=1, source_target_pairs={{9,24},{10,40},{11,56},{13,28},{14,44},{15,60},{24,9},{26,41},{27,... | collective-permute-start | bytes 393224 | tf_op jit(solution)/shard_map/ppermute | solution.py:219
  147.4 4.9 %collective-permute-done.22 = bf16[512,128]{1,0:T(8,128)(2,1)S(1)} collective-permute-done((bf16[512,128]{1,0:T(8,128)(2,1)S(1)}, bf16[512,128]{1,0:T(8,128)(2,1)S(1)}, u32[]{:S(2)}, u32[]{:S(2)}) %collective-permute-start.22) | collective-permute-done | bytes 131104 | tf_op jit(solution)/shard_map/ppermute | solution.py:219
  (82 shorter events, 16.1 us)
Async XLA Ops:
  1.7 30.1 %copy-start.1 = (bf16[2,128,512]{2,1,0:T(8,128)(2,1)}, bf16[2,128,512]{2,1,0:T(8,128)(2,1)S(1)}, u32[]{:S(2)}) copy-start(bf16[2,128,512]{2,1,0:T(8,128)(2,1)S(1)} %pad_maximum_fusion.refs_4_) | copy-start | bytes 786436
  1.7 30.0 %copy-start.13 = (s32[4]{0:T(128)}, s32[4]{0:T(128)S(1)}, u32[]{:S(2)}) copy-start(s32[4]{0:T(128)S(1)} %pad_add_fusion.place_ref.here_ref) | copy-start | bytes 52
  1.7 10.6 %collective-permute-start = (bf16[2,128,512]{2,1,0:T(8,128)(2,1)S(1)}, bf16[2,128,512]{2,1,0:T(8,128)(2,1)S(1)}, u32[]{:S(2)}, u32[]{:S(2)}) collective-permute-start(bf16[2,128,512]{2,1,0:T(8,128)(2,1)S(1)} %pad_maximum_fusion.refs_4_), channel_id=1, source_target_pairs={{0,4},{1,5},{2,6},{3,7},{4,8},{5,9},{6,10},{7,11},{8,12},{9,13},{1... | collective-permute-start | bytes 786440 | tf_op jit(solution)/shard_map/ppermute | solution.py:209
  7.8 23.9 %copy-start.20 = (s32[128]{0:T(128)S(1)}, s32[128]{0:T(128)}, u32[]{:S(2)}) copy-start(s32[128]{0:T(128)} %param.15) | copy-start | bytes 1540
  8.8 6.0 %collective-permute-start.4 = (bf16[128,2048]{1,0:T(8,128)(2,1)S(1)}, bf16[128,2048]{1,0:T(8,128)(2,1)S(1)}, u32[]{:S(2)}, u32[]{:S(2)}) collective-permute-start(bf16[128,2048]{1,0:T(8,128)(2,1)S(1)} %get-tuple-element.49), channel_id=1, source_target_pairs={{0,8},{1,9},{2,10},{3,11},{4,12},{5,13},{6,14},{7,15},{8,0},{9,1},... | collective-permute-start | bytes 1572872 | tf_op jit(solution)/shard_map/ppermute | solution.py:219
  12.4 13.9 %collective-permute-start.3 = (bf16[2,128,512]{2,1,0:T(8,128)(2,1)S(1)}, bf16[2,128,512]{2,1,0:T(8,128)(2,1)S(1)}, u32[]{:S(2)}, u32[]{:S(2)}) collective-permute-start(bf16[2,128,512]{2,1,0:T(8,128)(2,1)S(1)} %get-tuple-element.90), channel_id=1, source_target_pairs={{0,1},{1,2},{2,3},{3,0},{4,5},{5,6},{6,7},{7,4},{8,9},{9,10},{10,1... | collective-permute-start | bytes 786440 | tf_op jit(solution)/shard_map/ppermute | solution.py:219
  13.5 12.9 %collective-permute-start.2 = (bf16[2,128,512]{2,1,0:T(8,128)(2,1)S(1)}, bf16[2,128,512]{2,1,0:T(8,128)(2,1)S(1)}, u32[]{:S(2)}, u32[]{:S(2)}) collective-permute-start(bf16[2,128,512]{2,1,0:T(8,128)(2,1)S(1)} %get-tuple-element.91), channel_id=1, source_target_pairs={{0,2},{1,3},{2,0},{3,1},{4,6},{5,7},{6,4},{7,5},{8,10},{9,11},{10,... | collective-permute-start | bytes 786440 | tf_op jit(solution)/shard_map/ppermute | solution.py:219
  13.8 14.2 %collective-permute-start.1 = (bf16[2,128,512]{2,1,0:T(8,128)(2,1)S(1)}, bf16[2,128,512]{2,1,0:T(8,128)(2,1)S(1)}, u32[]{:S(2)}, u32[]{:S(2)}) collective-permute-start(bf16[2,128,512]{2,1,0:T(8,128)(2,1)S(1)} %get-tuple-element.92), channel_id=1, source_target_pairs={{0,3},{1,0},{2,1},{3,2},{4,7},{5,4},{6,5},{7,6},{8,11},{9,8},{10,9... | collective-permute-start | bytes 786440 | tf_op jit(solution)/shard_map/ppermute | solution.py:219
  14.8 17.0 %copy-start.5 = (bf16[2,128,512]{2,1,0:T(8,128)(2,1)S(1)}, bf16[2,128,512]{2,1,0:T(8,128)(2,1)}, u32[]{:S(2)}) copy-start(bf16[2,128,512]{2,1,0:T(8,128)(2,1)} %copy-done.4) | copy-start | bytes 786436
  28.0 28.3 %collective-permute-start.9 = (bf16[256,2048]{1,0:T(8,128)(2,1)S(1)}, bf16[256,2048]{1,0:T(8,128)(2,1)S(1)}, u32[]{:S(2)}, u32[]{:S(2)}) collective-permute-start(bf16[256,2048]{1,0:T(8,128)(2,1)S(1)} %constant_dynamic-update-slice_fusion.refs_8_), channel_id=1, source_target_pairs={{0,3},{1,0},{2,1},{3,2},{4,7},{5,4},{6,5},{7,6},{8,56},{9,57},{10,... | collective-permute-start | bytes 3145736 | tf_op jit(solution)/shard_map/ppermute | solution.py:219
  28.0 28.3 %collective-permute-start.7 = (bf16[256,2048]{1,0:T(8,128)(2,1)S(1)}, bf16[256,2048]{1,0:T(8,128)(2,1)S(1)}, u32[]{:S(2)}, u32[]{:S(2)}) collective-permute-start(bf16[256,2048]{1,0:T(8,128)(2,1)S(1)} %constant_dynamic-update-slice_fusion.refs_8_), channel_id=1, source_target_pairs={{0,1},{1,2},{2,3},{3,0},{4,5},{5,6},{6,7},{7,4},{8,24},{9,25},{10,... | collective-permute-start | bytes 3145736 | tf_op jit(solution)/shard_map/ppermute | solution.py:219
  29.5 28.4 %collective-permute-start.8 = (bf16[256,2048]{1,0:T(8,128)(2,1)S(1)}, bf16[256,2048]{1,0:T(8,128)(2,1)S(1)}, u32[]{:S(2)}, u32[]{:S(2)}) collective-permute-start(bf16[256,2048]{1,0:T(8,128)(2,1)S(1)} %constant_dynamic-update-slice_fusion.refs_8_), channel_id=1, source_target_pairs={{0,2},{1,3},{2,0},{3,1},{4,6},{5,7},{6,4},{7,5},{8,40},{9,41},{10,... | collective-permute-start | bytes 3145736 | tf_op jit(solution)/shard_map/ppermute | solution.py:219
  41.4 13.5 %collective-permute-start.5 = (bf16[2,512,128]{2,1,0:T(8,128)(2,1)S(1)}, bf16[2,512,128]{2,1,0:T(8,128)(2,1)S(1)}, u32[]{:S(2)}, u32[]{:S(2)}) collective-permute-start(bf16[2,512,128]{2,1,0:T(8,128)(2,1)S(1)} %get-tuple-element.61), channel_id=1, source_target_pairs={{0,8},{1,9},{2,10},{3,11},{4,12},{5,13},{6,14},{7,15},{8,0},{9,1},... | collective-permute-start | bytes 786440 | tf_op jit(solution)/shard_map/ppermute | solution.py:219
  41.5 14.1 %collective-permute-start.6 = (bf16[2,512,128]{2,1,0:T(8,128)(2,1)S(1)}, bf16[2,512,128]{2,1,0:T(8,128)(2,1)S(1)}, u32[]{:S(2)}, u32[]{:S(2)}) collective-permute-start(bf16[2,512,128]{2,1,0:T(8,128)(2,1)S(1)} %get-tuple-element.63), channel_id=1, source_target_pairs={{0,40},{1,41},{2,42},{3,43},{4,44},{5,45},{6,46},{7,47},{8,2},{9,3... | collective-permute-start | bytes 786440 | tf_op jit(solution)/shard_map/ppermute | solution.py:219
  43.5 31.8 %copy-start.7 = (bf16[2,512,128]{2,1,0:T(8,128)(2,1)S(1)}, bf16[2,512,128]{2,1,0:T(8,128)(2,1)}, u32[]{:S(2)}) copy-start(bf16[2,512,128]{2,1,0:T(8,128)(2,1)} %copy-done.6) | copy-start | bytes 786436
  58.9 9.0 %collective-permute-start.14 = (bf16[2,512,128]{2,1,0:T(8,128)(2,1)}, bf16[2,512,128]{2,1,0:T(8,128)(2,1)}, u32[]{:S(2)}, u32[]{:S(2)}) collective-permute-start(bf16[2,512,128]{2,1,0:T(8,128)(2,1)} %get-tuple-element.74), channel_id=1, source_target_pairs={{0,1},{1,2},{2,3},{3,0},{4,5},{5,6},{6,7},{7,4},{8,24},{9,25},{10,... | collective-permute-start | bytes 786440 | tf_op jit(solution)/shard_map/ppermute | solution.py:219
  58.9 12.5 %collective-permute-start.15 = (bf16[2,512,128]{2,1,0:T(8,128)(2,1)}, bf16[2,512,128]{2,1,0:T(8,128)(2,1)}, u32[]{:S(2)}, u32[]{:S(2)}) collective-permute-start(bf16[2,512,128]{2,1,0:T(8,128)(2,1)} %get-tuple-element.75), channel_id=1, source_target_pairs={{0,24},{1,25},{2,26},{3,27},{4,28},{5,29},{6,30},{7,31},{8,1},{9,2... | collective-permute-start | bytes 786440 | tf_op jit(solution)/shard_map/ppermute | solution.py:219
  63.6 10.5 %collective-permute-start.16 = (bf16[2,512,128]{2,1,0:T(8,128)(2,1)}, bf16[2,512,128]{2,1,0:T(8,128)(2,1)}, u32[]{:S(2)}, u32[]{:S(2)}) collective-permute-start(bf16[2,512,128]{2,1,0:T(8,128)(2,1)} %get-tuple-element.76), channel_id=1, source_target_pairs={{0,2},{1,3},{2,0},{3,1},{4,6},{5,7},{6,4},{7,5},{8,40},{9,41},{10,... | collective-permute-start | bytes 786440 | tf_op jit(solution)/shard_map/ppermute | solution.py:219
  66.8 7.3 %collective-permute-start.17 = (bf16[2,512,128]{2,1,0:T(8,128)(2,1)}, bf16[2,512,128]{2,1,0:T(8,128)(2,1)}, u32[]{:S(2)}, u32[]{:S(2)}) collective-permute-start(bf16[2,512,128]{2,1,0:T(8,128)(2,1)} %get-tuple-element.78), channel_id=1, source_target_pairs={{0,3},{1,0},{2,1},{3,2},{4,7},{5,4},{6,5},{7,6},{8,56},{9,57},{10,... | collective-permute-start | bytes 786440 | tf_op jit(solution)/shard_map/ppermute | solution.py:219
  67.5 7.9 %collective-permute-start.18 = (bf16[2,512,128]{2,1,0:T(8,128)(2,1)}, bf16[2,512,128]{2,1,0:T(8,128)(2,1)}, u32[]{:S(2)}, u32[]{:S(2)}) collective-permute-start(bf16[2,512,128]{2,1,0:T(8,128)(2,1)} %get-tuple-element.79), channel_id=1, source_target_pairs={{0,56},{1,57},{2,58},{3,59},{4,60},{5,61},{6,62},{7,63},{8,3},{9,0... | collective-permute-start | bytes 786440 | tf_op jit(solution)/shard_map/ppermute | solution.py:219
  67.9 18.0 %collective-permute-start.10 = (bf16[2,128,512]{2,1,0:T(8,128)(2,1)}, bf16[2,128,512]{2,1,0:T(8,128)(2,1)S(1)}, u32[]{:S(2)}, u32[]{:S(2)}) collective-permute-start(bf16[2,128,512]{2,1,0:T(8,128)(2,1)} %get-tuple-element.68), channel_id=1, source_target_pairs={{0,3},{1,0},{2,1},{3,2},{4,7},{5,4},{6,5},{7,6},{8,11},{9,8},{10,9... | collective-permute-start | bytes 786440 | tf_op jit(solution)/shard_map/ppermute | solution.py:219
  71.4 15.7 %collective-permute-start.11 = (bf16[2,128,512]{2,1,0:T(8,128)(2,1)}, bf16[2,128,512]{2,1,0:T(8,128)(2,1)S(1)}, u32[]{:S(2)}, u32[]{:S(2)}) collective-permute-start(bf16[2,128,512]{2,1,0:T(8,128)(2,1)} %get-tuple-element.69), channel_id=1, source_target_pairs={{0,2},{1,3},{2,0},{3,1},{4,6},{5,7},{6,4},{7,5},{8,10},{9,11},{10,... | collective-permute-start | bytes 786440 | tf_op jit(solution)/shard_map/ppermute | solution.py:219
  74.1 13.1 %collective-permute-start.12 = (bf16[2,128,512]{2,1,0:T(8,128)(2,1)}, bf16[2,128,512]{2,1,0:T(8,128)(2,1)S(1)}, u32[]{:S(2)}, u32[]{:S(2)}) collective-permute-start(bf16[2,128,512]{2,1,0:T(8,128)(2,1)} %get-tuple-element.70), channel_id=1, source_target_pairs={{0,1},{1,2},{2,3},{3,0},{4,5},{5,6},{6,7},{7,4},{8,9},{9,10},{10,1... | collective-permute-start | bytes 786440 | tf_op jit(solution)/shard_map/ppermute | solution.py:219
  78.5 23.4 %copy-start.23 = (f32[2,128,512]{2,1,0:T(8,128)S(1)}, f32[2,128,512]{2,1,0:T(8,128)}, u32[]{:S(2)}) copy-start(f32[2,128,512]{2,1,0:T(8,128)} %get-tuple-element.67) | copy-start | bytes 1572868
  84.5 18.4 %copy-start.12 = (bf16[2,512,128]{2,1,0:T(8,128)(2,1)S(1)}, bf16[2,512,128]{2,1,0:T(8,128)(2,1)}, u32[]{:S(2)}) copy-start(bf16[2,512,128]{2,1,0:T(8,128)(2,1)} %copy-done.10) | copy-start | bytes 786436
  84.5 20.9 %collective-permute-start.19 = (bf16[8,512,128]{2,1,0:T(8,128)(2,1)S(1)}, bf16[8,512,128]{2,1,0:T(8,128)(2,1)S(1)}, u32[]{:S(2)}, u32[]{:S(2)}) collective-permute-start(bf16[8,512,128]{2,1,0:T(8,128)(2,1)S(1)} %get-tuple-element.83), channel_id=1, source_target_pairs={{0,16},{1,17},{2,18},{3,19},{4,20},{5,21},{6,22},{7,23},{8,9},{9,1... | collective-permute-start | bytes 3145736 | tf_op jit(solution)/shard_map/ppermute | solution.py:219
  84.6 25.1 %collective-permute-start.20 = (bf16[8,512,128]{2,1,0:T(8,128)(2,1)S(1)}, bf16[8,512,128]{2,1,0:T(8,128)(2,1)S(1)}, u32[]{:S(2)}, u32[]{:S(2)}) collective-permute-start(bf16[8,512,128]{2,1,0:T(8,128)(2,1)S(1)} %get-tuple-element.84), channel_id=1, source_target_pairs={{0,32},{1,33},{2,34},{3,35},{4,36},{5,37},{6,38},{7,39},{8,10},{9,... | collective-permute-start | bytes 3145736 | tf_op jit(solution)/shard_map/ppermute | solution.py:219
  86.0 25.6 %collective-permute-start.21 = (bf16[8,512,128]{2,1,0:T(8,128)(2,1)S(1)}, bf16[8,512,128]{2,1,0:T(8,128)(2,1)S(1)}, u32[]{:S(2)}, u32[]{:S(2)}) collective-permute-start(bf16[8,512,128]{2,1,0:T(8,128)(2,1)S(1)} %get-tuple-element.85), channel_id=1, source_target_pairs={{0,48},{1,49},{2,50},{3,51},{4,52},{5,53},{6,54},{7,55},{8,11},{9,... | collective-permute-start | bytes 3145736 | tf_op jit(solution)/shard_map/ppermute | solution.py:219
  87.4 14.5 %collective-permute-start.13 = (bf16[2,128,512]{2,1,0:T(8,128)(2,1)S(1)}, bf16[2,128,512]{2,1,0:T(8,128)(2,1)S(1)}, u32[]{:S(2)}, u32[]{:S(2)}) collective-permute-start(bf16[2,128,512]{2,1,0:T(8,128)(2,1)S(1)} %fusion.7), channel_id=1, source_target_pairs={{4,0},{5,1},{6,2},{7,3},{8,4},{9,5},{10,6},{11,7},{12,8},{13,9},{1... | collective-permute-start | bytes 786440 | tf_op jit(solution)/shard_map/ppermute | solution.py:209
  113.1 33.5 %copy-start.22 = (f32[2,128,512]{2,1,0:T(8,128)S(1)}, f32[2,128,512]{2,1,0:T(8,128)}, u32[]{:S(2)}) copy-start(f32[2,128,512]{2,1,0:T(8,128)} %fusion.3) | copy-start | bytes 1572868
  113.1 28.4 %all-to-all-start = ((bf16[8,512,128]{2,1,0:T(8,128)(2,1)}), bf16[8,512,128]{2,1,0:T(8,128)(2,1)S(1)}, u32[]{:S(2)}, u32[]{:S(2)}) async-start(bf16[8,512,128]{2,1,0:T(8,128)(2,1)} %add_convert_fusion), calls=%async_computation | async-start | bytes 2097152 | tf_op jit(solution)/shard_map/all_to_all | solution.py:362
  141.7 10.6 %collective-permute-start.22 = (bf16[512,128]{1,0:T(8,128)(2,1)S(1)}, bf16[512,128]{1,0:T(8,128)(2,1)S(1)}, u32[]{:S(2)}, u32[]{:S(2)}) collective-permute-start(bf16[512,128]{1,0:T(8,128)(2,1)S(1)} %reduce_sum.12), channel_id=1, source_target_pairs={{9,24},{10,40},{11,56},{13,28},{14,44},{15,60},{24,9},{26,41},{27,... | collective-permute-start | bytes 393224 | tf_op jit(solution)/shard_map/ppermute | solution.py:219
  (17 other events, 61.4 us)
